TPU v7x, 1024 devices: a whole 4x8x16 slice. The times are simulated.
1024 devices in a mesh: blk: 64 (over x, y, core), mp: 8 (over z_lo), tower: 2 (over z_hi).
Axes of the slice: x: 4, y: 8, z: 16 (z_hi: 2, z_lo: 8; z = z_hi * 8 + z_lo), core: 2. Of those that a mesh axis runs over, the one named last changes fastest.
Arguments:
- image_features: bfloat16 [16384, 1536], P('blk'), may hold values from -12 to 12
- text_features: bfloat16 [16384, 1024], P('blk'), may hold values from -12 to 12
- image_head: bfloat16 [1536, 1024], P(None, 'mp')
- text_head: bfloat16 [1024, 1024], P(None, 'mp')
- positive: int32 [16384], replicated, may hold values from 0 to 16383, as said below
- log_scale: float32 [1], replicated, may hold values from 1.4 to 2.3
- bias: float32 [1], replicated, may hold values from -4 to -2
Outputs:
- embed_grads: float32 [2, 16384, 1024], P('tower', 'blk', 'mp')
Inputs may be any that keep to these rules, and one draw needn't show every extreme that they name: `positive`: each text index appears exactly once.
All inputs are finite; a program needn't handle non-finite values.
Results may differ from a plain program's by a relative error of at most 0.0015.
Values may be sent and summed in bfloat16 or wider, within the bound.
No kernel may reach another device: no remote copies, remote signals or barrier semaphores. Data moves between devices by JAX's collectives and lax.ppermute only.
A program may use at most 32 MiB of HBM per device.

v0:
```python
import jax
import jax.numpy as jnp
from jax import lax
from jax.sharding import PartitionSpec as P


def partner(value, axis, apart):
    mask = 2**apart
    pairs = [(source, source ^ mask) for source in range(lax.axis_size(axis))]
    return lax.ppermute(value, axis, pairs)


def passed_along(value, axis, steps):
    count = lax.axis_size(axis)
    pairs = [(source, (source + steps) % count) for source in range(count)]
    return lax.ppermute(value, axis, pairs)


def normalize(embed):
    norm = jnp.sqrt(jnp.sum(embed * embed, axis=1, keepdims=True) + 1e-06)
    return (embed / norm, norm)


def shards(image_features, text_features, image_head, text_head, positive, log_scale, bias):
    rows = image_features.shape[0]
    num_blocks = lax.axis_size("blk")
    num_lanes = lax.axis_size("mp")
    span = num_blocks // num_lanes
    block = lax.axis_index("blk")
    lane = lax.axis_index("mp")
    side = lax.axis_index("tower")
    positions = jnp.arange(rows, dtype=jnp.int32)

    def image_side():
        return jnp.dot(image_features, image_head, preferred_element_type=jnp.float32)

    def text_side():
        return jnp.dot(text_features, text_head, preferred_element_type=jnp.float32)

    shard = lax.cond(side == 0, image_side, text_side)
    whole = lax.all_gather(shard, "mp", axis=1, tiled=True)
    unit, norm = normalize(whole)
    unit_b = unit.astype(jnp.bfloat16)
    partner_b = partner(unit_b, "tower", 0)
    moves = [(span << bit_pos, bit_pos) for bit_pos in range(num_lanes.bit_length() - 1)]
    for amount, bit_pos in moves:
        moved = passed_along(partner_b, "blk", amount)
        partner_b = jnp.where(lane >> bit_pos & 1 == 1, moved, partner_b)
    own_image_key = lax.dynamic_slice_in_dim(positive, block * rows, rows)
    own_key = jnp.where(side == 0, own_image_key, block * rows + positions)
    scale = jnp.exp(log_scale[0])
    offset = bias[0]

    def pair_tile(other_b, index):
        index = index % num_blocks
        other_image_key = lax.dynamic_slice_in_dim(positive, index * rows, rows)
        other_key = jnp.where(side == 0, index * rows + positions, other_image_key)
        logits = (
            scale * jnp.einsum("re,ce->rc", unit_b, other_b, preferred_element_type=jnp.float32)
            + offset
        )
        sign = jnp.where(own_key[:, None] == other_key[None, :], 1.0, -1.0)
        weight = (-sign * jax.nn.sigmoid(-sign * logits) * scale).astype(jnp.bfloat16)
        return jnp.dot(weight, other_b, preferred_element_type=jnp.float32)

    start = block - lane * span
    grads = pair_tile(partner_b, start)
    current = partner_b
    for step in range(1, span):
        current = passed_along(current, "blk", 1)
        grads = grads + pair_tile(current, start - step)
    partial_grads = (grads - unit * jnp.sum(unit * grads, axis=1, keepdims=True)) / norm
    result = lax.psum_scatter(partial_grads, "mp", scatter_dimension=1, tiled=True)
    return result[None]


def solution(mesh):
    placed = (P("blk", None), P("blk", None), P(None, "mp"), P(None, "mp"), P(), P(), P())
    return jax.shard_map(
        shards, mesh=mesh, in_specs=placed, out_specs=P("tower", "blk", "mp"), check_vma=False
    )
```

profile of v0, /device:TPU:6, one launch (start us, length us, event | category | flops | bytes accessed | tf_op | source)
XLA Modules:
  0.0 362.4 jit_solution(55584737507109767)
XLA Ops:
  6.5 0.0 all-gather.2.cloned.1.call-start
  6.5 1.6 conditional.1
  6.5 1.6 fusion.163
  8.1 0.0 copy-start.4
  8.1 0.6 copy-done.4
  8.8 0.0 all-gather.2.cloned.1.call-update
  8.8 0.0 reduce-scatter.2.cloned.1.call-start
  8.9 71.9 %all-gather.2.cloned.1.call-done = f32[256,1024]{1,0:T(8,128)} async-done(((f32[256,128]{1,0:T(8,128)}), f32[256,1024]{1,0:T(8,128)}) %all-gather.2.cloned.1.call-update) | async-done | bytes 1048592 | tf_op jit(solution)/shard_map/all_gather | solution.py:41
  80.8 0.0 copy-start
  80.8 1.5 multiply_reduce_fusion.1
  82.2 0.1 copy-done
  82.3 0.2 fusion.161
  82.5 5.7 %collective-permute-start = (bf16[256,1024]{1,0:T(8,128)(2,1)S(1)}, bf16[256,1024]{1,0:T(8,128)(2,1)S(1)}, u32[]{:S(2)}, u32[]{:S(2)}) collective-permute-start(bf16[256,1024]{1,0:T(8,128)(2,1)S(1)} %fusion.161), channel_id=1, source_target_pairs={{0,1},{1,0},{2,3},{3,2},{4,5},{5,4},{6,7},{7,6},{8,9},{9,8},{10,11... | collective-permute-start | bytes 1572872 | tf_op jit(solution)/shard_map/ppermute | solution.py:10
  88.1 48.2 %collective-permute-done = bf16[256,1024]{1,0:T(8,128)(2,1)S(1)} collective-permute-done((bf16[256,1024]{1,0:T(8,128)(2,1)S(1)}, bf16[256,1024]{1,0:T(8,128)(2,1)S(1)}, u32[]{:S(2)}, u32[]{:S(2)}) %collective-permute-start) | collective-permute-done | bytes 524320 | tf_op jit(solution)/shard_map/ppermute | solution.py:10
  136.3 7.4 %collective-permute-start.1 = (bf16[256,1024]{1,0:T(8,128)(2,1)S(1)}, bf16[256,1024]{1,0:T(8,128)(2,1)S(1)}, u32[]{:S(2)}, u32[]{:S(2)}) collective-permute-start(bf16[256,1024]{1,0:T(8,128)(2,1)S(1)} %collective-permute-done), channel_id=1, source_target_pairs={{0,128},{16,144},{32,160},{48,176},{64,192},{80,208},{96,224},{112... | collective-permute-start | bytes 1572872 | tf_op jit(solution)/shard_map/ppermute | solution.py:16
  143.7 21.8 %collective-permute-done.1 = bf16[256,1024]{1,0:T(8,128)(2,1)S(1)} collective-permute-done((bf16[256,1024]{1,0:T(8,128)(2,1)S(1)}, bf16[256,1024]{1,0:T(8,128)(2,1)S(1)}, u32[]{:S(2)}, u32[]{:S(2)}) %collective-permute-start.1) | collective-permute-done | bytes 524320 | tf_op jit(solution)/shard_map/ppermute | solution.py:16
  165.5 0.1 broadcast_select_fusion
  165.5 1.9 collective-permute-start.2
  167.5 9.1 %collective-permute-done.2 = bf16[256,1024]{1,0:T(8,128)(2,1)S(1)} collective-permute-done((bf16[256,1024]{1,0:T(8,128)(2,1)S(1)}, bf16[256,1024]{1,0:T(8,128)(2,1)S(1)}, u32[]{:S(2)}, u32[]{:S(2)}) %collective-permute-start.2) | collective-permute-done | bytes 524320 | tf_op jit(solution)/shard_map/ppermute | solution.py:16
  176.6 0.1 broadcast_select_fusion.1
  176.7 2.7 collective-permute-start.3
  179.4 9.8 %collective-permute-done.3 = bf16[256,1024]{1,0:T(8,128)(2,1)S(1)} collective-permute-done((bf16[256,1024]{1,0:T(8,128)(2,1)S(1)}, bf16[256,1024]{1,0:T(8,128)(2,1)S(1)}, u32[]{:S(2)}, u32[]{:S(2)}) %collective-permute-start.3) | collective-permute-done | bytes 524320 | tf_op jit(solution)/shard_map/ppermute | solution.py:16
  189.2 0.1 broadcast_select_fusion.2
  189.3 1.9 collective-permute-start.4
  191.2 10.7 %collective-permute-done.4 = bf16[256,1024]{1,0:T(8,128)(2,1)S(1)} collective-permute-done((bf16[256,1024]{1,0:T(8,128)(2,1)S(1)}, bf16[256,1024]{1,0:T(8,128)(2,1)S(1)}, u32[]{:S(2)}, u32[]{:S(2)}) %collective-permute-start.4) | collective-permute-done | bytes 524320 | tf_op jit(solution)/shard_map/ppermute | solution.py:16
  201.9 0.0 copy-start.5
  201.9 5.6 %collective-permute-start.5 = (bf16[256,1024]{1,0:T(8,128)(2,1)S(1)}, bf16[256,1024]{1,0:T(8,128)(2,1)S(1)}, u32[]{:S(2)}, u32[]{:S(2)}) collective-permute-start(bf16[256,1024]{1,0:T(8,128)(2,1)S(1)} %collective-permute-done.4), channel_id=1, source_target_pairs={{0,16},{16,32},{32,48},{48,64},{64,80},{80,96},{96,112},{112,128},... | collective-permute-start | bytes 1572872 | tf_op jit(solution)/shard_map/ppermute | solution.py:16
  207.5 7.0 %collective-permute-done.5 = bf16[256,1024]{1,0:T(8,128)(2,1)S(1)} collective-permute-done((bf16[256,1024]{1,0:T(8,128)(2,1)S(1)}, bf16[256,1024]{1,0:T(8,128)(2,1)S(1)}, u32[]{:S(2)}, u32[]{:S(2)}) %collective-permute-start.5) | collective-permute-done | bytes 524320 | tf_op jit(solution)/shard_map/ppermute | solution.py:16
  214.5 0.0 copy-start.3
  214.5 3.5 collective-permute-start.6
  218.0 9.1 %collective-permute-done.6 = bf16[256,1024]{1,0:T(8,128)(2,1)S(1)} collective-permute-done((bf16[256,1024]{1,0:T(8,128)(2,1)S(1)}, bf16[256,1024]{1,0:T(8,128)(2,1)S(1)}, u32[]{:S(2)}, u32[]{:S(2)}) %collective-permute-start.6) | collective-permute-done | bytes 524320 | tf_op jit(solution)/shard_map/ppermute | solution.py:16
  227.1 0.0 copy-done.5
  227.1 0.0 copy-done.3
  227.1 0.0 copy-start.1
  227.1 1.9 collective-permute-start.7
  230.6 0.8 dynamic-slice_select_fusion.1
  231.3 0.9 dynamic-slice_select_fusion
  232.3 3.0 fusion.72
  235.3 0.0 copy-done.1
  235.3 4.5 %collective-permute-done.7 = bf16[256,1024]{1,0:T(8,128)(2,1)} collective-permute-done((bf16[256,1024]{1,0:T(8,128)(2,1)S(1)}, bf16[256,1024]{1,0:T(8,128)(2,1)}, u32[]{:S(2)}, u32[]{:S(2)}) %collective-permute-start.7) | collective-permute-done | bytes 524320 | tf_op jit(solution)/shard_map/ppermute | solution.py:16
  239.8 1.9 collective-permute-start.8
  241.8 3.0 convolution_add_fusion.6
  244.8 0.0 copy-start.2
  244.8 2.4 convolution_add_fusion.5
  247.2 5.5 %collective-permute-done.8 = bf16[256,1024]{1,0:T(8,128)(2,1)} collective-permute-done((bf16[256,1024]{1,0:T(8,128)(2,1)}, bf16[256,1024]{1,0:T(8,128)(2,1)}, u32[]{:S(2)}, u32[]{:S(2)}) %collective-permute-start.8) | collective-permute-done | bytes 524320 | tf_op jit(solution)/shard_map/ppermute | solution.py:16
  252.7 1.9 collective-permute-start.9
  254.7 0.0 copy-done.2
  254.7 1.8 convolution_add_fusion.4
  256.5 2.4 convolution_add_fusion.3
  258.9 6.8 %collective-permute-done.9 = bf16[256,1024]{1,0:T(8,128)(2,1)} collective-permute-done((bf16[256,1024]{1,0:T(8,128)(2,1)}, bf16[256,1024]{1,0:T(8,128)(2,1)}, u32[]{:S(2)}, u32[]{:S(2)}) %collective-permute-start.9) | collective-permute-done | bytes 524320 | tf_op jit(solution)/shard_map/ppermute | solution.py:16
  265.7 1.9 collective-permute-start.10
  267.6 3.0 convolution_add_fusion.2
  270.6 2.4 convolution_add_fusion.1
  273.0 5.5 %collective-permute-done.10 = bf16[256,1024]{1,0:T(8,128)(2,1)S(1)} collective-permute-done((bf16[256,1024]{1,0:T(8,128)(2,1)}, bf16[256,1024]{1,0:T(8,128)(2,1)S(1)}, u32[]{:S(2)}, u32[]{:S(2)}) %collective-permute-start.10) | collective-permute-done | bytes 524320 | tf_op jit(solution)/shard_map/ppermute | solution.py:16
  278.5 0.0 copy-start.6
  278.5 0.8 copy-done.6
  279.3 3.0 multiply_reduce_fusion
  282.3 2.4 subtract_divide_fusion
  284.7 0.0 reduce-scatter.2.cloned.1.call-update
  284.8 70.8 %reduce-scatter.2.cloned.1.call-done = f32[256,128]{1,0:T(8,128)} async-done(((f32[256,1024]{1,0:T(8,128)}), f32[256,128]{1,0:T(8,128)}) %reduce-scatter.2.cloned.1.call-update) | async-done | bytes 131088 | tf_op jit(solution)/shard_map/reduce_scatter | solution.py:73
  (1 shorter events, 0.0 us)
Async XLA Ops:
  6.5 74.2 %all-gather.2.cloned.1.call-start = ((), (), s32[]{:S(2)}) async-start(), calls=%async_computation.1 | async-start | bytes 1179648 | tf_op jit(solution)/shard_map/all_gather | solution.py:41
  8.1 0.7 copy-start.4
  8.8 346.7 %reduce-scatter.2.cloned.1.call-start = ((), (), s32[]{:S(2)}) async-start(), calls=%async_computation.2 | async-start | bytes 1179648 | tf_op jit(solution)/shard_map/reduce_scatter | solution.py:73
  80.8 1.5 copy-start
  82.5 53.8 %collective-permute-start = (bf16[256,1024]{1,0:T(8,128)(2,1)S(1)}, bf16[256,1024]{1,0:T(8,128)(2,1)S(1)}, u32[]{:S(2)}, u32[]{:S(2)}) collective-permute-start(bf16[256,1024]{1,0:T(8,128)(2,1)S(1)} %fusion.161), channel_id=1, source_target_pairs={{0,1},{1,0},{2,3},{3,2},{4,5},{5,4},{6,7},{7,6},{8,9},{9,8},{10,11... | collective-permute-start | bytes 1572872 | tf_op jit(solution)/shard_map/ppermute | solution.py:10
  136.3 29.2 %collective-permute-start.1 = (bf16[256,1024]{1,0:T(8,128)(2,1)S(1)}, bf16[256,1024]{1,0:T(8,128)(2,1)S(1)}, u32[]{:S(2)}, u32[]{:S(2)}) collective-permute-start(bf16[256,1024]{1,0:T(8,128)(2,1)S(1)} %collective-permute-done), channel_id=1, source_target_pairs={{0,128},{16,144},{32,160},{48,176},{64,192},{80,208},{96,224},{112... | collective-permute-start | bytes 1572872 | tf_op jit(solution)/shard_map/ppermute | solution.py:16
  165.5 11.1 %collective-permute-start.2 = (bf16[256,1024]{1,0:T(8,128)(2,1)S(1)}, bf16[256,1024]{1,0:T(8,128)(2,1)S(1)}, u32[]{:S(2)}, u32[]{:S(2)}) collective-permute-start(bf16[256,1024]{1,0:T(8,128)(2,1)S(1)} %broadcast_select_fusion), channel_id=1, source_target_pairs={{0,256},{16,272},{32,288},{48,304},{64,320},{80,336},{96,352},{112... | collective-permute-start | bytes 1572872 | tf_op jit(solution)/shard_map/ppermute | solution.py:16
  176.7 12.6 %collective-permute-start.3 = (bf16[256,1024]{1,0:T(8,128)(2,1)S(1)}, bf16[256,1024]{1,0:T(8,128)(2,1)S(1)}, u32[]{:S(2)}, u32[]{:S(2)}) collective-permute-start(bf16[256,1024]{1,0:T(8,128)(2,1)S(1)} %broadcast_select_fusion.1), channel_id=1, source_target_pairs={{0,512},{16,528},{32,544},{48,560},{64,576},{80,592},{96,608},{112... | collective-permute-start | bytes 1572872 | tf_op jit(solution)/shard_map/ppermute | solution.py:16
  189.3 12.6 %collective-permute-start.4 = (bf16[256,1024]{1,0:T(8,128)(2,1)S(1)}, bf16[256,1024]{1,0:T(8,128)(2,1)S(1)}, u32[]{:S(2)}, u32[]{:S(2)}) collective-permute-start(bf16[256,1024]{1,0:T(8,128)(2,1)S(1)} %broadcast_select_fusion.2), channel_id=1, source_target_pairs={{0,16},{16,32},{32,48},{48,64},{64,80},{80,96},{96,112},{112,128},... | collective-permute-start | bytes 1572872 | tf_op jit(solution)/shard_map/ppermute | solution.py:16
  201.9 25.2 %copy-start.5 = (bf16[256,1024]{1,0:T(8,128)(2,1)}, bf16[256,1024]{1,0:T(8,128)(2,1)S(1)}, u32[]{:S(2)}) copy-start(bf16[256,1024]{1,0:T(8,128)(2,1)S(1)} %collective-permute-done.4) | copy-start | bytes 1572868
  201.9 12.6 %collective-permute-start.5 = (bf16[256,1024]{1,0:T(8,128)(2,1)S(1)}, bf16[256,1024]{1,0:T(8,128)(2,1)S(1)}, u32[]{:S(2)}, u32[]{:S(2)}) collective-permute-start(bf16[256,1024]{1,0:T(8,128)(2,1)S(1)} %collective-permute-done.4), channel_id=1, source_target_pairs={{0,16},{16,32},{32,48},{48,64},{64,80},{80,96},{96,112},{112,128},... | collective-permute-start | bytes 1572872 | tf_op jit(solution)/shard_map/ppermute | solution.py:16
  214.5 12.6 %copy-start.3 = (bf16[256,1024]{1,0:T(8,128)(2,1)}, bf16[256,1024]{1,0:T(8,128)(2,1)S(1)}, u32[]{:S(2)}) copy-start(bf16[256,1024]{1,0:T(8,128)(2,1)S(1)} %collective-permute-done.5) | copy-start | bytes 1572868
  214.5 12.6 %collective-permute-start.6 = (bf16[256,1024]{1,0:T(8,128)(2,1)S(1)}, bf16[256,1024]{1,0:T(8,128)(2,1)S(1)}, u32[]{:S(2)}, u32[]{:S(2)}) collective-permute-start(bf16[256,1024]{1,0:T(8,128)(2,1)S(1)} %collective-permute-done.5), channel_id=1, source_target_pairs={{0,16},{16,32},{32,48},{48,64},{64,80},{80,96},{96,112},{112,128},... | collective-permute-start | bytes 1572872 | tf_op jit(solution)/shard_map/ppermute | solution.py:16
  227.1 8.2 %copy-start.1 = (bf16[256,1024]{1,0:T(8,128)(2,1)}, bf16[256,1024]{1,0:T(8,128)(2,1)S(1)}, u32[]{:S(2)}) copy-start(bf16[256,1024]{1,0:T(8,128)(2,1)S(1)} %collective-permute-done.6) | copy-start | bytes 1572868
  227.1 12.7 %collective-permute-start.7 = (bf16[256,1024]{1,0:T(8,128)(2,1)S(1)}, bf16[256,1024]{1,0:T(8,128)(2,1)}, u32[]{:S(2)}, u32[]{:S(2)}) collective-permute-start(bf16[256,1024]{1,0:T(8,128)(2,1)S(1)} %collective-permute-done.6), channel_id=1, source_target_pairs={{0,16},{16,32},{32,48},{48,64},{64,80},{80,96},{96,112},{112,128},... | collective-permute-start | bytes 1572872 | tf_op jit(solution)/shard_map/ppermute | solution.py:16
  239.8 12.9 %collective-permute-start.8 = (bf16[256,1024]{1,0:T(8,128)(2,1)}, bf16[256,1024]{1,0:T(8,128)(2,1)}, u32[]{:S(2)}, u32[]{:S(2)}) collective-permute-start(bf16[256,1024]{1,0:T(8,128)(2,1)} %collective-permute-done.7), channel_id=1, source_target_pairs={{0,16},{16,32},{32,48},{48,64},{64,80},{80,96},{96,112},{112,128},... | collective-permute-start | bytes 1572872 | tf_op jit(solution)/shard_map/ppermute | solution.py:16
  244.8 9.9 %copy-start.2 = (bf16[256,1024]{1,0:T(8,128)(2,1)S(1)}, bf16[256,1024]{1,0:T(8,128)(2,1)}, u32[]{:S(2)}) copy-start(bf16[256,1024]{1,0:T(8,128)(2,1)} %copy-done.1) | copy-start | bytes 1572868
  252.7 12.9 %collective-permute-start.9 = (bf16[256,1024]{1,0:T(8,128)(2,1)}, bf16[256,1024]{1,0:T(8,128)(2,1)}, u32[]{:S(2)}, u32[]{:S(2)}) collective-permute-start(bf16[256,1024]{1,0:T(8,128)(2,1)} %collective-permute-done.8), channel_id=1, source_target_pairs={{0,16},{16,32},{32,48},{48,64},{64,80},{80,96},{96,112},{112,128},... | collective-permute-start | bytes 1572872 | tf_op jit(solution)/shard_map/ppermute | solution.py:16
  265.7 12.8 %collective-permute-start.10 = (bf16[256,1024]{1,0:T(8,128)(2,1)}, bf16[256,1024]{1,0:T(8,128)(2,1)S(1)}, u32[]{:S(2)}, u32[]{:S(2)}) collective-permute-start(bf16[256,1024]{1,0:T(8,128)(2,1)} %collective-permute-done.9), channel_id=1, source_target_pairs={{0,16},{16,32},{32,48},{48,64},{64,80},{80,96},{96,112},{112,128},... | collective-permute-start | bytes 1572872 | tf_op jit(solution)/shard_map/ppermute | solution.py:16
  278.5 0.8 copy-start.6
Sparse Core Ops, SparseCore 0:
  9.9 70.7 all-gather.1
  284.9 70.6 reduce-scatter.1
where the time goes:
time: 363 us; the launch traced here: 362 us
  waiting for transfers between devices  281 us (77%)
  starting transfers between devices  36.3 us (10%)
  matrix products  22.7 us (6%)
  between operations  15.1 us (4%)
  other arithmetic  5.9 us (2%)
    ppermute x10, waiting for transfers between devices, passed_along(): return lax.ppermute(value, axis, pairs)  90 us
    all_gather x1, waiting for transfers between devices, shards(): whole = lax.all_gather(shard, 'mp', axis=1, tiled=True)  71.9 us
    reduce_scatter x1, waiting for transfers between devices, shards(): lax.psum_scatter(partial_grads, 'mp', scatter_dimension=1, tiled=True)  70.8 us
    ppermute x1, waiting for transfers between devices, partner(): return lax.ppermute(value, axis, pairs)  48.2 us
    ppermute x10, starting transfers between devices, passed_along(): return lax.ppermute(value, axis, pairs)  30.6 us
    dot_general x8, matrix products, pair_tile(): return jnp.dot(weight, other_b, preferred_element_type=jnp.float32)  21.1 us
  transfers between devices with their start and end apart: 13, of which 13 were waited for; matrix products, arithmetic and copies ran while one was open for 5% of the time, Pallas kernels for 0%

commit v1 on v0

v1 whole, which is shorter than its diff:
```python
import jax
import jax.numpy as jnp
from jax import lax
from jax.sharding import Mesh, PartitionSpec as P

BLK = ("x", "ya", "yb", "c")
AXES = BLK + ("zl", "zh")
COLUMN = ("zh", "zl")
IMAGE_GROUP = ("x", "yb")
F32 = jnp.float32


def spread(value, axis):
    count = lax.axis_size(axis)
    copies = jnp.broadcast_to(value[None], (count,) + value.shape)
    return lax.all_to_all(copies, axis, 0, 0, tiled=True)


def summed(parts, axis):
    count = lax.axis_size(axis)
    parts = parts.reshape((count, -1) + parts.shape[1:])
    return jnp.sum(lax.all_to_all(parts, axis, 0, 0, tiled=True).astype(F32), axis=0)


def swapped(value):
    return lax.ppermute(value, "c", [(0, 1), (1, 0)])


def normalize(embed):
    norm = jnp.sqrt(jnp.sum(embed * embed, axis=1, keepdims=True) + 1e-06)
    return embed / norm, norm


def projected(grad, unit, norm):
    return (grad - unit * jnp.sum(unit * grad, axis=1, keepdims=True)) / norm


def shards(image_features, text_features, image_head, text_head, positive, log_scale, bias):
    rows = image_features.shape[0]
    planes = lax.axis_size(COLUMN)
    lanes = lax.axis_size("zl")
    quarter = rows // 4
    half = quarter // 2
    x, ya, yb, c = (lax.axis_index(name) for name in BLK)
    zh = lax.axis_index("zh")
    plane = zh * lanes + lax.axis_index("zl")
    image_part, text_part = plane // 4, plane % 4
    scale = jnp.exp(log_scale[0])
    offset = bias[0]

    def head_part(features, head):
        own = features.reshape(4, 2, half, -1)
        own = lax.dynamic_index_in_dim(own, zh, 1, keepdims=False).reshape(4 * half, -1)
        return jnp.dot(own, head, preferred_element_type=F32).reshape(4, half, -1)

    image_cols = head_part(image_features, image_head)
    text_cols = head_part(text_features, text_head)
    width = image_cols.shape[-1]
    pieces = jnp.concatenate(
        [
            jnp.broadcast_to(image_cols[:, None], (4, 4, half, width)),
            jnp.broadcast_to(text_cols[None], (4, 4, half, width)),
        ],
        axis=2,
    ).reshape(planes, 2 * half, width)
    pieces = lax.all_to_all(pieces, COLUMN, 0, 0, tiled=True)
    pieces = pieces.reshape(2, lanes, 2, half, width)
    whole = pieces.transpose(2, 0, 3, 1, 4).reshape(2, quarter, lanes * width)
    image_unit, image_norm = normalize(whole[0])
    text_unit, text_norm = normalize(whole[1])

    text_own = spread(text_unit.astype(jnp.bfloat16), "ya").reshape(4 * quarter, -1)
    text_far = swapped(text_own)
    image_b = spread(image_unit.astype(jnp.bfloat16), IMAGE_GROUP).reshape(8 * quarter, -1)

    keys = positive.reshape(4, 4, 2, 2, 4, quarter)
    keys = lax.dynamic_slice(keys, (0, ya, 0, c, image_part, 0), (4, 1, 2, 1, 1, quarter))
    keys = keys.reshape(8 * quarter)

    def text_index(core):
        block = ((x * 4 + jnp.arange(4, dtype=jnp.int32)) * 2 + yb) * 2 + core
        start = block * rows + text_part * quarter
        return (start[:, None] + jnp.arange(quarter, dtype=jnp.int32)[None]).reshape(-1)

    def weights(text_b, index):
        logits = scale * jnp.einsum("re,ce->rc", image_b, text_b, preferred_element_type=F32)
        logits = logits + offset
        sign = jnp.where(keys[:, None] == index[None, :], 1.0, -1.0)
        return (-sign * jax.nn.sigmoid(-sign * logits) * scale).astype(jnp.bfloat16)

    def to_texts(weight):
        return jnp.einsum("rc,re->ce", weight, image_b, preferred_element_type=F32)

    def to_images(weight, text_b):
        return jnp.dot(weight, text_b, preferred_element_type=F32)

    weight_far = weights(text_far, text_index(1 - c))
    far_grad = swapped(to_texts(weight_far))
    weight_own = weights(text_own, text_index(c))
    image_grad = to_images(weight_far, text_far) + to_images(weight_own, text_own)
    text_grad = to_texts(weight_own) + far_grad

    image_grad = summed(image_grad.astype(jnp.bfloat16), IMAGE_GROUP)
    text_grad = summed(text_grad.astype(jnp.bfloat16), "ya")
    both = jnp.stack(
        [projected(image_grad, image_unit, image_norm), projected(text_grad, text_unit, text_norm)]
    )
    both = both.reshape(2, quarter, lanes, width).transpose(0, 2, 1, 3)
    both = lax.all_to_all(both.reshape(planes, quarter, width), COLUMN, 0, 0, tiled=True)
    both = both.reshape(4, 4, quarter, width)
    result = jnp.where(zh == 0, jnp.sum(both, axis=1), jnp.sum(both, axis=0))
    return result.reshape(1, rows, width)


def solution(mesh):
    fine = Mesh(mesh.devices.reshape(4, 4, 2, 2, 8, 2), AXES)
    placed = (P(BLK, None), P(BLK, None), P(None, "zl"), P(None, "zl"), P(), P(), P())
    return jax.shard_map(
        shards, mesh=fine, in_specs=placed, out_specs=P("zh", BLK, "zl"), check_vma=False
    )
```

time: 363 us -> 184 us (0.51)
  the two profiles are of different devices: /device:TPU:6 before, /device:TPU:26 now
where the time goes in v1:
time: 184 us; the launch traced here: 183 us
  waiting for transfers between devices  71.1 us (39%)
  blocking collectives  47.8 us (26%)
  starting transfers between devices  41.1 us (22%)
  matrix products  12.6 us (7%)
  local copies, waits for them, and re-layouts  6.72 us (4%)
  other arithmetic  2.21 us (1%)
    all_to_all x1, blocking collectives, shards(): pieces = lax.all_to_all(pieces, COLUMN, 0, 0, tiled=True)  47.8 us
    all_to_all x1, waiting for transfers between devices, shards(): lax.all_to_all(both.reshape(planes, quarter, width), COLUMN, 0, 0, tiled=...  29.2 us
    all_to_all x2, waiting for transfers between devices, summed(): lax.all_to_all(parts, axis, 0, 0, tiled=True).astype(F32)  24.3 us
    all_to_all x2, waiting for transfers between devices, spread(): return lax.all_to_all(copies, axis, 0, 0, tiled=True)  15.4 us
    all_to_all x1, starting transfers between devices, shards(): lax.all_to_all(both.reshape(planes, quarter, width), COLUMN, 0, 0, tiled=...  13.9 us
    all_to_all x2, starting transfers between devices, spread(): return lax.all_to_all(copies, axis, 0, 0, tiled=True)  12.3 us
    all_to_all x2, starting transfers between devices, summed(): lax.all_to_all(parts, axis, 0, 0, tiled=True).astype(F32)  11.2 us
    dot_general x2, matrix products, to_texts(): return jnp.einsum('rc,re->ce', weight, image_b, preferred_element_type=F32)  4.01 us
  transfers between devices with their start and end apart: 7, of which 6 were waited for; matrix products, arithmetic and copies ran while one was open for 3% of the time, Pallas kernels for 0%

profile of v1, /device:TPU:26, one launch (start us, length us, event | category | flops | bytes accessed | tf_op | source)
XLA Modules:
  0.0 183.1 jit_solution(11836784326758946940)
XLA Ops:
  0.0 0.0 copy-start
  0.0 1.1 copy-done
  1.1 1.2 fusion.19
  2.4 1.3 fusion.27
  3.7 47.8 %all_to_all.30 = f32[16,64,128]{2,1,0:T(8,128)S(1)} all-to-all(f32[16,64,128]{2,1,0:T(8,128)S(1)} %bitcast.98), channel_id=1, replica_groups=mesh['x'=4,'ya'=4,'yb'=2,'c'=2,'zl'=8,'zh'=2] {'zh','zl'}, dimensions={0} | all-to-all | bytes 1048576 | tf_op jit(solution)/shard_map/all_to_all | solution.py:66
  51.5 0.1 multiply_reduce_fusion
  51.7 0.1 sqrt.27
  51.7 0.2 copy.16
  51.9 0.1 fusion.25
  52.0 0.8 broadcast_in_dim.23
  52.9 6.5 %all-to-all-start.2 = ((bf16[4,64,1024]{2,1,0:T(8,128)(2,1)}), bf16[4,64,1024]{2,1,0:T(8,128)(2,1)S(1)}, u32[]{:S(2)}, u32[]{:S(2)}) async-start(bf16[4,64,1024]{2,1,0:T(8,128)(2,1)} %broadcast_in_dim.23), calls=%async_computation.2 | async-start | bytes 1048576 | tf_op jit(solution)/shard_map/all_to_all | solution.py:16
  59.4 0.1 sqrt.25
  59.5 0.0 copy-start.4
  59.5 0.2 copy.15
  59.6 0.1 fusion.26
  59.7 10.5 %all-to-all-done.2 = bf16[4,64,1024]{2,1,0:T(8,128)(2,1)S(1)} async-done(((bf16[4,64,1024]{2,1,0:T(8,128)(2,1)}), bf16[4,64,1024]{2,1,0:T(8,128)(2,1)S(1)}, u32[]{:S(2)}, u32[]{:S(2)}) %all-to-all-start.2) | async-done | bytes 524320 | tf_op jit(solution)/shard_map/all_to_all | solution.py:16
  70.2 1.1 broadcast_in_dim.22
  71.3 0.0 copy-done.4
  71.3 5.7 %all-to-all-start.1 = ((bf16[8,64,1024]{2,1,0:T(8,128)(2,1)}), bf16[8,64,1024]{2,1,0:T(8,128)(2,1)S(1)}, u32[]{:S(2)}, u32[]{:S(2)}) async-start(bf16[8,64,1024]{2,1,0:T(8,128)(2,1)} %broadcast_in_dim.22), calls=%async_computation.1 | async-start | bytes 2097152 | tf_op jit(solution)/shard_map/all_to_all | solution.py:16
  77.1 1.9 %collective-permute-start = (bf16[256,1024]{1,0:T(8,128)(2,1)S(1)}, bf16[256,1024]{1,0:T(8,128)(2,1)}, u32[]{:S(2)}, u32[]{:S(2)}) collective-permute-start(bf16[256,1024]{1,0:T(8,128)(2,1)S(1)} %bitcast.99), channel_id=1, source_target_pairs={{0,16},{16,0},{1,17},{17,1},{2,18},{18,2},{3,19},{19,3},{4,20},{20... | collective-permute-start | bytes 1572872 | tf_op jit(solution)/shard_map/ppermute | solution.py:26
  79.0 1.0 reshape.313
  80.0 0.1 eq.32
  80.1 0.1 iota_add_fusion.1
  80.2 0.1 add.189
  81.6 0.0 collective-permute-done
  81.6 4.9 %all-to-all-done.1 = bf16[8,64,1024]{2,1,0:T(8,128)(2,1)S(1)} async-done(((bf16[8,64,1024]{2,1,0:T(8,128)(2,1)}), bf16[8,64,1024]{2,1,0:T(8,128)(2,1)S(1)}, u32[]{:S(2)}, u32[]{:S(2)}) %all-to-all-start.1) | async-done | bytes 1048608 | tf_op jit(solution)/shard_map/all_to_all | solution.py:16
  86.5 1.6 fusion.17
  88.1 0.0 copy-start.1
  88.1 0.7 copy-done.1
  88.8 1.5 fusion.36
  90.3 1.9 %collective-permute-start.1 = (f32[256,1024]{1,0:T(8,128)}, f32[256,1024]{1,0:T(8,128)}, u32[]{:S(2)}, u32[]{:S(2)}) collective-permute-start(f32[256,1024]{1,0:T(8,128)} %fusion.36), channel_id=1, source_target_pairs={{0,16},{16,0},{1,17},{17,1},{2,18},{18,2},{3,19},{19,3},{4,20},{20... | collective-permute-start | bytes 3145736 | tf_op jit(solution)/shard_map/ppermute | solution.py:26
  92.3 0.1 iota_add_fusion
  92.3 0.1 add.202
  92.4 0.6 fusion.18
  93.0 0.0 copy-start.3
  93.0 2.2 %collective-permute-done.1 = f32[256,1024]{1,0:T(8,128)} collective-permute-done((f32[256,1024]{1,0:T(8,128)}, f32[256,1024]{1,0:T(8,128)}, u32[]{:S(2)}, u32[]{:S(2)}) %collective-permute-start.1) | collective-permute-done | bytes 1048608 | tf_op jit(solution)/shard_map/ppermute | solution.py:26
  95.2 2.5 %fusion = bf16[256,1024]{1,0:T(8,128)(2,1)} fusion(f32[256,1024]{1,0:T(8,128)} %collective-permute-done.1, bf16[512,256]{1,0:T(8,128)(2,1)S(1)} %fusion.18, bf16[512,1024]{1,0:T(8,128)(2,1)S(1)} %bitcast.86), kind=kOutput, calls=%fused_computation.3 | convolution fusion | flops 268959744 | bytes 2883584 | tf_op jit(solution)/shard_map/rc,re->ce/dot_general | solution.py:92
  97.7 0.0 copy-done.3
  97.7 0.0 copy-start.2
  97.7 4.5 %all-to-all-start.4 = ((bf16[4,64,1024]{2,1,0:T(8,128)(2,1)}), bf16[4,64,1024]{2,1,0:T(8,128)(2,1)S(1)}, u32[]{:S(2)}, u32[]{:S(2)}) async-start(bf16[4,64,1024]{2,1,0:T(8,128)(2,1)} %bitcast.102), calls=%async_computation.4 | async-start | bytes 1048576 | tf_op jit(solution)/shard_map/all_to_all | solution.py:22
  102.2 1.4 fusion.35
  103.6 0.0 copy-done.2
  103.6 2.5 %add_convert_fusion = bf16[512,1024]{1,0:T(8,128)(2,1)} fusion(f32[512,1024]{1,0:T(8,128)S(1)} %fusion.35, bf16[512,256]{1,0:T(8,128)(2,1)S(1)} %copy-done.2, bf16[256,1024]{1,0:T(8,128)(2,1)} %collective-permute-done), kind=kOutput, calls=%fused_computation.1 | convolution fusion | flops 269484032 | bytes 3932160 | tf_op jit(solution)/shard_map/dot_general | solution.py:95
  106.1 10.8 %all-to-all-done.4 = bf16[4,64,1024]{2,1,0:T(8,128)(2,1)S(1)} async-done(((bf16[4,64,1024]{2,1,0:T(8,128)(2,1)}), bf16[4,64,1024]{2,1,0:T(8,128)(2,1)S(1)}, u32[]{:S(2)}, u32[]{:S(2)}) %all-to-all-start.4) | async-done | bytes 524320 | tf_op jit(solution)/shard_map/all_to_all | solution.py:22
  116.9 6.6 %all-to-all-start.3 = ((bf16[8,64,1024]{2,1,0:T(8,128)(2,1)}), bf16[8,64,1024]{2,1,0:T(8,128)(2,1)S(1)}, u32[]{:S(2)}, u32[]{:S(2)}) async-start(bf16[8,64,1024]{2,1,0:T(8,128)(2,1)} %bitcast.14), calls=%async_computation.3 | async-start | bytes 2097152 | tf_op jit(solution)/shard_map/all_to_all | solution.py:22
  123.6 0.0 copy-start.5
  123.6 0.1 convert_reduce_fusion.1
  123.7 13.6 %all-to-all-done.3 = bf16[8,64,1024]{2,1,0:T(8,128)(2,1)S(1)} async-done(((bf16[8,64,1024]{2,1,0:T(8,128)(2,1)}), bf16[8,64,1024]{2,1,0:T(8,128)(2,1)S(1)}, u32[]{:S(2)}, u32[]{:S(2)}) %all-to-all-start.3) | async-done | bytes 1048608 | tf_op jit(solution)/shard_map/all_to_all | solution.py:22
  137.2 0.2 convert_reduce_fusion
  137.5 0.3 fusion.31
  137.7 0.1 mul.148
  137.8 0.1 mul.152
  137.9 0.0 copy-done.5
  137.9 0.2 fusion.24
  138.1 0.2 fusion.23
  138.4 0.9 copy.21
  139.3 13.9 %all-to-all-start.5 = ((f32[16,64,128]{2,1,0:T(8,128)}), f32[16,64,128]{2,1,0:T(8,128)S(1)}, u32[]{:S(2)}, u32[]{:S(2)}) async-start(f32[16,64,128]{2,1,0:T(8,128)} %bitcast.19), calls=%async_computation.5 | async-start | bytes 1048576 | tf_op jit(solution)/shard_map/all_to_all | solution.py:109
  153.2 29.2 %all-to-all-done.5 = f32[16,64,128]{2,1,0:T(8,128)S(1)} async-done(((f32[16,64,128]{2,1,0:T(8,128)}), f32[16,64,128]{2,1,0:T(8,128)S(1)}, u32[]{:S(2)}, u32[]{:S(2)}) %all-to-all-start.5) | async-done | bytes 524320 | tf_op jit(solution)/shard_map/all_to_all | solution.py:109
  182.4 0.7 broadcast_select_fusion
  (11 shorter events, 0.3 us)
Async XLA Ops:
  0.0 1.1 copy-start
  52.9 17.4 %all-to-all-start.2 = ((bf16[4,64,1024]{2,1,0:T(8,128)(2,1)}), bf16[4,64,1024]{2,1,0:T(8,128)(2,1)S(1)}, u32[]{:S(2)}, u32[]{:S(2)}) async-start(bf16[4,64,1024]{2,1,0:T(8,128)(2,1)} %broadcast_in_dim.23), calls=%async_computation.2 | async-start | bytes 1048576 | tf_op jit(solution)/shard_map/all_to_all | solution.py:16
  59.5 11.9 %copy-start.4 = (f32[64]{0:T(128)}, f32[64]{0:T(128)S(1)}, u32[]{:S(2)}) copy-start(f32[64]{0:T(128)S(1)} %sqrt.25) | copy-start | bytes 772
  71.3 15.2 %all-to-all-start.1 = ((bf16[8,64,1024]{2,1,0:T(8,128)(2,1)}), bf16[8,64,1024]{2,1,0:T(8,128)(2,1)S(1)}, u32[]{:S(2)}, u32[]{:S(2)}) async-start(bf16[8,64,1024]{2,1,0:T(8,128)(2,1)} %broadcast_in_dim.22), calls=%async_computation.1 | async-start | bytes 2097152 | tf_op jit(solution)/shard_map/all_to_all | solution.py:16
  77.1 4.5 %collective-permute-start = (bf16[256,1024]{1,0:T(8,128)(2,1)S(1)}, bf16[256,1024]{1,0:T(8,128)(2,1)}, u32[]{:S(2)}, u32[]{:S(2)}) collective-permute-start(bf16[256,1024]{1,0:T(8,128)(2,1)S(1)} %bitcast.99), channel_id=1, source_target_pairs={{0,16},{16,0},{1,17},{17,1},{2,18},{18,2},{3,19},{19,3},{4,20},{20... | collective-permute-start | bytes 1572872 | tf_op jit(solution)/shard_map/ppermute | solution.py:26
  88.1 0.7 copy-start.1
  90.3 4.9 %collective-permute-start.1 = (f32[256,1024]{1,0:T(8,128)}, f32[256,1024]{1,0:T(8,128)}, u32[]{:S(2)}, u32[]{:S(2)}) collective-permute-start(f32[256,1024]{1,0:T(8,128)} %fusion.36), channel_id=1, source_target_pairs={{0,16},{16,0},{1,17},{17,1},{2,18},{18,2},{3,19},{19,3},{4,20},{20... | collective-permute-start | bytes 3145736 | tf_op jit(solution)/shard_map/ppermute | solution.py:26
  93.0 4.7 %copy-start.3 = (bf16[512,256]{1,0:T(8,128)(2,1)}, bf16[512,256]{1,0:T(8,128)(2,1)S(1)}, u32[]{:S(2)}) copy-start(bf16[512,256]{1,0:T(8,128)(2,1)S(1)} %fusion.18) | copy-start | bytes 786436
  97.7 5.9 %copy-start.2 = (bf16[512,256]{1,0:T(8,128)(2,1)S(1)}, bf16[512,256]{1,0:T(8,128)(2,1)}, u32[]{:S(2)}) copy-start(bf16[512,256]{1,0:T(8,128)(2,1)} %copy-done.1) | copy-start | bytes 786436
  97.7 19.2 %all-to-all-start.4 = ((bf16[4,64,1024]{2,1,0:T(8,128)(2,1)}), bf16[4,64,1024]{2,1,0:T(8,128)(2,1)S(1)}, u32[]{:S(2)}, u32[]{:S(2)}) async-start(bf16[4,64,1024]{2,1,0:T(8,128)(2,1)} %bitcast.102), calls=%async_computation.4 | async-start | bytes 1048576 | tf_op jit(solution)/shard_map/all_to_all | solution.py:22
  116.9 20.3 %all-to-all-start.3 = ((bf16[8,64,1024]{2,1,0:T(8,128)(2,1)}), bf16[8,64,1024]{2,1,0:T(8,128)(2,1)S(1)}, u32[]{:S(2)}, u32[]{:S(2)}) async-start(bf16[8,64,1024]{2,1,0:T(8,128)(2,1)} %bitcast.14), calls=%async_computation.3 | async-start | bytes 2097152 | tf_op jit(solution)/shard_map/all_to_all | solution.py:22
  123.6 14.3 %copy-start.5 = (f32[64]{0:T(128)S(1)}, f32[64]{0:T(128)}, u32[]{:S(2)}) copy-start(f32[64]{0:T(128)} %copy-done.4) | copy-start | bytes 772
  139.3 43.1 %all-to-all-start.5 = ((f32[16,64,128]{2,1,0:T(8,128)}), f32[16,64,128]{2,1,0:T(8,128)S(1)}, u32[]{:S(2)}, u32[]{:S(2)}) async-start(f32[16,64,128]{2,1,0:T(8,128)} %bitcast.19), calls=%async_computation.5 | async-start | bytes 1048576 | tf_op jit(solution)/shard_map/all_to_all | solution.py:109

commit v2 on v1

--- a/solution.py
+++ b/solution.py
@@ -26,13 +26,22 @@
     return lax.ppermute(value, "c", [(0, 1), (1, 0)])
 
 
+def shifted(value, axis, steps):
+    count = lax.axis_size(axis)
+    return lax.ppermute(value, axis, [(k, (k + steps) % count) for k in range(count)])
+
+
+def floor_power(value):
+    return jnp.floor(jnp.log2(value))
+
+
 def normalize(embed):
     norm = jnp.sqrt(jnp.sum(embed * embed, axis=1, keepdims=True) + 1e-06)
     return embed / norm, norm
 
 
-def projected(grad, unit, norm):
-    return (grad - unit * jnp.sum(unit * grad, axis=1, keepdims=True)) / norm
+def projected(grad, unit):
+    return grad - unit * jnp.sum(unit * grad, axis=1, keepdims=True)
 
 
 def shards(image_features, text_features, image_head, text_head, positive, log_scale, bias):
@@ -69,7 +78,8 @@
     image_unit, image_norm = normalize(whole[0])
     text_unit, text_norm = normalize(whole[1])
 
-    text_own = spread(text_unit.astype(jnp.bfloat16), "ya").reshape(4 * quarter, -1)
+    text_b = text_unit.astype(jnp.bfloat16)
+    text_own = jnp.concatenate([text_b] + [shifted(text_b, "ya", k) for k in range(1, 4)])
     text_far = swapped(text_own)
     image_b = spread(image_unit.astype(jnp.bfloat16), IMAGE_GROUP).reshape(8 * quarter, -1)
 
@@ -78,7 +88,7 @@
     keys = keys.reshape(8 * quarter)
 
     def text_index(core):
-        block = ((x * 4 + jnp.arange(4, dtype=jnp.int32)) * 2 + yb) * 2 + core
+        block = ((x * 4 + (ya - jnp.arange(4, dtype=jnp.int32)) % 4) * 2 + yb) * 2 + core
         start = block * rows + text_part * quarter
         return (start[:, None] + jnp.arange(quarter, dtype=jnp.int32)[None]).reshape(-1)
 
@@ -100,15 +110,26 @@
     image_grad = to_images(weight_far, text_far) + to_images(weight_own, text_own)
     text_grad = to_texts(weight_own) + far_grad
 
-    image_grad = summed(image_grad.astype(jnp.bfloat16), IMAGE_GROUP)
-    text_grad = summed(text_grad.astype(jnp.bfloat16), "ya")
-    both = jnp.stack(
-        [projected(image_grad, image_unit, image_norm), projected(text_grad, text_unit, text_norm)]
-    )
+    text_parts = text_grad.astype(jnp.float16).reshape(4, quarter, -1)
+    text_grad = text_parts[0].astype(F32)
+    for k in range(1, 4):
+        text_grad = text_grad + shifted(text_parts[k], "ya", -k).astype(F32)
+    image_grad = summed(image_grad.astype(jnp.float16), IMAGE_GROUP)
+
+    both = jnp.stack([projected(image_grad, image_unit), projected(text_grad, text_unit)])
+    norms = jnp.stack([image_norm, text_norm])
+    powers = floor_power(norms)
+    both = (both * (jnp.exp2(powers) / norms)).astype(jnp.float16)
     both = both.reshape(2, quarter, lanes, width).transpose(0, 2, 1, 3)
-    both = lax.all_to_all(both.reshape(planes, quarter, width), COLUMN, 0, 0, tiled=True)
-    both = both.reshape(4, 4, quarter, width)
+    powers = jnp.pad(powers.reshape(2, 1, quarter), ((0, 0), (0, 15), (0, width - quarter)))
+    powers = jnp.broadcast_to(powers[:, None], (2, lanes, 16, width)).astype(jnp.float16)
+    both = jnp.concatenate([both, powers], axis=2).reshape(planes, quarter + 16, width)
+    both = lax.all_to_all(both, COLUMN, 0, 0, tiled=True)
+    powers = both[:, quarter, :quarter].astype(F32).reshape(4, 4, quarter)
+    powers = jnp.where(zh == 0, powers[:, 0], powers[0])
+    both = both[:, :quarter].astype(F32).reshape(4, 4, quarter, width)
     result = jnp.where(zh == 0, jnp.sum(both, axis=1), jnp.sum(both, axis=0))
+    result = result / jnp.exp2(powers)[:, :, None]
     return result.reshape(1, rows, width)
 
 

time: 184 us -> 167 us (0.908)
  the two profiles are of different devices: /device:TPU:26 before, /device:TPU:6 now
where the time goes in v2:
time: 167 us
  starting transfers between devices  54.8 us (33%)
  blocking collectives  47.8 us (29%)
  waiting for transfers between devices  34.8 us (21%)
  local copies, waits for them, and re-layouts  11.6 us (7%)
  matrix products  9.45 us (6%)
  other arithmetic  6.3 us (4%)
  between operations  1.84 us (1%)
    all_to_all x1, blocking collectives, shards(): pieces = lax.all_to_all(pieces, COLUMN, 0, 0, tiled=True)  47.8 us
    ppermute x6, starting transfers between devices, shifted(): lax.ppermute(value, axis, [(k, (k + steps) % count) for k in range(count)])  26 us
    all_to_all x1, waiting for transfers between devices, shards(): both = lax.all_to_all(both, COLUMN, 0, 0, tiled=True)  20.8 us
    ppermute x6, waiting for transfers between devices, shifted(): lax.ppermute(value, axis, [(k, (k + steps) % count) for k in range(count)])  14 us
    all_to_all x1, starting transfers between devices, shards(): both = lax.all_to_all(both, COLUMN, 0, 0, tiled=True)  11.7 us
    all_to_all x1, starting transfers between devices, summed(): lax.all_to_all(parts, axis, 0, 0, tiled=True).astype(F32)  7.01 us
    all_to_all x1, starting transfers between devices, spread(): return lax.all_to_all(copies, axis, 0, 0, tiled=True)  5.79 us
    ppermute x2, starting transfers between devices, swapped(): return lax.ppermute(value, 'c', [(0, 1), (1, 0)])  4.31 us
  transfers between devices with their start and end apart: 11, of which 6 were waited for; matrix products, arithmetic and copies ran while one was open for 8% of the time, Pallas kernels for 0%

profile of v2, /device:TPU:6, one launch (start us, length us, event | category | flops | bytes accessed | tf_op | source)
XLA Modules:
  0.0 166.6 jit_solution(13199447347979528274)
XLA Ops:
  0.0 1.3 fusion.26
  1.3 1.3 fusion.20
  2.7 47.8 %all_to_all.20 = f32[16,64,128]{2,1,0:T(8,128)S(1)} all-to-all(f32[16,64,128]{2,1,0:T(8,128)S(1)} %bitcast.92), channel_id=1, replica_groups=mesh['x'=4,'ya'=4,'yb'=2,'c'=2,'zl'=8,'zh'=2] {'zh','zl'}, dimensions={0} | all-to-all | bytes 1048576 | tf_op jit(solution)/shard_map/all_to_all | solution.py:75
  50.5 0.8 copy-done.1
  51.2 0.1 multiply_reduce_fusion.2
  51.4 0.2 copy.16
  51.6 0.1 sqrt.66
  51.6 0.1 fusion.25
  51.7 1.1 broadcast_in_dim.22
  52.8 5.8 %all-to-all-start.1 = ((bf16[8,64,1024]{2,1,0:T(8,128)(2,1)}), bf16[8,64,1024]{2,1,0:T(8,128)(2,1)S(1)}, u32[]{:S(2)}, u32[]{:S(2)}) async-start(bf16[8,64,1024]{2,1,0:T(8,128)(2,1)} %broadcast_in_dim.22), calls=%async_computation.1 | async-start | bytes 2097152 | tf_op jit(solution)/shard_map/all_to_all | solution.py:16
  58.6 0.1 sqrt.68
  58.7 0.5 copy-done.15
  59.2 0.2 copy.17
  59.4 0.1 fusion.44
  59.5 5.3 %collective-permute-start.2 = (bf16[64,1024]{1,0:T(8,128)(2,1)S(1)}, bf16[64,1024]{1,0:T(8,128)(2,1)S(1)}, u32[]{:S(2)}, u32[]{:S(2)}) collective-permute-start(bf16[64,1024]{1,0:T(8,128)(2,1)S(1)} %fusion.44), channel_id=1, source_target_pairs={{0,192},{64,0},{128,64},{192,128},{1,193},{65,1},{129,65},{193,129... | collective-permute-start | bytes 393224 | tf_op jit(solution)/shard_map/ppermute | solution.py:31
  64.7 4.7 %collective-permute-start.1 = (bf16[64,1024]{1,0:T(8,128)(2,1)S(1)}, bf16[64,1024]{1,0:T(8,128)(2,1)S(1)}, u32[]{:S(2)}, u32[]{:S(2)}) collective-permute-start(bf16[64,1024]{1,0:T(8,128)(2,1)S(1)} %fusion.44), channel_id=1, source_target_pairs={{0,128},{64,192},{128,0},{192,64},{1,129},{65,193},{129,1},{193,65... | collective-permute-start | bytes 393224 | tf_op jit(solution)/shard_map/ppermute | solution.py:31
  69.5 3.6 %collective-permute-start = (bf16[64,1024]{1,0:T(8,128)(2,1)S(1)}, bf16[64,1024]{1,0:T(8,128)(2,1)S(1)}, u32[]{:S(2)}, u32[]{:S(2)}) collective-permute-start(bf16[64,1024]{1,0:T(8,128)(2,1)S(1)} %fusion.44), channel_id=1, source_target_pairs={{0,64},{64,128},{128,192},{192,0},{1,65},{65,129},{129,193},{193,1... | collective-permute-start | bytes 393224 | tf_op jit(solution)/shard_map/ppermute | solution.py:31
  74.5 3.8 %collective-permute-done.1 = bf16[64,1024]{1,0:T(8,128)(2,1)S(1)} collective-permute-done((bf16[64,1024]{1,0:T(8,128)(2,1)S(1)}, bf16[64,1024]{1,0:T(8,128)(2,1)S(1)}, u32[]{:S(2)}, u32[]{:S(2)}) %collective-permute-start.1) | collective-permute-done | bytes 131104 | tf_op jit(solution)/shard_map/ppermute | solution.py:31
  78.2 1.3 collective-permute-done
  79.5 0.7 copy-done.9
  80.2 1.9 %collective-permute-start.3 = (bf16[256,1024]{1,0:T(8,128)(2,1)S(1)}, bf16[256,1024]{1,0:T(8,128)(2,1)S(1)}, u32[]{:S(2)}, u32[]{:S(2)}) collective-permute-start(bf16[256,1024]{1,0:T(8,128)(2,1)S(1)} %pad_maximum_fusion.1), channel_id=1, source_target_pairs={{0,16},{16,0},{1,17},{17,1},{2,18},{18,2},{3,19},{19,3},{4,20},{20... | collective-permute-start | bytes 1572872 | tf_op jit(solution)/shard_map/ppermute | solution.py:26
  82.2 0.6 multiply_add_fusion
  82.7 0.1 iota_add_fusion.1
  82.8 0.6 add.253
  83.4 1.6 reshape.421
  85.0 0.7 dynamic-slice_reduce_fusion
  85.8 0.1 eq.36
  85.9 0.7 iota_add_fusion
  86.6 0.6 add.266
  87.2 1.2 fusion.17
  88.5 1.4 fusion.47
  89.9 2.4 %collective-permute-start.4 = (f32[256,1024]{1,0:T(8,128)}, f32[256,1024]{1,0:T(8,128)}, u32[]{:S(2)}, u32[]{:S(2)}) collective-permute-start(f32[256,1024]{1,0:T(8,128)} %fusion.47), channel_id=1, source_target_pairs={{0,16},{16,0},{1,17},{17,1},{2,18},{18,2},{3,19},{19,3},{4,20},{20... | collective-permute-start | bytes 3145736 | tf_op jit(solution)/shard_map/ppermute | solution.py:26
  92.4 0.6 fusion.18
  93.0 0.7 copy-done.4
  93.6 0.4 fusion.45
  94.1 1.4 add_convert_fusion
  95.5 7.0 %all-to-all-start.2 = ((f16[8,64,1024]{2,1,0:T(8,128)(2,1)}), f16[8,64,1024]{2,1,0:T(8,128)(2,1)S(1)}, u32[]{:S(2)}, u32[]{:S(2)}) async-start(f16[8,64,1024]{2,1,0:T(8,128)(2,1)} %bitcast.85), calls=%async_computation.2 | async-start | bytes 2097152 | tf_op jit(solution)/shard_map/all_to_all | solution.py:22
  102.5 0.1 stack.22
  102.6 0.6 stack.21
  103.2 1.8 %fusion = f16[256,1024]{1,0:T(8,128)(2,1)S(1)} fusion(f32[256,1024]{1,0:T(8,128)} %collective-permute-done.4, bf16[512,256]{1,0:T(8,128)(2,1)} %copy-done.4, bf16[512,1024]{1,0:T(8,128)(2,1)S(1)} %bitcast.81), kind=kOutput, calls=%fused_computation.3 | convolution fusion | flops 268959744 | bytes 2883584 | tf_op jit(solution)/shard_map/rc,re->ce/dot_general | solution.py:102
  105.0 0.8 copy-done.3
  105.8 0.7 fusion.46
  106.5 2.8 %collective-permute-start.7 = (f16[64,1024]{1,0:T(8,128)(2,1)}, f16[64,1024]{1,0:T(8,128)(2,1)S(1)}, u32[]{:S(2)}, u32[]{:S(2)}) collective-permute-start(f16[64,1024]{1,0:T(8,128)(2,1)} %get-tuple-element.8), channel_id=1, source_target_pairs={{0,64},{64,128},{128,192},{192,0},{1,65},{65,129},{129,193},{193,1... | collective-permute-start | bytes 393224 | tf_op jit(solution)/shard_map/ppermute | solution.py:31
  109.3 4.8 %collective-permute-start.6 = (f16[64,1024]{1,0:T(8,128)(2,1)S(1)}, f16[64,1024]{1,0:T(8,128)(2,1)S(1)}, u32[]{:S(2)}, u32[]{:S(2)}) collective-permute-start(f16[64,1024]{1,0:T(8,128)(2,1)S(1)} %get-tuple-element.9), channel_id=1, source_target_pairs={{0,128},{64,192},{128,0},{192,64},{1,129},{65,193},{129,1},{193,65... | collective-permute-start | bytes 393224 | tf_op jit(solution)/shard_map/ppermute | solution.py:31
  114.1 4.9 %collective-permute-start.5 = (f16[64,1024]{1,0:T(8,128)(2,1)S(1)}, f16[64,1024]{1,0:T(8,128)(2,1)S(1)}, u32[]{:S(2)}, u32[]{:S(2)}) collective-permute-start(f16[64,1024]{1,0:T(8,128)(2,1)S(1)} %get-tuple-element.7), channel_id=1, source_target_pairs={{0,192},{64,0},{128,64},{192,128},{1,193},{65,1},{129,65},{193,129... | collective-permute-start | bytes 393224 | tf_op jit(solution)/shard_map/ppermute | solution.py:31
  119.0 0.1 sqrt.70
  119.1 0.1 sqrt.69
  119.2 0.6 exponential_divide_fusion
  119.7 3.7 %collective-permute-done.7 = f16[64,1024]{1,0:T(8,128)(2,1)S(1)} collective-permute-done((f16[64,1024]{1,0:T(8,128)(2,1)}, f16[64,1024]{1,0:T(8,128)(2,1)S(1)}, u32[]{:S(2)}, u32[]{:S(2)}) %collective-permute-start.7) | collective-permute-done | bytes 131104 | tf_op jit(solution)/shard_map/ppermute | solution.py:31
  123.4 4.5 %collective-permute-done.6 = f16[64,1024]{1,0:T(8,128)(2,1)S(1)} collective-permute-done((f16[64,1024]{1,0:T(8,128)(2,1)S(1)}, f16[64,1024]{1,0:T(8,128)(2,1)S(1)}, u32[]{:S(2)}, u32[]{:S(2)}) %collective-permute-start.6) | collective-permute-done | bytes 131104 | tf_op jit(solution)/shard_map/ppermute | solution.py:31
  127.9 0.8 collective-permute-done.5
  128.7 1.1 multiply_reduce_fusion
  129.9 1.0 subtract_bitcast_fusion
  131.0 0.2 convert_reduce_fusion
  131.3 0.2 fusion.29
  131.5 0.1 mul.146
  131.6 0.2 bitcast_subtract_fusion
  131.8 0.2 fusion.24
  132.0 0.1 pad_maximum_fusion.2
  132.1 0.8 copy.20
  132.9 11.7 %all-to-all-start.3 = ((f16[16,80,128]{2,1,0:T(8,128)(2,1)}), f16[16,80,128]{2,1,0:T(8,128)(2,1)S(1)}, u32[]{:S(2)}, u32[]{:S(2)}) async-start(f16[16,80,128]{2,1,0:T(8,128)(2,1)} %bitcast.16), calls=%async_computation.3 | async-start | bytes 655360 | tf_op jit(solution)/shard_map/all_to_all | solution.py:127
  144.7 20.8 %all-to-all-done.3 = f16[16,80,128]{2,1,0:T(8,128)(2,1)S(1)} async-done(((f16[16,80,128]{2,1,0:T(8,128)(2,1)}), f16[16,80,128]{2,1,0:T(8,128)(2,1)S(1)}, u32[]{:S(2)}, u32[]{:S(2)}) %all-to-all-start.3) | async-done | bytes 327712 | tf_op jit(solution)/shard_map/all_to_all | solution.py:127
  165.5 0.1 div.89
  165.8 0.8 bitcast_divide_fusion.2
  (54 shorter events, 0.5 us)
Async XLA Ops:
  0.0 1.3 copy-start
  50.4 0.8 copy-start.1
  51.6 7.1 %copy-start.12 = (f32[64]{0:T(128)}, f32[64]{0:T(128)S(1)}, u32[]{:S(2)}) copy-start(f32[64]{0:T(128)S(1)} %sqrt.66) | copy-start | bytes 772
  52.8 34.4 %all-to-all-start.1 = ((bf16[8,64,1024]{2,1,0:T(8,128)(2,1)}), bf16[8,64,1024]{2,1,0:T(8,128)(2,1)S(1)}, u32[]{:S(2)}, u32[]{:S(2)}) async-start(bf16[8,64,1024]{2,1,0:T(8,128)(2,1)} %broadcast_in_dim.22), calls=%async_computation.1 | async-start | bytes 2097152 | tf_op jit(solution)/shard_map/all_to_all | solution.py:16
  58.6 0.6 copy-start.15
  59.5 15.0 %collective-permute-start.2 = (bf16[64,1024]{1,0:T(8,128)(2,1)S(1)}, bf16[64,1024]{1,0:T(8,128)(2,1)S(1)}, u32[]{:S(2)}, u32[]{:S(2)}) collective-permute-start(bf16[64,1024]{1,0:T(8,128)(2,1)S(1)} %fusion.44), channel_id=1, source_target_pairs={{0,192},{64,0},{128,64},{192,128},{1,193},{65,1},{129,65},{193,129... | collective-permute-start | bytes 393224 | tf_op jit(solution)/shard_map/ppermute | solution.py:31
  64.7 13.5 %collective-permute-start.1 = (bf16[64,1024]{1,0:T(8,128)(2,1)S(1)}, bf16[64,1024]{1,0:T(8,128)(2,1)S(1)}, u32[]{:S(2)}, u32[]{:S(2)}) collective-permute-start(bf16[64,1024]{1,0:T(8,128)(2,1)S(1)} %fusion.44), channel_id=1, source_target_pairs={{0,128},{64,192},{128,0},{192,64},{1,129},{65,193},{129,1},{193,65... | collective-permute-start | bytes 393224 | tf_op jit(solution)/shard_map/ppermute | solution.py:31
  69.5 10.1 %collective-permute-start = (bf16[64,1024]{1,0:T(8,128)(2,1)S(1)}, bf16[64,1024]{1,0:T(8,128)(2,1)S(1)}, u32[]{:S(2)}, u32[]{:S(2)}) collective-permute-start(bf16[64,1024]{1,0:T(8,128)(2,1)S(1)} %fusion.44), channel_id=1, source_target_pairs={{0,64},{64,128},{128,192},{192,0},{1,65},{65,129},{129,193},{193,1... | collective-permute-start | bytes 393224 | tf_op jit(solution)/shard_map/ppermute | solution.py:31
  74.5 5.1 %copy-start.5 = (bf16[64,1024]{1,0:T(8,128)(2,1)}, bf16[64,1024]{1,0:T(8,128)(2,1)S(1)}, u32[]{:S(2)}) copy-start(bf16[64,1024]{1,0:T(8,128)(2,1)S(1)} %collective-permute-done.2) | copy-start | bytes 393220
  78.2 1.3 copy-start.7
  79.5 0.7 copy-start.9
  80.2 6.9 %collective-permute-start.3 = (bf16[256,1024]{1,0:T(8,128)(2,1)S(1)}, bf16[256,1024]{1,0:T(8,128)(2,1)S(1)}, u32[]{:S(2)}, u32[]{:S(2)}) collective-permute-start(bf16[256,1024]{1,0:T(8,128)(2,1)S(1)} %pad_maximum_fusion.1), channel_id=1, source_target_pairs={{0,16},{16,0},{1,17},{17,1},{2,18},{18,2},{3,19},{19,3},{4,20},{20... | collective-permute-start | bytes 1572872 | tf_op jit(solution)/shard_map/ppermute | solution.py:26
  88.4 3.9 %copy-start.6 = (bf16[64,1024]{1,0:T(8,128)(2,1)S(1)}, bf16[64,1024]{1,0:T(8,128)(2,1)}, u32[]{:S(2)}) copy-start(bf16[64,1024]{1,0:T(8,128)(2,1)} %copy-done.5) | copy-start | bytes 393220
  88.4 3.9 %copy-start.8 = (bf16[64,1024]{1,0:T(8,128)(2,1)S(1)}, bf16[64,1024]{1,0:T(8,128)(2,1)}, u32[]{:S(2)}) copy-start(bf16[64,1024]{1,0:T(8,128)(2,1)} %copy-done.7) | copy-start | bytes 393220
  88.4 3.9 %copy-start.10 = (bf16[64,1024]{1,0:T(8,128)(2,1)S(1)}, bf16[64,1024]{1,0:T(8,128)(2,1)}, u32[]{:S(2)}) copy-start(bf16[64,1024]{1,0:T(8,128)(2,1)} %copy-done.9) | copy-start | bytes 393220
  88.5 3.9 %copy-start.14 = (s32[256]{0:T(256)S(1)}, s32[256]{0:T(256)}, u32[]{:S(2)}) copy-start(s32[256]{0:T(256)} %add.266) | copy-start | bytes 3076
  89.9 13.3 %collective-permute-start.4 = (f32[256,1024]{1,0:T(8,128)}, f32[256,1024]{1,0:T(8,128)}, u32[]{:S(2)}, u32[]{:S(2)}) collective-permute-start(f32[256,1024]{1,0:T(8,128)} %fusion.47), channel_id=1, source_target_pairs={{0,16},{16,0},{1,17},{17,1},{2,18},{18,2},{3,19},{19,3},{4,20},{20... | collective-permute-start | bytes 3145736 | tf_op jit(solution)/shard_map/ppermute | solution.py:26
  92.9 0.7 copy-start.4
  94.1 8.5 %copy-start.16 = (f32[2,32]{1,0:T(2,128)S(1)}, f32[2,32]{1,0:T(2,128)}, u32[]{:S(2)}) copy-start(f32[2,32]{1,0:T(2,128)} %copy-done.15) | copy-start | bytes 772
  95.5 35.5 %all-to-all-start.2 = ((f16[8,64,1024]{2,1,0:T(8,128)(2,1)}), f16[8,64,1024]{2,1,0:T(8,128)(2,1)S(1)}, u32[]{:S(2)}, u32[]{:S(2)}) async-start(f16[8,64,1024]{2,1,0:T(8,128)(2,1)} %bitcast.85), calls=%async_computation.2 | async-start | bytes 2097152 | tf_op jit(solution)/shard_map/all_to_all | solution.py:22
  103.2 15.7 %copy-start.17 = (f32[1,1,64]{2,1,0:T(1,128)S(1)}, f32[1,1,64]{2,1,0:T(1,128)}, u32[]{:S(2)}) copy-start(f32[1,1,64]{2,1,0:T(1,128)} %stack.21) | copy-start | bytes 772
  105.0 0.8 copy-start.3
  106.5 16.9 %collective-permute-start.7 = (f16[64,1024]{1,0:T(8,128)(2,1)}, f16[64,1024]{1,0:T(8,128)(2,1)S(1)}, u32[]{:S(2)}, u32[]{:S(2)}) collective-permute-start(f16[64,1024]{1,0:T(8,128)(2,1)} %get-tuple-element.8), channel_id=1, source_target_pairs={{0,64},{64,128},{128,192},{192,0},{1,65},{65,129},{129,193},{193,1... | collective-permute-start | bytes 393224 | tf_op jit(solution)/shard_map/ppermute | solution.py:31
  109.3 18.6 %collective-permute-start.6 = (f16[64,1024]{1,0:T(8,128)(2,1)S(1)}, f16[64,1024]{1,0:T(8,128)(2,1)S(1)}, u32[]{:S(2)}, u32[]{:S(2)}) collective-permute-start(f16[64,1024]{1,0:T(8,128)(2,1)S(1)} %get-tuple-element.9), channel_id=1, source_target_pairs={{0,128},{64,192},{128,0},{192,64},{1,129},{65,193},{129,1},{193,65... | collective-permute-start | bytes 393224 | tf_op jit(solution)/shard_map/ppermute | solution.py:31
  114.1 14.6 %collective-permute-start.5 = (f16[64,1024]{1,0:T(8,128)(2,1)S(1)}, f16[64,1024]{1,0:T(8,128)(2,1)S(1)}, u32[]{:S(2)}, u32[]{:S(2)}) collective-permute-start(f16[64,1024]{1,0:T(8,128)(2,1)S(1)} %get-tuple-element.7), channel_id=1, source_target_pairs={{0,192},{64,0},{128,64},{192,128},{1,193},{65,1},{129,65},{193,129... | collective-permute-start | bytes 393224 | tf_op jit(solution)/shard_map/ppermute | solution.py:31
  119.7 11.5 %copy-start.2 = (f32[16,64,128]{2,1,0:T(8,128)S(1)}, f32[16,64,128]{2,1,0:T(8,128)}, u32[]{:S(2)}) copy-start(f32[16,64,128]{2,1,0:T(8,128)} %copy-done.1) | copy-start | bytes 1572868
  129.9 1.7 %copy-start.13 = (f32[64]{0:T(128)S(1)}, f32[64]{0:T(128)}, u32[]{:S(2)}) copy-start(f32[64]{0:T(128)} %copy-done.12) | copy-start | bytes 772
  130.9 0.9 copy-start.11
  132.9 32.5 %all-to-all-start.3 = ((f16[16,80,128]{2,1,0:T(8,128)(2,1)}), f16[16,80,128]{2,1,0:T(8,128)(2,1)S(1)}, u32[]{:S(2)}, u32[]{:S(2)}) async-start(f16[16,80,128]{2,1,0:T(8,128)(2,1)} %bitcast.16), calls=%async_computation.3 | async-start | bytes 655360 | tf_op jit(solution)/shard_map/all_to_all | solution.py:127

commit v3 on v2

v3 whole, which is shorter than its diff:
```python
import jax
import jax.numpy as jnp
from jax import lax
from jax.sharding import Mesh, PartitionSpec as P

BLK = ("x", "y", "c")
AXES = BLK + ("zl", "zh")
COLUMN = ("zh", "zl")
F32 = jnp.float32
HALF = jnp.float16


def spread(value, axis):
    count = lax.axis_size(axis)
    copies = jnp.broadcast_to(value[None], (count,) + value.shape)
    return lax.all_to_all(copies, axis, 0, 0, tiled=True)


def summed(parts, axis):
    count = lax.axis_size(axis)
    parts = parts.reshape((count, -1) + parts.shape[1:])
    return jnp.sum(lax.all_to_all(parts, axis, 0, 0, tiled=True).astype(F32), axis=0)


def swapped(value):
    return lax.ppermute(value, "c", [(0, 1), (1, 0)])


def shifted(value, axis, steps):
    count = lax.axis_size(axis)
    return lax.ppermute(value, axis, [(k, (k + steps) % count) for k in range(count)])


def exponent(value):
    return jnp.clip(jnp.floor(jnp.log2(jnp.maximum(value, 1e-30))), -100.0, 126.0)


def with_exponents(rows, powers):
    count, width = rows.shape[-2:]
    lead = [(0, 0)] * (powers.ndim - 1)
    powers = jnp.pad(powers[..., None, :], lead + [(0, 7), (0, width - count)])
    powers = jnp.broadcast_to(powers, rows.shape[:-2] + (8, width))
    return jnp.concatenate([rows.astype(HALF), powers.astype(HALF)], axis=-2)


def without_exponents(pieces, count):
    return pieces[..., :count, :].astype(F32), pieces[..., count, :count].astype(F32)


def normalize(embed):
    norm = jnp.sqrt(jnp.sum(embed * embed, axis=1, keepdims=True) + 1e-06)
    return embed / norm, norm


def projected(grad, unit):
    return grad - unit * jnp.sum(unit * grad, axis=1, keepdims=True)


def shards(image_features, text_features, image_head, text_head, positive, log_scale, bias):
    rows = image_features.shape[0]
    planes = lax.axis_size(COLUMN)
    lanes = lax.axis_size("zl")
    quarter = rows // 4
    half = quarter // 2
    x, y, c = (lax.axis_index(name) for name in BLK)
    zh = lax.axis_index("zh")
    plane = zh * lanes + lax.axis_index("zl")
    image_part, text_part = plane // 4, plane % 4
    scale = jnp.exp(log_scale[0])
    offset = bias[0]

    def head_part(features, head):
        own = features.reshape(4, 2, half, -1)
        own = lax.dynamic_index_in_dim(own, zh, 1, keepdims=False).reshape(4 * half, -1)
        return jnp.dot(own, head, preferred_element_type=F32).reshape(4, half, -1)

    image_cols = head_part(image_features, image_head)
    text_cols = head_part(text_features, text_head)
    width = image_cols.shape[-1]
    image_powers = exponent(jnp.max(jnp.abs(image_cols), axis=-1))
    text_powers = exponent(jnp.max(jnp.abs(text_cols), axis=-1))
    image_cols = (image_cols * jnp.exp2(-image_powers)[..., None]).astype(HALF)
    text_cols = (text_cols * jnp.exp2(-text_powers)[..., None]).astype(HALF)

    def for_planes(image, text):
        image = jnp.broadcast_to(image[:, None], (4,) + image.shape)
        text = jnp.broadcast_to(text[None], (4,) + text.shape)
        return jnp.concatenate([image, text], axis=2).reshape((planes, quarter) + image.shape[3:])

    pieces = with_exponents(
        for_planes(image_cols, text_cols), for_planes(image_powers, text_powers)
    )
    pieces = lax.all_to_all(pieces, COLUMN, 0, 0, tiled=True)
    pieces, powers = without_exponents(pieces, quarter)
    pieces = pieces * jnp.exp2(powers)[..., None]
    pieces = pieces.reshape(2, lanes, 2, half, width)
    whole = pieces.transpose(2, 0, 3, 1, 4).reshape(2, quarter, lanes * width)
    image_unit, image_norm = normalize(whole[0])
    text_unit, text_norm = normalize(whole[1])

    text_b = text_unit.astype(jnp.bfloat16)
    image_b = spread(image_unit.astype(jnp.bfloat16), "y").reshape(8 * quarter, -1)
    text_own = jnp.concatenate([text_b] + [shifted(text_b, "x", k) for k in range(1, 4)])
    text_far = swapped(text_own)

    keys = positive.reshape(4, 8, 2, 4, quarter)
    keys = lax.dynamic_slice(keys, (x, 0, c, image_part, 0), (1, 8, 1, 1, quarter))
    keys = keys.reshape(1, 8 * quarter)

    def weights(text_b, core):
        logits = scale * jnp.einsum("ce,re->cr", text_b, image_b, preferred_element_type=F32)
        logits = logits + offset
        row = lax.broadcasted_iota(jnp.int32, (4 * quarter, 1), 0)
        block = (((x - row // quarter) & 3) * 8 + y) * 2 + core
        index = block * rows + text_part * quarter + row % quarter
        sign = jnp.where(keys == index, 1.0, -1.0)
        return (-sign * jax.nn.sigmoid(-sign * logits) * scale).astype(jnp.bfloat16)

    def to_texts(weight):
        return jnp.dot(weight, image_b, preferred_element_type=F32)

    def to_images(weight, text_b):
        return jnp.einsum("cr,ce->re", weight, text_b, preferred_element_type=F32)

    weight_far = weights(text_far, 1 - c)
    far_grad = swapped(to_texts(weight_far))
    weight_own = weights(text_own, c)
    image_grad = to_images(weight_far, text_far) + to_images(weight_own, text_own)
    text_grad = to_texts(weight_own) + far_grad

    text_parts = text_grad.astype(HALF).reshape(4, quarter, -1)
    text_grad = text_parts[0].astype(F32)
    for k in range(1, 4):
        text_grad = text_grad + shifted(text_parts[k], "x", -k).astype(F32)
    image_grad = summed(image_grad.astype(HALF), "y")

    both = jnp.stack([projected(image_grad, image_unit), projected(text_grad, text_unit)])
    norms = jnp.stack([image_norm, text_norm])
    powers = exponent(norms)
    both = both * (jnp.exp2(powers) / norms)
    both = both.reshape(2, quarter, lanes, width).transpose(0, 2, 1, 3)
    both = with_exponents(both, powers.reshape(2, 1, quarter)).reshape(planes, quarter + 8, width)
    both = lax.all_to_all(both, COLUMN, 0, 0, tiled=True)
    both, powers = without_exponents(both.reshape(4, 4, quarter + 8, width), quarter)
    powers = jnp.where(zh == 0, powers[:, 0], powers[0])
    result = jnp.where(zh == 0, jnp.sum(both, axis=1), jnp.sum(both, axis=0))
    result = result / jnp.exp2(powers)[:, :, None]
    return result.reshape(1, rows, width)


def solution(mesh):
    fine = Mesh(mesh.devices.reshape(4, 8, 2, 8, 2), AXES)
    placed = (P(BLK, None), P(BLK, None), P(None, "zl"), P(None, "zl"), P(), P(), P())
    return jax.shard_map(
        shards, mesh=fine, in_specs=placed, out_specs=P("zh", BLK, "zl"), check_vma=False
    )
```

time: 167 us -> 150 us (0.90)
  blocking collectives: 47.8 us -> 37.9 us
  starting transfers between devices: 54.8 us -> 46.7 us
  waiting for transfers between devices: 34.8 us -> 41 us
  local copies, waits for them, and re-layouts: 11.6 us -> 8.21 us
  other arithmetic: 6.3 us -> 3.79 us
    all_to_all x1, waiting for transfers between devices: 0.01 us -> 9.87 us  [summed(): lax.all_to_all(parts, axis, 0, 0, tiled=True).astype(F32)]
    all_to_all x1, blocking collectives: 47.8 us -> 37.9 us  [shards(): pieces = lax.all_to_all(pieces, COLUMN, 0, 0, tiled=True)]
    ppermute x6, starting transfers between devices: 26 us -> 19.6 us  [shifted(): lax.ppermute(value, axis, [(k, (k + steps) % count) for k in range(count)])]
    ppermute x6, waiting for transfers between devices: 14 us -> 9.54 us  [shifted(): lax.ppermute(value, axis, [(k, (k + steps) % count) for k in range(count)])]
    all_to_all x1, waiting for transfers between devices: 0.01 us -> 1.76 us  [spread(): return lax.all_to_all(copies, axis, 0, 0, tiled=True)]
    unnamed x39 -> x29, local copies, waits for them, and re-layouts: 3.59 us -> 2.06 us
  transfers between devices with their start and end apart: 11 -> 11, of which waited for: 6 -> 8; matrix products, arithmetic and copies ran while one was open for 8% -> 6% of each run, Pallas kernels for 0% -> 0%
where the time goes in v3:
time: 150 us; the launch traced here: 149 us
  starting transfers between devices  46.7 us (31%)
  waiting for transfers between devices  41 us (27%)
  blocking collectives  37.9 us (25%)
  matrix products  9.77 us (7%)
  local copies, waits for them, and re-layouts  8.21 us (5%)
  other arithmetic  3.79 us (3%)
  between operations  1.84 us (1%)
    all_to_all x1, blocking collectives, shards(): pieces = lax.all_to_all(pieces, COLUMN, 0, 0, tiled=True)  37.9 us
    all_to_all x1, waiting for transfers between devices, shards(): both = lax.all_to_all(both, COLUMN, 0, 0, tiled=True)  19.8 us
    ppermute x6, starting transfers between devices, shifted(): lax.ppermute(value, axis, [(k, (k + steps) % count) for k in range(count)])  19.6 us
    all_to_all x1, starting transfers between devices, shards(): both = lax.all_to_all(both, COLUMN, 0, 0, tiled=True)  10.2 us
    all_to_all x1, waiting for transfers between devices, summed(): lax.all_to_all(parts, axis, 0, 0, tiled=True).astype(F32)  9.87 us
    ppermute x6, waiting for transfers between devices, shifted(): lax.ppermute(value, axis, [(k, (k + steps) % count) for k in range(count)])  9.54 us
    all_to_all x1, starting transfers between devices, spread(): return lax.all_to_all(copies, axis, 0, 0, tiled=True)  7.11 us
    all_to_all x1, starting transfers between devices, summed(): lax.all_to_all(parts, axis, 0, 0, tiled=True).astype(F32)  5.93 us
  transfers between devices with their start and end apart: 11, of which 8 were waited for; matrix products, arithmetic and copies ran while one was open for 6% of the time, Pallas kernels for 0%

profile of v3, /device:TPU:6, one launch (start us, length us, event | category | flops | bytes accessed | tf_op | source)
XLA Modules:
  0.0 149.2 jit_solution(2027287534364233630)
XLA Ops:
  0.0 1.4 abs_reduce_fusion
  1.4 1.3 abs_reduce_fusion.1
  2.8 0.1 pad_maximum_fusion.3
  2.9 0.1 multiply_convert_fusion
  3.0 0.1 multiply_convert_fusion.1
  3.1 0.1 pad_maximum_fusion.2
  3.3 37.9 %all_to_all.20 = f16[16,72,128]{2,1,0:T(8,128)(2,1)S(1)} all-to-all(f16[16,72,128]{2,1,0:T(8,128)(2,1)S(1)} %fusion.25), channel_id=1, replica_groups=mesh['x'=4,'y'=8,'c'=2,'zl'=8,'zh'=2] {'zh','zl'}, dimensions={0} | all-to-all | bytes 589824 | tf_op jit(solution)/shard_map/all_to_all | solution.py:93
  41.3 0.2 convert_multiply_fusion
  41.5 0.8 copy-done.1
  42.3 0.1 multiply_reduce_fusion.1
  42.4 0.2 copy.19
  42.6 0.1 sqrt.68
  42.7 0.1 fusion.27
  42.8 1.1 broadcast_in_dim.26
  43.9 7.1 %all-to-all-start.1 = ((bf16[8,64,1024]{2,1,0:T(8,128)(2,1)}), bf16[8,64,1024]{2,1,0:T(8,128)(2,1)S(1)}, u32[]{:S(2)}, u32[]{:S(2)}) async-start(bf16[8,64,1024]{2,1,0:T(8,128)(2,1)} %broadcast_in_dim.26), calls=%async_computation.1 | async-start | bytes 2097152 | tf_op jit(solution)/shard_map/all_to_all | solution.py:16
  51.0 0.1 sqrt.66
  51.1 0.5 copy-done.11
  51.6 0.2 copy.18
  51.7 0.1 fusion.51
  51.8 2.7 %collective-permute-start.2 = (bf16[64,1024]{1,0:T(8,128)(2,1)S(1)}, bf16[64,1024]{1,0:T(8,128)(2,1)S(1)}, u32[]{:S(2)}, u32[]{:S(2)}) collective-permute-start(bf16[64,1024]{1,0:T(8,128)(2,1)S(1)} %fusion.51), channel_id=1, source_target_pairs={{0,768},{256,0},{512,256},{768,512},{1,769},{257,1},{513,257},{769... | collective-permute-start | bytes 393224 | tf_op jit(solution)/shard_map/ppermute | solution.py:31
  54.6 3.0 %collective-permute-start.1 = (bf16[64,1024]{1,0:T(8,128)(2,1)S(1)}, bf16[64,1024]{1,0:T(8,128)(2,1)S(1)}, u32[]{:S(2)}, u32[]{:S(2)}) collective-permute-start(bf16[64,1024]{1,0:T(8,128)(2,1)S(1)} %fusion.51), channel_id=1, source_target_pairs={{0,512},{256,768},{512,0},{768,256},{1,513},{257,769},{513,1},{769... | collective-permute-start | bytes 393224 | tf_op jit(solution)/shard_map/ppermute | solution.py:31
  57.6 4.0 %collective-permute-start = (bf16[64,1024]{1,0:T(8,128)(2,1)S(1)}, bf16[64,1024]{1,0:T(8,128)(2,1)S(1)}, u32[]{:S(2)}, u32[]{:S(2)}) collective-permute-start(bf16[64,1024]{1,0:T(8,128)(2,1)S(1)} %fusion.51), channel_id=1, source_target_pairs={{0,256},{256,512},{512,768},{768,0},{1,257},{257,513},{513,769},{7... | collective-permute-start | bytes 393224 | tf_op jit(solution)/shard_map/ppermute | solution.py:31
  61.6 1.3 collective-permute-done.1
  62.9 1.7 %collective-permute-done = bf16[64,1024]{1,0:T(8,128)(2,1)S(1)} collective-permute-done((bf16[64,1024]{1,0:T(8,128)(2,1)S(1)}, bf16[64,1024]{1,0:T(8,128)(2,1)S(1)}, u32[]{:S(2)}, u32[]{:S(2)}) %collective-permute-start) | collective-permute-done | bytes 131104 | tf_op jit(solution)/shard_map/ppermute | solution.py:31
  64.6 0.6 copy-done.8
  65.3 1.9 %collective-permute-start.3 = (bf16[256,1024]{1,0:T(8,128)(2,1)S(1)}, bf16[256,1024]{1,0:T(8,128)(2,1)S(1)}, u32[]{:S(2)}, u32[]{:S(2)}) collective-permute-start(bf16[256,1024]{1,0:T(8,128)(2,1)S(1)} %pad_maximum_fusion), channel_id=1, source_target_pairs={{0,16},{16,0},{1,17},{17,1},{2,18},{18,2},{3,19},{19,3},{4,20},{20... | collective-permute-start | bytes 1572872 | tf_op jit(solution)/shard_map/ppermute | solution.py:26
  68.6 1.6 %reshape.473 = s32[4,8,2,4,64]{4,3,2,1,0:T(4,128)} reshape(s32[16384]{0:T(1024)} %param.11) | data formatting | bytes 131072 | tf_op jit(solution)/shard_map/reshape | solution.py:106
  70.2 0.7 dynamic-slice_reduce_fusion
  70.9 0.7 eq.36
  71.6 0.6 add_add_fusion.1
  72.2 1.8 %all-to-all-done.1 = bf16[8,64,1024]{2,1,0:T(8,128)(2,1)S(1)} async-done(((bf16[8,64,1024]{2,1,0:T(8,128)(2,1)}), bf16[8,64,1024]{2,1,0:T(8,128)(2,1)S(1)}, u32[]{:S(2)}, u32[]{:S(2)}) %all-to-all-start.1) | async-done | bytes 1048608 | tf_op jit(solution)/shard_map/all_to_all | solution.py:16
  74.0 1.3 fusion.17
  75.3 1.4 fusion.54
  76.8 1.9 %collective-permute-start.4 = (f32[256,1024]{1,0:T(8,128)}, f32[256,1024]{1,0:T(8,128)}, u32[]{:S(2)}, u32[]{:S(2)}) collective-permute-start(f32[256,1024]{1,0:T(8,128)} %fusion.54), channel_id=1, source_target_pairs={{0,16},{16,0},{1,17},{17,1},{2,18},{18,2},{3,19},{19,3},{4,20},{20... | collective-permute-start | bytes 3145736 | tf_op jit(solution)/shard_map/ppermute | solution.py:26
  78.7 0.6 fusion.18
  79.4 0.5 fusion.52
  79.8 1.4 add_convert_fusion
  81.3 5.9 %all-to-all-start.2 = ((f16[8,64,1024]{2,1,0:T(8,128)(2,1)}), f16[8,64,1024]{2,1,0:T(8,128)(2,1)S(1)}, u32[]{:S(2)}, u32[]{:S(2)}) async-start(f16[8,64,1024]{2,1,0:T(8,128)(2,1)} %bitcast.95), calls=%async_computation.2 | async-start | bytes 2097152 | tf_op jit(solution)/shard_map/all_to_all | solution.py:22
  87.2 0.1 stack.22
  87.3 0.1 stack.21
  87.4 0.1 sqrt.70
  87.5 0.1 sqrt.69
  87.6 1.8 %fusion = f16[256,1024]{1,0:T(8,128)(2,1)S(1)} fusion(f32[256,1024]{1,0:T(8,128)} %collective-permute-done.4, bf16[256,512]{1,0:T(8,128)(2,1)} %copy-done.3, bf16[512,1024]{1,0:T(8,128)(2,1)S(1)} %bitcast.91), kind=kOutput, calls=%fused_computation.3 | convolution fusion | flops 268959744 | bytes 2883584 | tf_op jit(solution)/shard_map/dot_general | solution.py:120
  89.4 5.1 %collective-permute-start.7 = (f16[64,1024]{1,0:T(8,128)(2,1)S(1)}, f16[64,1024]{1,0:T(8,128)(2,1)S(1)}, u32[]{:S(2)}, u32[]{:S(2)}) collective-permute-start(f16[64,1024]{1,0:T(8,128)(2,1)S(1)} %get-tuple-element.10), channel_id=1, source_target_pairs={{0,256},{256,512},{512,768},{768,0},{1,257},{257,513},{513,769},{7... | collective-permute-start | bytes 393224 | tf_op jit(solution)/shard_map/ppermute | solution.py:31
  94.5 2.8 %collective-permute-start.6 = (f16[64,1024]{1,0:T(8,128)(2,1)S(1)}, f16[64,1024]{1,0:T(8,128)(2,1)S(1)}, u32[]{:S(2)}, u32[]{:S(2)}) collective-permute-start(f16[64,1024]{1,0:T(8,128)(2,1)S(1)} %get-tuple-element.11), channel_id=1, source_target_pairs={{0,512},{256,768},{512,0},{768,256},{1,513},{257,769},{513,1},{769... | collective-permute-start | bytes 393224 | tf_op jit(solution)/shard_map/ppermute | solution.py:31
  97.3 1.9 %collective-permute-start.5 = (f16[64,1024]{1,0:T(8,128)(2,1)S(1)}, f16[64,1024]{1,0:T(8,128)(2,1)S(1)}, u32[]{:S(2)}, u32[]{:S(2)}) collective-permute-start(f16[64,1024]{1,0:T(8,128)(2,1)S(1)} %get-tuple-element.9), channel_id=1, source_target_pairs={{0,768},{256,0},{512,256},{768,512},{1,769},{257,1},{513,257},{769... | collective-permute-start | bytes 393224 | tf_op jit(solution)/shard_map/ppermute | solution.py:31
  99.3 0.7 collective-permute-done.7
  100.0 3.9 %collective-permute-done.6 = f16[64,1024]{1,0:T(8,128)(2,1)S(1)} collective-permute-done((f16[64,1024]{1,0:T(8,128)(2,1)S(1)}, f16[64,1024]{1,0:T(8,128)(2,1)S(1)}, u32[]{:S(2)}, u32[]{:S(2)}) %collective-permute-start.6) | collective-permute-done | bytes 131104 | tf_op jit(solution)/shard_map/ppermute | solution.py:31
  103.9 1.9 %collective-permute-done.5 = f16[64,1024]{1,0:T(8,128)(2,1)S(1)} collective-permute-done((f16[64,1024]{1,0:T(8,128)(2,1)S(1)}, f16[64,1024]{1,0:T(8,128)(2,1)S(1)}, u32[]{:S(2)}, u32[]{:S(2)}) %collective-permute-start.5) | collective-permute-done | bytes 131104 | tf_op jit(solution)/shard_map/ppermute | solution.py:31
  105.9 0.2 multiply_reduce_fusion
  106.1 0.1 subtract_bitcast_fusion
  106.3 9.9 %all-to-all-done.2 = f16[8,64,1024]{2,1,0:T(8,128)(2,1)S(1)} async-done(((f16[8,64,1024]{2,1,0:T(8,128)(2,1)}), f16[8,64,1024]{2,1,0:T(8,128)(2,1)S(1)}, u32[]{:S(2)}, u32[]{:S(2)}) %all-to-all-start.2) | async-done | bytes 1048608 | tf_op jit(solution)/shard_map/all_to_all | solution.py:22
  116.2 0.2 convert_reduce_fusion
  116.5 0.2 fusion.31
  116.7 0.1 mul.175
  116.8 0.2 bitcast_subtract_fusion
  117.0 0.2 fusion.26
  117.2 0.1 pad_maximum_fusion.1
  117.3 0.8 copy.22
  118.1 10.2 %all-to-all-start.3 = ((f16[16,72,128]{2,1,0:T(8,128)(2,1)}), f16[16,72,128]{2,1,0:T(8,128)(2,1)S(1)}, u32[]{:S(2)}, u32[]{:S(2)}) async-start(f16[16,72,128]{2,1,0:T(8,128)(2,1)} %bitcast.19), calls=%async_computation.3 | async-start | bytes 589824 | tf_op jit(solution)/shard_map/all_to_all | solution.py:143
  128.3 19.8 %all-to-all-done.3 = f16[16,72,128]{2,1,0:T(8,128)(2,1)S(1)} async-done(((f16[16,72,128]{2,1,0:T(8,128)(2,1)}), f16[16,72,128]{2,1,0:T(8,128)(2,1)S(1)}, u32[]{:S(2)}, u32[]{:S(2)}) %all-to-all-start.3) | async-done | bytes 294944 | tf_op jit(solution)/shard_map/all_to_all | solution.py:143
  148.2 0.1 squeeze.32
  148.3 0.1 squeeze.33
  148.5 0.8 bitcast_divide_fusion.2
  (52 shorter events, 0.7 us)
Async XLA Ops:
  0.0 1.4 copy-start
  41.5 0.8 copy-start.1
  43.9 30.1 %all-to-all-start.1 = ((bf16[8,64,1024]{2,1,0:T(8,128)(2,1)}), bf16[8,64,1024]{2,1,0:T(8,128)(2,1)S(1)}, u32[]{:S(2)}, u32[]{:S(2)}) async-start(bf16[8,64,1024]{2,1,0:T(8,128)(2,1)} %broadcast_in_dim.26), calls=%async_computation.1 | async-start | bytes 2097152 | tf_op jit(solution)/shard_map/all_to_all | solution.py:16
  51.0 0.6 copy-start.11
  51.8 9.8 %collective-permute-start.2 = (bf16[64,1024]{1,0:T(8,128)(2,1)S(1)}, bf16[64,1024]{1,0:T(8,128)(2,1)S(1)}, u32[]{:S(2)}, u32[]{:S(2)}) collective-permute-start(bf16[64,1024]{1,0:T(8,128)(2,1)S(1)} %fusion.51), channel_id=1, source_target_pairs={{0,768},{256,0},{512,256},{768,512},{1,769},{257,1},{513,257},{769... | collective-permute-start | bytes 393224 | tf_op jit(solution)/shard_map/ppermute | solution.py:31
  54.6 8.4 %collective-permute-start.1 = (bf16[64,1024]{1,0:T(8,128)(2,1)S(1)}, bf16[64,1024]{1,0:T(8,128)(2,1)S(1)}, u32[]{:S(2)}, u32[]{:S(2)}) collective-permute-start(bf16[64,1024]{1,0:T(8,128)(2,1)S(1)} %fusion.51), channel_id=1, source_target_pairs={{0,512},{256,768},{512,0},{768,256},{1,513},{257,769},{513,1},{769... | collective-permute-start | bytes 393224 | tf_op jit(solution)/shard_map/ppermute | solution.py:31
  57.6 7.0 %collective-permute-start = (bf16[64,1024]{1,0:T(8,128)(2,1)S(1)}, bf16[64,1024]{1,0:T(8,128)(2,1)S(1)}, u32[]{:S(2)}, u32[]{:S(2)}) collective-permute-start(bf16[64,1024]{1,0:T(8,128)(2,1)S(1)} %fusion.51), channel_id=1, source_target_pairs={{0,256},{256,512},{512,768},{768,0},{1,257},{257,513},{513,769},{7... | collective-permute-start | bytes 393224 | tf_op jit(solution)/shard_map/ppermute | solution.py:31
  61.6 3.0 %copy-start.4 = (bf16[64,1024]{1,0:T(8,128)(2,1)}, bf16[64,1024]{1,0:T(8,128)(2,1)S(1)}, u32[]{:S(2)}) copy-start(bf16[64,1024]{1,0:T(8,128)(2,1)S(1)} %collective-permute-done.2) | copy-start | bytes 393220
  62.9 1.7 %copy-start.6 = (bf16[64,1024]{1,0:T(8,128)(2,1)}, bf16[64,1024]{1,0:T(8,128)(2,1)S(1)}, u32[]{:S(2)}) copy-start(bf16[64,1024]{1,0:T(8,128)(2,1)S(1)} %collective-permute-done.1) | copy-start | bytes 393220
  64.6 0.6 copy-start.8
  65.3 6.9 %collective-permute-start.3 = (bf16[256,1024]{1,0:T(8,128)(2,1)S(1)}, bf16[256,1024]{1,0:T(8,128)(2,1)S(1)}, u32[]{:S(2)}, u32[]{:S(2)}) collective-permute-start(bf16[256,1024]{1,0:T(8,128)(2,1)S(1)} %pad_maximum_fusion), channel_id=1, source_target_pairs={{0,16},{16,0},{1,17},{17,1},{2,18},{18,2},{3,19},{19,3},{4,20},{20... | collective-permute-start | bytes 1572872 | tf_op jit(solution)/shard_map/ppermute | solution.py:26
  75.3 3.4 %copy-start.5 = (bf16[64,1024]{1,0:T(8,128)(2,1)S(1)}, bf16[64,1024]{1,0:T(8,128)(2,1)}, u32[]{:S(2)}) copy-start(bf16[64,1024]{1,0:T(8,128)(2,1)} %copy-done.4) | copy-start | bytes 393220
  75.3 3.4 %copy-start.7 = (bf16[64,1024]{1,0:T(8,128)(2,1)S(1)}, bf16[64,1024]{1,0:T(8,128)(2,1)}, u32[]{:S(2)}) copy-start(bf16[64,1024]{1,0:T(8,128)(2,1)} %copy-done.6) | copy-start | bytes 393220
  75.3 3.4 %copy-start.9 = (bf16[64,1024]{1,0:T(8,128)(2,1)S(1)}, bf16[64,1024]{1,0:T(8,128)(2,1)}, u32[]{:S(2)}) copy-start(bf16[64,1024]{1,0:T(8,128)(2,1)} %copy-done.8) | copy-start | bytes 393220
  75.3 3.4 %copy-start.10 = (s32[512]{0:T(512)S(1)}, s32[512]{0:T(512)}, u32[]{:S(2)}) copy-start(s32[512]{0:T(512)} %eq.36) | copy-start | bytes 6148
  76.8 10.8 %collective-permute-start.4 = (f32[256,1024]{1,0:T(8,128)}, f32[256,1024]{1,0:T(8,128)}, u32[]{:S(2)}, u32[]{:S(2)}) collective-permute-start(f32[256,1024]{1,0:T(8,128)} %fusion.54), channel_id=1, source_target_pairs={{0,16},{16,0},{1,17},{17,1},{2,18},{18,2},{3,19},{19,3},{4,20},{20... | collective-permute-start | bytes 3145736 | tf_op jit(solution)/shard_map/ppermute | solution.py:26
  79.4 1.9 %copy-start.3 = (bf16[256,512]{1,0:T(8,128)(2,1)}, bf16[256,512]{1,0:T(8,128)(2,1)S(1)}, u32[]{:S(2)}) copy-start(bf16[256,512]{1,0:T(8,128)(2,1)S(1)} %fusion.18) | copy-start | bytes 786436
  79.8 7.4 %copy-start.12 = (f32[2,32]{1,0:T(2,128)S(1)}, f32[2,32]{1,0:T(2,128)}, u32[]{:S(2)}) copy-start(f32[2,32]{1,0:T(2,128)} %copy-done.11) | copy-start | bytes 772
  81.3 34.9 %all-to-all-start.2 = ((f16[8,64,1024]{2,1,0:T(8,128)(2,1)}), f16[8,64,1024]{2,1,0:T(8,128)(2,1)S(1)}, u32[]{:S(2)}, u32[]{:S(2)}) async-start(f16[8,64,1024]{2,1,0:T(8,128)(2,1)} %bitcast.95), calls=%async_computation.2 | async-start | bytes 2097152 | tf_op jit(solution)/shard_map/all_to_all | solution.py:22
  89.4 10.6 %collective-permute-start.7 = (f16[64,1024]{1,0:T(8,128)(2,1)S(1)}, f16[64,1024]{1,0:T(8,128)(2,1)S(1)}, u32[]{:S(2)}, u32[]{:S(2)}) collective-permute-start(f16[64,1024]{1,0:T(8,128)(2,1)S(1)} %get-tuple-element.10), channel_id=1, source_target_pairs={{0,256},{256,512},{512,768},{768,0},{1,257},{257,513},{513,769},{7... | collective-permute-start | bytes 393224 | tf_op jit(solution)/shard_map/ppermute | solution.py:31
  94.5 9.4 %collective-permute-start.6 = (f16[64,1024]{1,0:T(8,128)(2,1)S(1)}, f16[64,1024]{1,0:T(8,128)(2,1)S(1)}, u32[]{:S(2)}, u32[]{:S(2)}) collective-permute-start(f16[64,1024]{1,0:T(8,128)(2,1)S(1)} %get-tuple-element.11), channel_id=1, source_target_pairs={{0,512},{256,768},{512,0},{768,256},{1,513},{257,769},{513,1},{769... | collective-permute-start | bytes 393224 | tf_op jit(solution)/shard_map/ppermute | solution.py:31
  97.3 8.5 %collective-permute-start.5 = (f16[64,1024]{1,0:T(8,128)(2,1)S(1)}, f16[64,1024]{1,0:T(8,128)(2,1)S(1)}, u32[]{:S(2)}, u32[]{:S(2)}) collective-permute-start(f16[64,1024]{1,0:T(8,128)(2,1)S(1)} %get-tuple-element.9), channel_id=1, source_target_pairs={{0,768},{256,0},{512,256},{768,512},{1,769},{257,1},{513,257},{769... | collective-permute-start | bytes 393224 | tf_op jit(solution)/shard_map/ppermute | solution.py:31
  99.3 17.2 %copy-start.2 = (f32[16,64,128]{2,1,0:T(8,128)S(1)}, f32[16,64,128]{2,1,0:T(8,128)}, u32[]{:S(2)}) copy-start(f32[16,64,128]{2,1,0:T(8,128)} %copy-done.1) | copy-start | bytes 1572868
  118.1 30.0 %all-to-all-start.3 = ((f16[16,72,128]{2,1,0:T(8,128)(2,1)}), f16[16,72,128]{2,1,0:T(8,128)(2,1)S(1)}, u32[]{:S(2)}, u32[]{:S(2)}) async-start(f16[16,72,128]{2,1,0:T(8,128)(2,1)} %bitcast.19), calls=%async_computation.3 | async-start | bytes 589824 | tf_op jit(solution)/shard_map/all_to_all | solution.py:143

commit v4 on v3

--- a/solution.py
+++ b/solution.py
@@ -103,17 +103,20 @@
     text_own = jnp.concatenate([text_b] + [shifted(text_b, "x", k) for k in range(1, 4)])
     text_far = swapped(text_own)
 
-    keys = positive.reshape(4, 8, 2, 4, quarter)
-    keys = lax.dynamic_slice(keys, (x, 0, c, image_part, 0), (1, 8, 1, 1, quarter))
+    keys = positive.reshape(-1, 2 * rows)
+    keys = lax.dynamic_slice(keys, (x * 8, c * rows + image_part * quarter), (8, quarter))
     keys = keys.reshape(1, 8 * quarter)
+    key_block, key_row = keys // rows, keys % rows
+    place = ((x - key_block // 16) & 3) * quarter + key_row % quarter
+    place = place + jnp.where(key_block % 2 == c, 0, 4 * quarter)
+    inside = (key_block // 2 % 8 == y) & (key_row // quarter == text_part)
+    place = jnp.where(inside, place, -1)
 
-    def weights(text_b, core):
+    def weights(text_b, first):
         logits = scale * jnp.einsum("ce,re->cr", text_b, image_b, preferred_element_type=F32)
         logits = logits + offset
-        row = lax.broadcasted_iota(jnp.int32, (4 * quarter, 1), 0)
-        block = (((x - row // quarter) & 3) * 8 + y) * 2 + core
-        index = block * rows + text_part * quarter + row % quarter
-        sign = jnp.where(keys == index, 1.0, -1.0)
+        index = lax.broadcasted_iota(jnp.int32, logits.shape, 0) + first
+        sign = jnp.where(place == index, 1.0, -1.0)
         return (-sign * jax.nn.sigmoid(-sign * logits) * scale).astype(jnp.bfloat16)
 
     def to_texts(weight):
@@ -122,17 +125,22 @@
     def to_images(weight, text_b):
         return jnp.einsum("cr,ce->re", weight, text_b, preferred_element_type=F32)
 
-    weight_far = weights(text_far, 1 - c)
+    weight_own = weights(text_own, 0)
+    image_grad = to_images(weight_own, text_own)
+    text_far, weight_own, image_grad = lax.optimization_barrier((text_far, weight_own, image_grad))
+    weight_far = weights(text_far, 4 * quarter)
+    image_grad = (image_grad + to_images(weight_far, text_far)).astype(HALF)
+    weight_own, weight_far, image_grad = lax.optimization_barrier(
+        (weight_own, weight_far, image_grad)
+    )
     far_grad = swapped(to_texts(weight_far))
-    weight_own = weights(text_own, c)
-    image_grad = to_images(weight_far, text_far) + to_images(weight_own, text_own)
     text_grad = to_texts(weight_own) + far_grad
 
     text_parts = text_grad.astype(HALF).reshape(4, quarter, -1)
     text_grad = text_parts[0].astype(F32)
     for k in range(1, 4):
         text_grad = text_grad + shifted(text_parts[k], "x", -k).astype(F32)
-    image_grad = summed(image_grad.astype(HALF), "y")
+    image_grad = summed(image_grad, "y")
 
     both = jnp.stack([projected(image_grad, image_unit), projected(text_grad, text_unit)])
     norms = jnp.stack([image_norm, text_norm])

time: 150 us -> 154 us (1.027)
  waiting for transfers between devices: 41 us -> 46.5 us
  local copies, waits for them, and re-layouts: 8.21 us -> 5.97 us
  starting transfers between devices: 46.7 us -> 44.8 us
    all_to_all x1, waiting for transfers between devices: 1.76 us -> 5.28 us  [spread(): return lax.all_to_all(copies, axis, 0, 0, tiled=True)]
    all_to_all x1, waiting for transfers between devices: 9.87 us -> 12.7 us  [summed(): lax.all_to_all(parts, axis, 0, 0, tiled=True).astype(F32)]
    all_to_all x1, starting transfers between devices: 5.93 us -> 3.57 us  [summed(): lax.all_to_all(parts, axis, 0, 0, tiled=True).astype(F32)]
    all_to_all x1, starting transfers between devices: 10.2 us -> 11.9 us  [shards(): both = lax.all_to_all(both, COLUMN, 0, 0, tiled=True)]
  transfers between devices with their start and end apart: 11 -> 11, of which waited for: 8 -> 7; matrix products, arithmetic and copies ran while one was open for 6% -> 4% of each run, Pallas kernels for 0% -> 0%
where the time goes in v4:
time: 154 us; the launch traced here: 153 us
  waiting for transfers between devices  46.5 us (30%)
  starting transfers between devices  44.8 us (29%)
  blocking collectives  37.9 us (25%)
  matrix products  11.1 us (7%)
  local copies, waits for them, and re-layouts  5.97 us (4%)
  other arithmetic  5.29 us (3%)
  between operations  1.8 us (1%)
    all_to_all x1, blocking collectives, shards(): pieces = lax.all_to_all(pieces, COLUMN, 0, 0, tiled=True)  37.9 us
    all_to_all x1, waiting for transfers between devices, shards(): both = lax.all_to_all(both, COLUMN, 0, 0, tiled=True)  19.8 us
    ppermute x6, starting transfers between devices, shifted(): lax.ppermute(value, axis, [(k, (k + steps) % count) for k in range(count)])  18.4 us
    all_to_all x1, waiting for transfers between devices, summed(): lax.all_to_all(parts, axis, 0, 0, tiled=True).astype(F32)  12.7 us
    all_to_all x1, starting transfers between devices, shards(): both = lax.all_to_all(both, COLUMN, 0, 0, tiled=True)  11.9 us
    ppermute x6, waiting for transfers between devices, shifted(): lax.ppermute(value, axis, [(k, (k + steps) % count) for k in range(count)])  8.67 us
    all_to_all x1, starting transfers between devices, spread(): return lax.all_to_all(copies, axis, 0, 0, tiled=True)  7.11 us
    all_to_all x1, waiting for transfers between devices, spread(): return lax.all_to_all(copies, axis, 0, 0, tiled=True)  5.28 us
  transfers between devices with their start and end apart: 11, of which 7 were waited for; matrix products, arithmetic and copies ran while one was open for 4% of the time, Pallas kernels for 0%

profile of v4, /device:TPU:6, one launch (start us, length us, event | category | flops | bytes accessed | tf_op | source)
XLA Modules:
  0.0 153.3 jit_solution(16481190904074490382)
XLA Ops:
  0.0 1.1 copy-done
  1.1 1.3 abs_reduce_fusion.1
  2.5 1.3 abs_reduce_fusion
  3.9 0.1 pad_maximum_fusion.3
  4.0 0.1 multiply_convert_fusion.1
  4.1 0.1 multiply_convert_fusion
  4.2 0.1 pad_maximum_fusion.2
  4.4 37.9 %all_to_all.20 = f16[16,72,128]{2,1,0:T(8,128)(2,1)S(1)} all-to-all(f16[16,72,128]{2,1,0:T(8,128)(2,1)S(1)} %fusion.25), channel_id=1, replica_groups=mesh['x'=4,'y'=8,'c'=2,'zl'=8,'zh'=2] {'zh','zl'}, dimensions={0} | all-to-all | bytes 589824 | tf_op jit(solution)/shard_map/all_to_all | solution.py:93
  42.3 0.2 convert_multiply_fusion
  42.6 0.8 copy-done.1
  43.3 0.1 multiply_reduce_fusion.1
  43.5 0.2 copy.19
  43.7 0.1 sqrt.68
  43.7 0.1 fusion.27
  43.8 1.1 broadcast_in_dim.32
  45.0 7.1 %all-to-all-start.1 = ((bf16[8,64,1024]{2,1,0:T(8,128)(2,1)}), bf16[8,64,1024]{2,1,0:T(8,128)(2,1)S(1)}, u32[]{:S(2)}, u32[]{:S(2)}) async-start(bf16[8,64,1024]{2,1,0:T(8,128)(2,1)} %broadcast_in_dim.32), calls=%async_computation.1 | async-start | bytes 2097152 | tf_op jit(solution)/shard_map/all_to_all | solution.py:16
  52.1 0.1 dynamic_slice.13
  52.2 0.1 reshape.654
  52.3 0.2 copy.18
  52.4 0.1 sqrt.66
  52.5 0.1 fusion.59
  52.6 0.4 copy-done.7
  53.0 2.4 %collective-permute-start = (bf16[64,1024]{1,0:T(8,128)(2,1)S(1)}, bf16[64,1024]{1,0:T(8,128)(2,1)S(1)}, u32[]{:S(2)}, u32[]{:S(2)}) collective-permute-start(bf16[64,1024]{1,0:T(8,128)(2,1)S(1)} %fusion.59), channel_id=1, source_target_pairs={{0,256},{256,512},{512,768},{768,0},{1,257},{257,513},{513,769},{7... | collective-permute-start | bytes 393224 | tf_op jit(solution)/shard_map/ppermute | solution.py:31
  55.4 4.3 %collective-permute-start.1 = (bf16[64,1024]{1,0:T(8,128)(2,1)S(1)}, bf16[64,1024]{1,0:T(8,128)(2,1)S(1)}, u32[]{:S(2)}, u32[]{:S(2)}) collective-permute-start(bf16[64,1024]{1,0:T(8,128)(2,1)S(1)} %fusion.59), channel_id=1, source_target_pairs={{0,512},{256,768},{512,0},{768,256},{1,513},{257,769},{513,1},{769... | collective-permute-start | bytes 393224 | tf_op jit(solution)/shard_map/ppermute | solution.py:31
  59.7 1.9 %collective-permute-start.2 = (bf16[64,1024]{1,0:T(8,128)(2,1)S(1)}, bf16[64,1024]{1,0:T(8,128)(2,1)S(1)}, u32[]{:S(2)}, u32[]{:S(2)}) collective-permute-start(bf16[64,1024]{1,0:T(8,128)(2,1)S(1)} %fusion.59), channel_id=1, source_target_pairs={{0,768},{256,0},{512,256},{768,512},{1,769},{257,1},{513,257},{769... | collective-permute-start | bytes 393224 | tf_op jit(solution)/shard_map/ppermute | solution.py:31
  63.0 0.6 iota_add_fusion
  63.6 0.2 collective-permute-done.1
  63.7 4.0 %collective-permute-done.2 = bf16[64,1024]{1,0:T(8,128)(2,1)S(1)} collective-permute-done((bf16[64,1024]{1,0:T(8,128)(2,1)S(1)}, bf16[64,1024]{1,0:T(8,128)(2,1)S(1)}, u32[]{:S(2)}, u32[]{:S(2)}) %collective-permute-start.2) | collective-permute-done | bytes 131104 | tf_op jit(solution)/shard_map/ppermute | solution.py:31
  67.8 1.9 %collective-permute-start.3 = (bf16[256,1024]{1,0:T(8,128)(2,1)S(1)}, bf16[256,1024]{1,0:T(8,128)(2,1)}, u32[]{:S(2)}, u32[]{:S(2)}) collective-permute-start(bf16[256,1024]{1,0:T(8,128)(2,1)S(1)} %pad_maximum_fusion), channel_id=1, source_target_pairs={{0,16},{16,0},{1,17},{17,1},{2,18},{18,2},{3,19},{19,3},{4,20},{20... | collective-permute-start | bytes 1572872 | tf_op jit(solution)/shard_map/ppermute | solution.py:26
  69.8 5.3 %all-to-all-done.1 = bf16[8,64,1024]{2,1,0:T(8,128)(2,1)S(1)} async-done(((bf16[8,64,1024]{2,1,0:T(8,128)(2,1)}), bf16[8,64,1024]{2,1,0:T(8,128)(2,1)S(1)}, u32[]{:S(2)}, u32[]{:S(2)}) %all-to-all-start.1) | async-done | bytes 1048608 | tf_op jit(solution)/shard_map/all_to_all | solution.py:16
  75.0 1.6 %fusion.17 = bf16[256,512]{1,0:T(8,128)(2,1)S(1)} fusion(bf16[512,1024]{1,0:T(8,128)(2,1)S(1)} %bitcast.88, f32[]{:T(128)} %bitcast.85, f32[]{:T(128)} %bitcast.11, s32[512]{0:T(512)S(1)} %fusion.44, bf16[64,1024]{1,0:T(8,128)(2,1)} %copy-done.4, bf16[64,1024]{1,0:T(8,128)(2,1)S(1)} %collective-permute-done.1, ...), kind=kOutput, calls=%fused_computation.22 | convolution fusion | flops 272105472 | bytes 1837064 | tf_op jit(solution)/shard_map/ce,re->cr/dot_general | solution.py:116
  76.7 0.5 fusion.60
  77.2 0.2 copy-done.3
  77.4 1.7 %fusion.18 = bf16[256,512]{1,0:T(8,128)(2,1)S(1)} fusion(bf16[256,1024]{1,0:T(8,128)(2,1)} %collective-permute-done.3, bf16[512,1024]{1,0:T(8,128)(2,1)S(1)} %bitcast.89, f32[]{:T(128)} %bitcast.86, f32[]{:T(128)} %bitcast.11, s32[512]{0:T(512)S(1)} %fusion.44, s32[256]{0:T(256)S(1)} %copy-done.9), kind=kOutput, calls=%fused_computation.23 | convolution fusion | flops 270008320 | bytes 1838088 | tf_op jit(solution)/shard_map/ce,re->cr/dot_general | solution.py:116
  79.0 1.5 fusion.62
  80.5 1.5 add_convert_fusion
  82.0 1.4 fusion.63
  83.5 1.9 %collective-permute-start.4 = (f32[256,1024]{1,0:T(8,128)}, f32[256,1024]{1,0:T(8,128)}, u32[]{:S(2)}, u32[]{:S(2)}) collective-permute-start(f32[256,1024]{1,0:T(8,128)} %fusion.63), channel_id=1, source_target_pairs={{0,16},{16,0},{1,17},{17,1},{2,18},{18,2},{3,19},{19,3},{4,20},{20... | collective-permute-start | bytes 3145736 | tf_op jit(solution)/shard_map/ppermute | solution.py:26
  85.4 3.6 %all-to-all-start.2 = ((f16[8,64,1024]{2,1,0:T(8,128)(2,1)}), f16[8,64,1024]{2,1,0:T(8,128)(2,1)S(1)}, u32[]{:S(2)}, u32[]{:S(2)}) async-start(f16[8,64,1024]{2,1,0:T(8,128)(2,1)} %bitcast.15), calls=%async_computation.2 | async-start | bytes 2097152 | tf_op jit(solution)/shard_map/all_to_all | solution.py:22
  89.0 0.1 sqrt.69
  89.0 0.1 sqrt.70
  89.1 0.1 stack.21
  89.2 0.1 stack.22
  89.3 1.8 %fusion = f16[256,1024]{1,0:T(8,128)(2,1)S(1)} fusion(f32[256,1024]{1,0:T(8,128)} %collective-permute-done.4, bf16[256,512]{1,0:T(8,128)(2,1)} %copy-done.3, bf16[512,1024]{1,0:T(8,128)(2,1)S(1)} %bitcast.91), kind=kOutput, calls=%fused_computation.3 | convolution fusion | flops 268959744 | bytes 2883584 | tf_op jit(solution)/shard_map/dot_general | solution.py:123
  91.2 2.7 %collective-permute-start.5 = (f16[64,1024]{1,0:T(8,128)(2,1)S(1)}, f16[64,1024]{1,0:T(8,128)(2,1)S(1)}, u32[]{:S(2)}, u32[]{:S(2)}) collective-permute-start(f16[64,1024]{1,0:T(8,128)(2,1)S(1)} %get-tuple-element.21), channel_id=1, source_target_pairs={{0,768},{256,0},{512,256},{768,512},{1,769},{257,1},{513,257},{769... | collective-permute-start | bytes 393224 | tf_op jit(solution)/shard_map/ppermute | solution.py:31
  93.9 3.0 %collective-permute-start.6 = (f16[64,1024]{1,0:T(8,128)(2,1)S(1)}, f16[64,1024]{1,0:T(8,128)(2,1)S(1)}, u32[]{:S(2)}, u32[]{:S(2)}) collective-permute-start(f16[64,1024]{1,0:T(8,128)(2,1)S(1)} %get-tuple-element.23), channel_id=1, source_target_pairs={{0,512},{256,768},{512,0},{768,256},{1,513},{257,769},{513,1},{769... | collective-permute-start | bytes 393224 | tf_op jit(solution)/shard_map/ppermute | solution.py:31
  96.9 4.0 %collective-permute-start.7 = (f16[64,1024]{1,0:T(8,128)(2,1)S(1)}, f16[64,1024]{1,0:T(8,128)(2,1)S(1)}, u32[]{:S(2)}, u32[]{:S(2)}) collective-permute-start(f16[64,1024]{1,0:T(8,128)(2,1)S(1)} %get-tuple-element.22), channel_id=1, source_target_pairs={{0,256},{256,512},{512,768},{768,0},{1,257},{257,513},{513,769},{7... | collective-permute-start | bytes 393224 | tf_op jit(solution)/shard_map/ppermute | solution.py:31
  101.0 2.0 %collective-permute-done.6 = f16[64,1024]{1,0:T(8,128)(2,1)S(1)} collective-permute-done((f16[64,1024]{1,0:T(8,128)(2,1)S(1)}, f16[64,1024]{1,0:T(8,128)(2,1)S(1)}, u32[]{:S(2)}, u32[]{:S(2)}) %collective-permute-start.6) | collective-permute-done | bytes 131104 | tf_op jit(solution)/shard_map/ppermute | solution.py:31
  103.0 2.5 %collective-permute-done.7 = f16[64,1024]{1,0:T(8,128)(2,1)S(1)} collective-permute-done((f16[64,1024]{1,0:T(8,128)(2,1)S(1)}, f16[64,1024]{1,0:T(8,128)(2,1)S(1)}, u32[]{:S(2)}, u32[]{:S(2)}) %collective-permute-start.7) | collective-permute-done | bytes 131104 | tf_op jit(solution)/shard_map/ppermute | solution.py:31
  105.5 0.2 multiply_reduce_fusion
  105.7 0.1 subtract_bitcast_fusion
  105.9 12.7 %all-to-all-done.2 = f16[8,64,1024]{2,1,0:T(8,128)(2,1)S(1)} async-done(((f16[8,64,1024]{2,1,0:T(8,128)(2,1)}), f16[8,64,1024]{2,1,0:T(8,128)(2,1)S(1)}, u32[]{:S(2)}, u32[]{:S(2)}) %all-to-all-start.2) | async-done | bytes 1048608 | tf_op jit(solution)/shard_map/all_to_all | solution.py:22
  118.6 0.2 convert_reduce_fusion
  118.9 0.2 fusion.31
  119.1 0.1 mul.148
  119.2 0.2 bitcast_subtract_fusion
  119.4 0.2 fusion.26
  119.6 0.1 pad_maximum_fusion.1
  119.7 0.8 copy.22
  120.5 11.9 %all-to-all-start.3 = ((f16[16,72,128]{2,1,0:T(8,128)(2,1)}), f16[16,72,128]{2,1,0:T(8,128)(2,1)S(1)}, u32[]{:S(2)}, u32[]{:S(2)}) async-start(f16[16,72,128]{2,1,0:T(8,128)(2,1)} %bitcast.19), calls=%async_computation.3 | async-start | bytes 589824 | tf_op jit(solution)/shard_map/all_to_all | solution.py:151
  132.4 19.8 %all-to-all-done.3 = f16[16,72,128]{2,1,0:T(8,128)(2,1)S(1)} async-done(((f16[16,72,128]{2,1,0:T(8,128)(2,1)}), f16[16,72,128]{2,1,0:T(8,128)(2,1)S(1)}, u32[]{:S(2)}, u32[]{:S(2)}) %all-to-all-start.3) | async-done | bytes 294944 | tf_op jit(solution)/shard_map/all_to_all | solution.py:151
  152.4 0.1 squeeze.32
  152.4 0.1 squeeze.33
  152.6 0.8 bitcast_divide_fusion.2
  (47 shorter events, 0.7 us)
Async XLA Ops:
  0.0 1.1 copy-start
  42.5 0.8 copy-start.1
  43.5 8.6 %copy-start.6 = (s32[16384]{0:T(1024)S(1)}, s32[16384]{0:T(1024)}, u32[]{:S(2)}) copy-start(s32[16384]{0:T(1024)} %param.11) | copy-start | bytes 196612
  45.0 30.1 %all-to-all-start.1 = ((bf16[8,64,1024]{2,1,0:T(8,128)(2,1)}), bf16[8,64,1024]{2,1,0:T(8,128)(2,1)S(1)}, u32[]{:S(2)}, u32[]{:S(2)}) async-start(bf16[8,64,1024]{2,1,0:T(8,128)(2,1)} %broadcast_in_dim.32), calls=%async_computation.1 | async-start | bytes 2097152 | tf_op jit(solution)/shard_map/all_to_all | solution.py:16
  52.4 0.6 copy-start.7
  53.0 10.6 %collective-permute-start = (bf16[64,1024]{1,0:T(8,128)(2,1)S(1)}, bf16[64,1024]{1,0:T(8,128)(2,1)S(1)}, u32[]{:S(2)}, u32[]{:S(2)}) collective-permute-start(bf16[64,1024]{1,0:T(8,128)(2,1)S(1)} %fusion.59), channel_id=1, source_target_pairs={{0,256},{256,512},{512,768},{768,0},{1,257},{257,513},{513,769},{7... | collective-permute-start | bytes 393224 | tf_op jit(solution)/shard_map/ppermute | solution.py:31
  55.4 8.4 %collective-permute-start.1 = (bf16[64,1024]{1,0:T(8,128)(2,1)S(1)}, bf16[64,1024]{1,0:T(8,128)(2,1)S(1)}, u32[]{:S(2)}, u32[]{:S(2)}) collective-permute-start(bf16[64,1024]{1,0:T(8,128)(2,1)S(1)} %fusion.59), channel_id=1, source_target_pairs={{0,512},{256,768},{512,0},{768,256},{1,513},{257,769},{513,1},{769... | collective-permute-start | bytes 393224 | tf_op jit(solution)/shard_map/ppermute | solution.py:31
  59.7 8.1 %collective-permute-start.2 = (bf16[64,1024]{1,0:T(8,128)(2,1)S(1)}, bf16[64,1024]{1,0:T(8,128)(2,1)S(1)}, u32[]{:S(2)}, u32[]{:S(2)}) collective-permute-start(bf16[64,1024]{1,0:T(8,128)(2,1)S(1)} %fusion.59), channel_id=1, source_target_pairs={{0,768},{256,0},{512,256},{768,512},{1,769},{257,1},{513,257},{769... | collective-permute-start | bytes 393224 | tf_op jit(solution)/shard_map/ppermute | solution.py:31
  67.8 7.3 %copy-start.4 = (bf16[64,1024]{1,0:T(8,128)(2,1)}, bf16[64,1024]{1,0:T(8,128)(2,1)S(1)}, u32[]{:S(2)}) copy-start(bf16[64,1024]{1,0:T(8,128)(2,1)S(1)} %collective-permute-done.2) | copy-start | bytes 393220
  67.8 9.3 %collective-permute-start.3 = (bf16[256,1024]{1,0:T(8,128)(2,1)S(1)}, bf16[256,1024]{1,0:T(8,128)(2,1)}, u32[]{:S(2)}, u32[]{:S(2)}) collective-permute-start(bf16[256,1024]{1,0:T(8,128)(2,1)S(1)} %pad_maximum_fusion), channel_id=1, source_target_pairs={{0,16},{16,0},{1,17},{17,1},{2,18},{18,2},{3,19},{19,3},{4,20},{20... | collective-permute-start | bytes 1572872 | tf_op jit(solution)/shard_map/ppermute | solution.py:26
  75.0 1.6 %copy-start.5 = (bf16[64,1024]{1,0:T(8,128)(2,1)S(1)}, bf16[64,1024]{1,0:T(8,128)(2,1)}, u32[]{:S(2)}) copy-start(bf16[64,1024]{1,0:T(8,128)(2,1)} %copy-done.4) | copy-start | bytes 393220
  76.7 0.7 copy-start.3
  76.7 0.7 copy-start.9
  82.0 7.0 %copy-start.8 = (f32[2,32]{1,0:T(2,128)S(1)}, f32[2,32]{1,0:T(2,128)}, u32[]{:S(2)}) copy-start(f32[2,32]{1,0:T(2,128)} %copy-done.7) | copy-start | bytes 772
  83.5 5.8 %collective-permute-start.4 = (f32[256,1024]{1,0:T(8,128)}, f32[256,1024]{1,0:T(8,128)}, u32[]{:S(2)}, u32[]{:S(2)}) collective-permute-start(f32[256,1024]{1,0:T(8,128)} %fusion.63), channel_id=1, source_target_pairs={{0,16},{16,0},{1,17},{17,1},{2,18},{18,2},{3,19},{19,3},{4,20},{20... | collective-permute-start | bytes 3145736 | tf_op jit(solution)/shard_map/ppermute | solution.py:26
  85.4 33.2 %all-to-all-start.2 = ((f16[8,64,1024]{2,1,0:T(8,128)(2,1)}), f16[8,64,1024]{2,1,0:T(8,128)(2,1)S(1)}, u32[]{:S(2)}, u32[]{:S(2)}) async-start(f16[8,64,1024]{2,1,0:T(8,128)(2,1)} %bitcast.15), calls=%async_computation.2 | async-start | bytes 2097152 | tf_op jit(solution)/shard_map/all_to_all | solution.py:22
  91.2 9.8 %collective-permute-start.5 = (f16[64,1024]{1,0:T(8,128)(2,1)S(1)}, f16[64,1024]{1,0:T(8,128)(2,1)S(1)}, u32[]{:S(2)}, u32[]{:S(2)}) collective-permute-start(f16[64,1024]{1,0:T(8,128)(2,1)S(1)} %get-tuple-element.21), channel_id=1, source_target_pairs={{0,768},{256,0},{512,256},{768,512},{1,769},{257,1},{513,257},{769... | collective-permute-start | bytes 393224 | tf_op jit(solution)/shard_map/ppermute | solution.py:31
  93.9 9.1 %collective-permute-start.6 = (f16[64,1024]{1,0:T(8,128)(2,1)S(1)}, f16[64,1024]{1,0:T(8,128)(2,1)S(1)}, u32[]{:S(2)}, u32[]{:S(2)}) collective-permute-start(f16[64,1024]{1,0:T(8,128)(2,1)S(1)} %get-tuple-element.23), channel_id=1, source_target_pairs={{0,512},{256,768},{512,0},{768,256},{1,513},{257,769},{513,1},{769... | collective-permute-start | bytes 393224 | tf_op jit(solution)/shard_map/ppermute | solution.py:31
  96.9 8.5 %collective-permute-start.7 = (f16[64,1024]{1,0:T(8,128)(2,1)S(1)}, f16[64,1024]{1,0:T(8,128)(2,1)S(1)}, u32[]{:S(2)}, u32[]{:S(2)}) collective-permute-start(f16[64,1024]{1,0:T(8,128)(2,1)S(1)} %get-tuple-element.22), channel_id=1, source_target_pairs={{0,256},{256,512},{512,768},{768,0},{1,257},{257,513},{513,769},{7... | collective-permute-start | bytes 393224 | tf_op jit(solution)/shard_map/ppermute | solution.py:31
  101.0 17.9 %copy-start.2 = (f32[16,64,128]{2,1,0:T(8,128)S(1)}, f32[16,64,128]{2,1,0:T(8,128)}, u32[]{:S(2)}) copy-start(f32[16,64,128]{2,1,0:T(8,128)} %copy-done.1) | copy-start | bytes 1572868
  120.5 31.7 %all-to-all-start.3 = ((f16[16,72,128]{2,1,0:T(8,128)(2,1)}), f16[16,72,128]{2,1,0:T(8,128)(2,1)S(1)}, u32[]{:S(2)}, u32[]{:S(2)}) async-start(f16[16,72,128]{2,1,0:T(8,128)(2,1)} %bitcast.19), calls=%async_computation.3 | async-start | bytes 589824 | tf_op jit(solution)/shard_map/all_to_all | solution.py:151

commit v5 on v4

--- a/solution.py
+++ b/solution.py
@@ -3,7 +3,8 @@
 from jax import lax
 from jax.sharding import Mesh, PartitionSpec as P
 
-BLK = ("x", "y", "c")
+BLK = ("x", "ya", "yb", "c")
+TEXT_GROUP = ("x", "yb")
 AXES = BLK + ("zl", "zh")
 COLUMN = ("zh", "zl")
 F32 = jnp.float32
@@ -62,7 +63,7 @@
     lanes = lax.axis_size("zl")
     quarter = rows // 4
     half = quarter // 2
-    x, y, c = (lax.axis_index(name) for name in BLK)
+    x, ya, yb, c = (lax.axis_index(name) for name in BLK)
     zh = lax.axis_index("zh")
     plane = zh * lanes + lax.axis_index("zl")
     image_part, text_part = plane // 4, plane % 4
@@ -98,18 +99,20 @@
     image_unit, image_norm = normalize(whole[0])
     text_unit, text_norm = normalize(whole[1])
 
-    text_b = text_unit.astype(jnp.bfloat16)
-    image_b = spread(image_unit.astype(jnp.bfloat16), "y").reshape(8 * quarter, -1)
-    text_own = jnp.concatenate([text_b] + [shifted(text_b, "x", k) for k in range(1, 4)])
+    text_own = spread(text_unit.astype(jnp.bfloat16), TEXT_GROUP).reshape(8 * quarter, -1)
+    image_b = image_unit.astype(jnp.bfloat16)
+    image_b = jnp.concatenate([image_b] + [shifted(image_b, "ya", k) for k in range(1, 4)])
     text_far = swapped(text_own)
 
-    keys = positive.reshape(-1, 2 * rows)
-    keys = lax.dynamic_slice(keys, (x * 8, c * rows + image_part * quarter), (8, quarter))
-    keys = keys.reshape(1, 8 * quarter)
+    keys = positive.reshape(4, 4, 2, 2 * rows)
+    keys = lax.dynamic_slice(keys, (x, 0, yb, c * rows + image_part * quarter), (1, 4, 1, quarter))
+    keys = keys.reshape(4, quarter)[::-1]
+    keys = lax.dynamic_slice(jnp.concatenate([keys, keys]), (3 - ya, 0), (4, quarter))
+    keys = keys.reshape(1, 4 * quarter)
     key_block, key_row = keys // rows, keys % rows
-    place = ((x - key_block // 16) & 3) * quarter + key_row % quarter
-    place = place + jnp.where(key_block % 2 == c, 0, 4 * quarter)
-    inside = (key_block // 2 % 8 == y) & (key_row // quarter == text_part)
+    place = (key_block // 16 * 2 + key_block // 2 % 2) * quarter + key_row % quarter
+    place = place + jnp.where(key_block % 2 == c, 0, 8 * quarter)
+    inside = (key_block // 4 % 4 == ya) & (key_row // quarter == text_part)
     place = jnp.where(inside, place, -1)
 
     def weights(text_b, first):
@@ -125,22 +128,19 @@
     def to_images(weight, text_b):
         return jnp.einsum("cr,ce->re", weight, text_b, preferred_element_type=F32)
 
+    weight_far = weights(text_far, 8 * quarter)
+    far_grad = swapped(to_texts(weight_far).astype(HALF))
     weight_own = weights(text_own, 0)
-    image_grad = to_images(weight_own, text_own)
-    text_far, weight_own, image_grad = lax.optimization_barrier((text_far, weight_own, image_grad))
-    weight_far = weights(text_far, 4 * quarter)
-    image_grad = (image_grad + to_images(weight_far, text_far)).astype(HALF)
-    weight_own, weight_far, image_grad = lax.optimization_barrier(
-        (weight_own, weight_far, image_grad)
+    text_grad = (to_texts(weight_own) + far_grad.astype(F32)).astype(HALF)
+    weight_own, weight_far, text_grad = lax.optimization_barrier(
+        (weight_own, weight_far, text_grad)
     )
-    far_grad = swapped(to_texts(weight_far))
-    text_grad = to_texts(weight_own) + far_grad
-
-    text_parts = text_grad.astype(HALF).reshape(4, quarter, -1)
-    text_grad = text_parts[0].astype(F32)
+    image_grad = to_images(weight_own, text_own) + to_images(weight_far, text_far)
+    image_parts = image_grad.astype(HALF).reshape(4, quarter, -1)
+    image_grad = image_parts[0].astype(F32)
     for k in range(1, 4):
-        text_grad = text_grad + shifted(text_parts[k], "x", -k).astype(F32)
-    image_grad = summed(image_grad, "y")
+        image_grad = image_grad + shifted(image_parts[k], "ya", -k).astype(F32)
+    text_grad = summed(text_grad, TEXT_GROUP)
 
     both = jnp.stack([projected(image_grad, image_unit), projected(text_grad, text_unit)])
     norms = jnp.stack([image_norm, text_norm])
@@ -157,7 +157,7 @@
 
 
 def solution(mesh):
-    fine = Mesh(mesh.devices.reshape(4, 8, 2, 8, 2), AXES)
+    fine = Mesh(mesh.devices.reshape(4, 4, 2, 2, 8, 2), AXES)
     placed = (P(BLK, None), P(BLK, None), P(None, "zl"), P(None, "zl"), P(), P(), P())
     return jax.shard_map(
         shards, mesh=fine, in_specs=placed, out_specs=P("zh", BLK, "zl"), check_vma=False

time: 154 us -> 162 us (1.052)
  the two profiles are of different devices: /device:TPU:6 before, /device:TPU:10 now
where the time goes in v5:
time: 162 us; the launch traced here: 161 us
  starting transfers between devices  57 us (35%)
  waiting for transfers between devices  44.7 us (28%)
  blocking collectives  38 us (23%)
  matrix products  10.1 us (6%)
  local copies, waits for them, and re-layouts  6.43 us (4%)
  other arithmetic  3.21 us (2%)
  between operations  1.77 us (1%)
    all_to_all x1, blocking collectives, shards(): pieces = lax.all_to_all(pieces, COLUMN, 0, 0, tiled=True)  38 us
    ppermute x6, starting transfers between devices, shifted(): lax.ppermute(value, axis, [(k, (k + steps) % count) for k in range(count)])  28.3 us
    all_to_all x1, waiting for transfers between devices, shards(): both = lax.all_to_all(both, COLUMN, 0, 0, tiled=True)  19.2 us
    ppermute x6, waiting for transfers between devices, shifted(): lax.ppermute(value, axis, [(k, (k + steps) % count) for k in range(count)])  14.1 us
    all_to_all x1, starting transfers between devices, shards(): both = lax.all_to_all(both, COLUMN, 0, 0, tiled=True)  10.4 us
    all_to_all x1, waiting for transfers between devices, spread(): return lax.all_to_all(copies, axis, 0, 0, tiled=True)  9.39 us
    all_to_all x1, starting transfers between devices, summed(): lax.all_to_all(parts, axis, 0, 0, tiled=True).astype(F32)  8.54 us
    all_to_all x1, starting transfers between devices, spread(): return lax.all_to_all(copies, axis, 0, 0, tiled=True)  5.85 us
  transfers between devices with their start and end apart: 11, of which 7 were waited for; matrix products, arithmetic and copies ran while one was open for 3% of the time, Pallas kernels for 0%

profile of v5, /device:TPU:10, one launch (start us, length us, event | category | flops | bytes accessed | tf_op | source)
XLA Modules:
  0.0 161.1 jit_solution(6610657430066977203)
XLA Ops:
  0.0 1.1 copy-done
  1.1 1.3 abs_reduce_fusion.1
  2.5 1.3 abs_reduce_fusion
  3.9 0.1 pad_maximum_fusion.3
  4.0 0.1 multiply_convert_fusion.1
  4.1 0.1 multiply_convert_fusion
  4.2 0.1 pad_maximum_fusion.2
  4.3 0.1 fusion.25
  4.4 38.0 %all_to_all.20 = f16[16,72,128]{2,1,0:T(8,128)(2,1)S(1)} all-to-all(f16[16,72,128]{2,1,0:T(8,128)(2,1)S(1)} %fusion.25), channel_id=1, replica_groups=mesh['x'=4,'ya'=4,'yb'=2,'c'=2,'zl'=8,'zh'=2] {'zh','zl'}, dimensions={0} | all-to-all | bytes 589824 | tf_op jit(solution)/shard_map/all_to_all | solution.py:94
  42.3 0.2 convert_multiply_fusion
  42.6 0.8 copy-done.1
  43.4 0.1 multiply_reduce_fusion.1
  43.5 0.2 copy.18
  43.7 0.1 sqrt.66
  43.8 0.1 fusion.27
  43.9 1.1 broadcast_in_dim.37
  45.0 5.8 %all-to-all-start.1 = ((bf16[8,64,1024]{2,1,0:T(8,128)(2,1)}), bf16[8,64,1024]{2,1,0:T(8,128)(2,1)S(1)}, u32[]{:S(2)}, u32[]{:S(2)}) async-start(bf16[8,64,1024]{2,1,0:T(8,128)(2,1)} %broadcast_in_dim.37), calls=%async_computation.1 | async-start | bytes 2097152 | tf_op jit(solution)/shard_map/all_to_all | solution.py:17
  50.9 9.4 %all-to-all-done.1 = bf16[8,64,1024]{2,1,0:T(8,128)(2,1)S(1)} async-done(((bf16[8,64,1024]{2,1,0:T(8,128)(2,1)}), bf16[8,64,1024]{2,1,0:T(8,128)(2,1)S(1)}, u32[]{:S(2)}, u32[]{:S(2)}) %all-to-all-start.1) | async-done | bytes 1048608 | tf_op jit(solution)/shard_map/all_to_all | solution.py:17
  60.3 1.9 %collective-permute-start.3 = (bf16[512,1024]{1,0:T(8,128)(2,1)S(1)}, bf16[512,1024]{1,0:T(8,128)(2,1)}, u32[]{:S(2)}, u32[]{:S(2)}) collective-permute-start(bf16[512,1024]{1,0:T(8,128)(2,1)S(1)} %bitcast.90), channel_id=1, source_target_pairs={{0,16},{16,0},{1,17},{17,1},{2,18},{18,2},{3,19},{19,3},{4,20},{20... | collective-permute-start | bytes 3145736 | tf_op jit(solution)/shard_map/ppermute | solution.py:27
  62.2 0.1 constant_dynamic-slice_fusion.1
  62.3 0.1 reshape.698
  62.4 0.2 copy.19
  62.6 0.1 sqrt.68
  62.7 0.1 fusion.49
  62.8 4.5 %collective-permute-start = (bf16[64,1024]{1,0:T(8,128)(2,1)S(1)}, bf16[64,1024]{1,0:T(8,128)(2,1)S(1)}, u32[]{:S(2)}, u32[]{:S(2)}) collective-permute-start(bf16[64,1024]{1,0:T(8,128)(2,1)S(1)} %fusion.49), channel_id=1, source_target_pairs={{0,64},{64,128},{128,192},{192,0},{1,65},{65,129},{129,193},{193,1... | collective-permute-start | bytes 393224 | tf_op jit(solution)/shard_map/ppermute | solution.py:32
  67.3 5.0 %collective-permute-start.1 = (bf16[64,1024]{1,0:T(8,128)(2,1)S(1)}, bf16[64,1024]{1,0:T(8,128)(2,1)S(1)}, u32[]{:S(2)}, u32[]{:S(2)}) collective-permute-start(bf16[64,1024]{1,0:T(8,128)(2,1)S(1)} %fusion.49), channel_id=1, source_target_pairs={{0,128},{64,192},{128,0},{192,64},{1,129},{65,193},{129,1},{193,65... | collective-permute-start | bytes 393224 | tf_op jit(solution)/shard_map/ppermute | solution.py:32
  72.3 5.2 %collective-permute-start.2 = (bf16[64,1024]{1,0:T(8,128)(2,1)S(1)}, bf16[64,1024]{1,0:T(8,128)(2,1)S(1)}, u32[]{:S(2)}, u32[]{:S(2)}) collective-permute-start(bf16[64,1024]{1,0:T(8,128)(2,1)S(1)} %fusion.49), channel_id=1, source_target_pairs={{0,192},{64,0},{128,64},{192,128},{1,193},{65,1},{129,65},{193,129... | collective-permute-start | bytes 393224 | tf_op jit(solution)/shard_map/ppermute | solution.py:32
  79.0 2.5 %collective-permute-done.1 = bf16[64,1024]{1,0:T(8,128)(2,1)S(1)} collective-permute-done((bf16[64,1024]{1,0:T(8,128)(2,1)S(1)}, bf16[64,1024]{1,0:T(8,128)(2,1)S(1)}, u32[]{:S(2)}, u32[]{:S(2)}) %collective-permute-start.1) | collective-permute-done | bytes 131104 | tf_op jit(solution)/shard_map/ppermute | solution.py:32
  81.4 1.0 collective-permute-done.2
  82.4 1.8 %fusion.18 = bf16[512,256]{1,0:T(8,128)(2,1)S(1)} fusion(bf16[512,1024]{1,0:T(8,128)(2,1)} %collective-permute-done.3, f32[]{:T(128)} %bitcast.85, f32[]{:T(128)} %bitcast.1, s32[256]{0:T(256)S(1)} %and_select_fusion.5, s32[512]{0:T(512)S(1)} %iota_add_fusion, bf16[64,1024]{1,0:T(8,128)(2,1)S(1)} %collective-permute-done.2, ...), kind=kOutput, calls=%fused_computation.24 | convolution fusion | flops 272105472 | bytes 1838088 | tf_op jit(solution)/shard_map/ce,re->cr/dot_general | solution.py:119
  84.3 0.5 convolution_convert_fusion
  84.7 0.2 copy-done.4
  84.9 1.9 %collective-permute-start.4 = (f16[512,1024]{1,0:T(8,128)(2,1)S(1)}, f16[512,1024]{1,0:T(8,128)(2,1)S(1)}, u32[]{:S(2)}, u32[]{:S(2)}) collective-permute-start(f16[512,1024]{1,0:T(8,128)(2,1)S(1)} %convolution_convert_fusion), channel_id=1, source_target_pairs={{0,16},{16,0},{1,17},{17,1},{2,18},{18,2},{3,19},{19,3},{4,20},{20... | collective-permute-start | bytes 3145736 | tf_op jit(solution)/shard_map/ppermute | solution.py:27
  86.9 0.6 fusion.17
  87.5 2.0 %collective-permute-done.4 = f16[512,1024]{1,0:T(8,128)(2,1)S(1)} collective-permute-done((f16[512,1024]{1,0:T(8,128)(2,1)S(1)}, f16[512,1024]{1,0:T(8,128)(2,1)S(1)}, u32[]{:S(2)}, u32[]{:S(2)}) %collective-permute-start.4) | collective-permute-done | bytes 1048608 | tf_op jit(solution)/shard_map/ppermute | solution.py:27
  89.5 1.5 add_convert_fusion
  91.0 8.5 %all-to-all-start.2 = ((f16[8,64,1024]{2,1,0:T(8,128)(2,1)}), f16[8,64,1024]{2,1,0:T(8,128)(2,1)S(1)}, u32[]{:S(2)}, u32[]{:S(2)}) async-start(f16[8,64,1024]{2,1,0:T(8,128)(2,1)} %bitcast.102), calls=%async_computation.2 | async-start | bytes 2097152 | tf_op jit(solution)/shard_map/all_to_all | solution.py:23
  99.5 0.1 sqrt.69
  99.6 0.1 sqrt.70
  99.7 0.1 stack.21
  99.8 0.1 stack.22
  99.9 1.4 fusion.51
  101.3 1.7 %fusion = f16[256,1024]{1,0:T(8,128)(2,1)S(1)} fusion(f32[256,1024]{1,0:T(8,128)S(1)} %fusion.51, bf16[512,256]{1,0:T(8,128)(2,1)S(1)} %copy-done.5, bf16[512,1024]{1,0:T(8,128)(2,1)} %collective-permute-done.3), kind=kOutput, calls=%fused_computation.4 | convolution fusion | flops 268959744 | bytes 2883584 | tf_op jit(solution)/shard_map/cr,ce->re/dot_general | solution.py:129
  103.0 0.1 fusion.50
  103.1 5.3 %collective-permute-start.5 = (f16[64,1024]{1,0:T(8,128)(2,1)S(1)}, f16[64,1024]{1,0:T(8,128)(2,1)S(1)}, u32[]{:S(2)}, u32[]{:S(2)}) collective-permute-start(f16[64,1024]{1,0:T(8,128)(2,1)S(1)} %get-tuple-element.15), channel_id=1, source_target_pairs={{0,192},{64,0},{128,64},{192,128},{1,193},{65,1},{129,65},{193,129... | collective-permute-start | bytes 393224 | tf_op jit(solution)/shard_map/ppermute | solution.py:32
  108.4 4.7 %collective-permute-start.6 = (f16[64,1024]{1,0:T(8,128)(2,1)S(1)}, f16[64,1024]{1,0:T(8,128)(2,1)S(1)}, u32[]{:S(2)}, u32[]{:S(2)}) collective-permute-start(f16[64,1024]{1,0:T(8,128)(2,1)S(1)} %get-tuple-element.17), channel_id=1, source_target_pairs={{0,128},{64,192},{128,0},{192,64},{1,129},{65,193},{129,1},{193,65... | collective-permute-start | bytes 393224 | tf_op jit(solution)/shard_map/ppermute | solution.py:32
  113.1 3.6 %collective-permute-start.7 = (f16[64,1024]{1,0:T(8,128)(2,1)S(1)}, f16[64,1024]{1,0:T(8,128)(2,1)S(1)}, u32[]{:S(2)}, u32[]{:S(2)}) collective-permute-start(f16[64,1024]{1,0:T(8,128)(2,1)S(1)} %get-tuple-element.16), channel_id=1, source_target_pairs={{0,64},{64,128},{128,192},{192,0},{1,65},{65,129},{129,193},{193,1... | collective-permute-start | bytes 393224 | tf_op jit(solution)/shard_map/ppermute | solution.py:32
  116.7 4.0 %collective-permute-done.5 = f16[64,1024]{1,0:T(8,128)(2,1)S(1)} collective-permute-done((f16[64,1024]{1,0:T(8,128)(2,1)S(1)}, f16[64,1024]{1,0:T(8,128)(2,1)S(1)}, u32[]{:S(2)}, u32[]{:S(2)}) %collective-permute-start.5) | collective-permute-done | bytes 131104 | tf_op jit(solution)/shard_map/ppermute | solution.py:32
  120.7 6.6 %collective-permute-done.6 = f16[64,1024]{1,0:T(8,128)(2,1)S(1)} collective-permute-done((f16[64,1024]{1,0:T(8,128)(2,1)S(1)}, f16[64,1024]{1,0:T(8,128)(2,1)S(1)}, u32[]{:S(2)}, u32[]{:S(2)}) %collective-permute-start.6) | collective-permute-done | bytes 131104 | tf_op jit(solution)/shard_map/ppermute | solution.py:32
  127.3 0.2 multiply_reduce_fusion
  127.6 0.1 subtract_bitcast_fusion
  127.8 0.2 convert_reduce_fusion
  128.1 0.7 copy-done.2
  128.8 0.2 fusion.31
  129.0 0.1 mul.157
  129.1 0.2 bitcast_subtract_fusion
  129.3 0.2 fusion.26
  129.5 0.1 pad_maximum_fusion.1
  129.6 0.8 copy.22
  130.4 10.4 %all-to-all-start.3 = ((f16[16,72,128]{2,1,0:T(8,128)(2,1)}), f16[16,72,128]{2,1,0:T(8,128)(2,1)S(1)}, u32[]{:S(2)}, u32[]{:S(2)}) async-start(f16[16,72,128]{2,1,0:T(8,128)(2,1)} %bitcast.20), calls=%async_computation.3 | async-start | bytes 589824 | tf_op jit(solution)/shard_map/all_to_all | solution.py:151
  140.9 19.2 %all-to-all-done.3 = f16[16,72,128]{2,1,0:T(8,128)(2,1)S(1)} async-done(((f16[16,72,128]{2,1,0:T(8,128)(2,1)}), f16[16,72,128]{2,1,0:T(8,128)(2,1)S(1)}, u32[]{:S(2)}, u32[]{:S(2)}) %all-to-all-start.3) | async-done | bytes 294944 | tf_op jit(solution)/shard_map/all_to_all | solution.py:151
  160.2 0.1 squeeze.32
  160.2 0.1 squeeze.33
  160.4 0.8 bitcast_divide_fusion.2
  (42 shorter events, 0.6 us)
Async XLA Ops:
  0.0 1.1 copy-start
  42.6 0.8 copy-start.1
  45.0 5.9 %copy-start.6 = (s32[16384]{0:T(1024)S(1)}, s32[16384]{0:T(1024)}, u32[]{:S(2)}) copy-start(s32[16384]{0:T(1024)} %param.11) | copy-start | bytes 196612
  45.0 15.3 %all-to-all-start.1 = ((bf16[8,64,1024]{2,1,0:T(8,128)(2,1)}), bf16[8,64,1024]{2,1,0:T(8,128)(2,1)S(1)}, u32[]{:S(2)}, u32[]{:S(2)}) async-start(bf16[8,64,1024]{2,1,0:T(8,128)(2,1)} %broadcast_in_dim.37), calls=%async_computation.1 | async-start | bytes 2097152 | tf_op jit(solution)/shard_map/all_to_all | solution.py:17
  60.3 22.2 %collective-permute-start.3 = (bf16[512,1024]{1,0:T(8,128)(2,1)S(1)}, bf16[512,1024]{1,0:T(8,128)(2,1)}, u32[]{:S(2)}, u32[]{:S(2)}) collective-permute-start(bf16[512,1024]{1,0:T(8,128)(2,1)S(1)} %bitcast.90), channel_id=1, source_target_pairs={{0,16},{16,0},{1,17},{17,1},{2,18},{18,2},{3,19},{19,3},{4,20},{20... | collective-permute-start | bytes 3145736 | tf_op jit(solution)/shard_map/ppermute | solution.py:27
  62.8 16.2 %collective-permute-start = (bf16[64,1024]{1,0:T(8,128)(2,1)S(1)}, bf16[64,1024]{1,0:T(8,128)(2,1)S(1)}, u32[]{:S(2)}, u32[]{:S(2)}) collective-permute-start(bf16[64,1024]{1,0:T(8,128)(2,1)S(1)} %fusion.49), channel_id=1, source_target_pairs={{0,64},{64,128},{128,192},{192,0},{1,65},{65,129},{129,193},{193,1... | collective-permute-start | bytes 393224 | tf_op jit(solution)/shard_map/ppermute | solution.py:32
  67.3 14.1 %collective-permute-start.1 = (bf16[64,1024]{1,0:T(8,128)(2,1)S(1)}, bf16[64,1024]{1,0:T(8,128)(2,1)S(1)}, u32[]{:S(2)}, u32[]{:S(2)}) collective-permute-start(bf16[64,1024]{1,0:T(8,128)(2,1)S(1)} %fusion.49), channel_id=1, source_target_pairs={{0,128},{64,192},{128,0},{192,64},{1,129},{65,193},{129,1},{193,65... | collective-permute-start | bytes 393224 | tf_op jit(solution)/shard_map/ppermute | solution.py:32
  72.3 10.1 %collective-permute-start.2 = (bf16[64,1024]{1,0:T(8,128)(2,1)S(1)}, bf16[64,1024]{1,0:T(8,128)(2,1)S(1)}, u32[]{:S(2)}, u32[]{:S(2)}) collective-permute-start(bf16[64,1024]{1,0:T(8,128)(2,1)S(1)} %fusion.49), channel_id=1, source_target_pairs={{0,192},{64,0},{128,64},{192,128},{1,193},{65,1},{129,65},{193,129... | collective-permute-start | bytes 393224 | tf_op jit(solution)/shard_map/ppermute | solution.py:32
  84.2 0.7 copy-start.4
  84.9 4.5 %collective-permute-start.4 = (f16[512,1024]{1,0:T(8,128)(2,1)S(1)}, f16[512,1024]{1,0:T(8,128)(2,1)S(1)}, u32[]{:S(2)}, u32[]{:S(2)}) collective-permute-start(f16[512,1024]{1,0:T(8,128)(2,1)S(1)} %convolution_convert_fusion), channel_id=1, source_target_pairs={{0,16},{16,0},{1,17},{17,1},{2,18},{18,2},{3,19},{19,3},{4,20},{20... | collective-permute-start | bytes 3145736 | tf_op jit(solution)/shard_map/ppermute | solution.py:27
  87.5 2.0 %copy-start.3 = (bf16[512,256]{1,0:T(8,128)(2,1)}, bf16[512,256]{1,0:T(8,128)(2,1)S(1)}, u32[]{:S(2)}) copy-start(bf16[512,256]{1,0:T(8,128)(2,1)S(1)} %fusion.17) | copy-start | bytes 786436
  91.0 36.8 %all-to-all-start.2 = ((f16[8,64,1024]{2,1,0:T(8,128)(2,1)}), f16[8,64,1024]{2,1,0:T(8,128)(2,1)S(1)}, u32[]{:S(2)}, u32[]{:S(2)}) async-start(f16[8,64,1024]{2,1,0:T(8,128)(2,1)} %bitcast.102), calls=%async_computation.2 | async-start | bytes 2097152 | tf_op jit(solution)/shard_map/all_to_all | solution.py:23
  99.9 1.5 copy-start.5
  103.1 17.6 %collective-permute-start.5 = (f16[64,1024]{1,0:T(8,128)(2,1)S(1)}, f16[64,1024]{1,0:T(8,128)(2,1)S(1)}, u32[]{:S(2)}, u32[]{:S(2)}) collective-permute-start(f16[64,1024]{1,0:T(8,128)(2,1)S(1)} %get-tuple-element.15), channel_id=1, source_target_pairs={{0,192},{64,0},{128,64},{192,128},{1,193},{65,1},{129,65},{193,129... | collective-permute-start | bytes 393224 | tf_op jit(solution)/shard_map/ppermute | solution.py:32
  108.4 18.9 %collective-permute-start.6 = (f16[64,1024]{1,0:T(8,128)(2,1)S(1)}, f16[64,1024]{1,0:T(8,128)(2,1)S(1)}, u32[]{:S(2)}, u32[]{:S(2)}) collective-permute-start(f16[64,1024]{1,0:T(8,128)(2,1)S(1)} %get-tuple-element.17), channel_id=1, source_target_pairs={{0,128},{64,192},{128,0},{192,64},{1,129},{65,193},{129,1},{193,65... | collective-permute-start | bytes 393224 | tf_op jit(solution)/shard_map/ppermute | solution.py:32
  113.1 14.2 %collective-permute-start.7 = (f16[64,1024]{1,0:T(8,128)(2,1)S(1)}, f16[64,1024]{1,0:T(8,128)(2,1)S(1)}, u32[]{:S(2)}, u32[]{:S(2)}) collective-permute-start(f16[64,1024]{1,0:T(8,128)(2,1)S(1)} %get-tuple-element.16), channel_id=1, source_target_pairs={{0,64},{64,128},{128,192},{192,0},{1,65},{65,129},{129,193},{193,1... | collective-permute-start | bytes 393224 | tf_op jit(solution)/shard_map/ppermute | solution.py:32
  127.8 1.0 copy-start.2
  130.4 29.6 %all-to-all-start.3 = ((f16[16,72,128]{2,1,0:T(8,128)(2,1)}), f16[16,72,128]{2,1,0:T(8,128)(2,1)S(1)}, u32[]{:S(2)}, u32[]{:S(2)}) async-start(f16[16,72,128]{2,1,0:T(8,128)(2,1)} %bitcast.20), calls=%async_computation.3 | async-start | bytes 589824 | tf_op jit(solution)/shard_map/all_to_all | solution.py:151

commit v6 on v5

--- a/solution.py
+++ b/solution.py
@@ -4,32 +4,28 @@
 from jax.sharding import Mesh, PartitionSpec as P
 
 BLK = ("x", "ya", "yb", "c")
-TEXT_GROUP = ("x", "yb")
+IMAGE_GROUP = ("x", "yb")
 AXES = BLK + ("zl", "zh")
 COLUMN = ("zh", "zl")
 F32 = jnp.float32
 HALF = jnp.float16
 
 
-def spread(value, axis):
+def copies(value, axis):
     count = lax.axis_size(axis)
-    copies = jnp.broadcast_to(value[None], (count,) + value.shape)
-    return lax.all_to_all(copies, axis, 0, 0, tiled=True)
+    return jnp.broadcast_to(value[None], (count,) + value.shape)
 
 
-def summed(parts, axis):
-    count = lax.axis_size(axis)
-    parts = parts.reshape((count, -1) + parts.shape[1:])
-    return jnp.sum(lax.all_to_all(parts, axis, 0, 0, tiled=True).astype(F32), axis=0)
+def exchanged(parts, axis):
+    return lax.all_to_all(parts, axis, 0, 0, tiled=True)
+
+
+def totals(parts):
+    return jnp.sum(parts.astype(F32), axis=0)
 
 
 def swapped(value):
     return lax.ppermute(value, "c", [(0, 1), (1, 0)])
-
-
-def shifted(value, axis, steps):
-    count = lax.axis_size(axis)
-    return lax.ppermute(value, axis, [(k, (k + steps) % count) for k in range(count)])
 
 
 def exponent(value):
@@ -91,7 +87,7 @@
     pieces = with_exponents(
         for_planes(image_cols, text_cols), for_planes(image_powers, text_powers)
     )
-    pieces = lax.all_to_all(pieces, COLUMN, 0, 0, tiled=True)
+    pieces = exchanged(pieces, COLUMN)
     pieces, powers = without_exponents(pieces, quarter)
     pieces = pieces * jnp.exp2(powers)[..., None]
     pieces = pieces.reshape(2, lanes, 2, half, width)
@@ -99,20 +95,24 @@
     image_unit, image_norm = normalize(whole[0])
     text_unit, text_norm = normalize(whole[1])
 
-    text_own = spread(text_unit.astype(jnp.bfloat16), TEXT_GROUP).reshape(8 * quarter, -1)
-    image_b = image_unit.astype(jnp.bfloat16)
-    image_b = jnp.concatenate([image_b] + [shifted(image_b, "ya", k) for k in range(1, 4)])
+    text_own = copies(text_unit.astype(jnp.bfloat16), "ya")
+    image_b = copies(image_unit.astype(jnp.bfloat16), IMAGE_GROUP)
+    text_own, image_b = lax.optimization_barrier((text_own, image_b))
+    text_own = exchanged(text_own, "ya")
+    text_own, image_b, positive = lax.optimization_barrier((text_own, image_b, positive))
+    text_own = text_own.reshape(4 * quarter, -1)
     text_far = swapped(text_own)
+    image_b = exchanged(image_b, IMAGE_GROUP)
+    image_b, text_far = lax.optimization_barrier((image_b, text_far))
+    image_b = image_b.reshape(8 * quarter, -1)
 
     keys = positive.reshape(4, 4, 2, 2 * rows)
-    keys = lax.dynamic_slice(keys, (x, 0, yb, c * rows + image_part * quarter), (1, 4, 1, quarter))
-    keys = keys.reshape(4, quarter)[::-1]
-    keys = lax.dynamic_slice(jnp.concatenate([keys, keys]), (3 - ya, 0), (4, quarter))
-    keys = keys.reshape(1, 4 * quarter)
+    keys = lax.dynamic_slice(keys, (0, ya, 0, c * rows + image_part * quarter), (4, 1, 2, quarter))
+    keys = keys.reshape(1, 8 * quarter)
     key_block, key_row = keys // rows, keys % rows
-    place = (key_block // 16 * 2 + key_block // 2 % 2) * quarter + key_row % quarter
-    place = place + jnp.where(key_block % 2 == c, 0, 8 * quarter)
-    inside = (key_block // 4 % 4 == ya) & (key_row // quarter == text_part)
+    place = key_block // 4 % 4 * quarter + key_row % quarter
+    place = place + jnp.where(key_block % 2 == c, 0, 4 * quarter)
+    inside = (key_block // 16 == x) & (key_block // 2 % 2 == yb) & (key_row // quarter == text_part)
     place = jnp.where(inside, place, -1)
 
     def weights(text_b, first):
@@ -128,30 +128,36 @@
     def to_images(weight, text_b):
         return jnp.einsum("cr,ce->re", weight, text_b, preferred_element_type=F32)
 
-    weight_far = weights(text_far, 8 * quarter)
-    far_grad = swapped(to_texts(weight_far).astype(HALF))
+    weight_far = weights(text_far, 4 * quarter)
+    far_grad = swapped(to_texts(weight_far))
     weight_own = weights(text_own, 0)
-    text_grad = (to_texts(weight_own) + far_grad.astype(F32)).astype(HALF)
-    weight_own, weight_far, text_grad = lax.optimization_barrier(
-        (weight_own, weight_far, text_grad)
+    image_grad = (to_images(weight_far, text_far) + to_images(weight_own, text_own)).astype(HALF)
+    text_grad = (to_texts(weight_own) + far_grad).astype(HALF)
+
+    image_grad = image_grad.reshape(8, quarter, -1)
+    text_grad = text_grad.reshape(4, quarter, -1)
+    powers = exponent(jnp.stack([image_norm, text_norm]))
+    factors = jnp.exp2(powers) / jnp.stack([image_norm, text_norm])
+    image_grad, text_grad, factors, powers, is_image = lax.optimization_barrier(
+        (image_grad, text_grad, factors, powers, zh == 0)
     )
-    image_grad = to_images(weight_own, text_own) + to_images(weight_far, text_far)
-    image_parts = image_grad.astype(HALF).reshape(4, quarter, -1)
-    image_grad = image_parts[0].astype(F32)
-    for k in range(1, 4):
-        image_grad = image_grad + shifted(image_parts[k], "ya", -k).astype(F32)
-    text_grad = summed(text_grad, TEXT_GROUP)
+    text_grad = exchanged(text_grad, "ya")
+    image_grad, text_grad = lax.optimization_barrier((image_grad, text_grad))
+    image_grad = exchanged(image_grad, IMAGE_GROUP)
+    image_grad, text_grad, factors, powers, is_image = lax.optimization_barrier(
+        (image_grad, text_grad, factors, powers, is_image)
+    )
+    image_grad, text_grad = totals(image_grad), totals(text_grad)
 
     both = jnp.stack([projected(image_grad, image_unit), projected(text_grad, text_unit)])
-    norms = jnp.stack([image_norm, text_norm])
-    powers = exponent(norms)
-    both = both * (jnp.exp2(powers) / norms)
+    both = both * factors
     both = both.reshape(2, quarter, lanes, width).transpose(0, 2, 1, 3)
     both = with_exponents(both, powers.reshape(2, 1, quarter)).reshape(planes, quarter + 8, width)
-    both = lax.all_to_all(both, COLUMN, 0, 0, tiled=True)
+    both, is_image = lax.optimization_barrier((both, is_image))
+    both = exchanged(both, COLUMN)
     both, powers = without_exponents(both.reshape(4, 4, quarter + 8, width), quarter)
-    powers = jnp.where(zh == 0, powers[:, 0], powers[0])
-    result = jnp.where(zh == 0, jnp.sum(both, axis=1), jnp.sum(both, axis=0))
+    powers = jnp.where(is_image, powers[:, 0], powers[0])
+    result = jnp.where(is_image, jnp.sum(both, axis=1), jnp.sum(both, axis=0))
     result = result / jnp.exp2(powers)[:, :, None]
     return result.reshape(1, rows, width)
 

time: 162 us -> 161 us (level)
  the two profiles are of different devices: /device:TPU:10 before, /device:TPU:16 now
where the time goes in v6:
time: 161 us; the launch traced here: 160 us
  blocking collectives  127 us (79%)
  starting transfers between devices  8.13 us (5%)
  matrix products  7.81 us (5%)
  waiting for transfers between devices  6.27 us (4%)
  local copies, waits for them, and re-layouts  4.84 us (3%)
  other arithmetic  4.43 us (3%)
  between operations  1.66 us (1%)
    all_to_all x5, blocking collectives, exchanged(): return lax.all_to_all(parts, axis, 0, 0, tiled=True)  127 us
    all_to_all x1, waiting for transfers between devices, exchanged(): return lax.all_to_all(parts, axis, 0, 0, tiled=True)  5.53 us
    all_to_all x1, starting transfers between devices, exchanged(): return lax.all_to_all(parts, axis, 0, 0, tiled=True)  4.3 us
    ppermute x2, starting transfers between devices, swapped(): return lax.ppermute(value, 'c', [(0, 1), (1, 0)])  3.83 us
  transfers between devices with their start and end apart: 3, of which 2 were waited for; matrix products, arithmetic and copies ran while one was open for 3% of the time, Pallas kernels for 0%

profile of v6, /device:TPU:16, one launch (start us, length us, event | category | flops | bytes accessed | tf_op | source)
XLA Modules:
  0.0 160.0 jit_solution(8840340488537736596)
XLA Ops:
  0.0 0.0 copy-start
  0.0 1.1 copy-done
  1.1 1.3 abs_reduce_fusion.1
  2.5 1.3 abs_reduce_fusion
  3.9 0.1 pad_maximum_fusion.2
  4.0 0.1 multiply_convert_fusion.1
  4.1 0.1 multiply_convert_fusion
  4.2 0.1 pad_maximum_fusion.1
  4.3 0.1 fusion.25
  4.4 37.9 %all_to_all.30 = f16[16,72,128]{2,1,0:T(8,128)(2,1)S(1)} all-to-all(f16[16,72,128]{2,1,0:T(8,128)(2,1)S(1)} %fusion.25), channel_id=1, replica_groups=mesh['x'=4,'ya'=4,'yb'=2,'c'=2,'zl'=8,'zh'=2] {'zh','zl'}, dimensions={0} | all-to-all | bytes 589824 | tf_op jit(solution)/shard_map/all_to_all | solution.py:20
  42.3 0.2 convert_multiply_fusion
  42.5 0.1 multiply_reduce_fusion
  42.7 0.1 sqrt.65
  42.8 0.2 copy.20
  42.9 0.1 sqrt.63
  43.0 0.2 copy.19
  43.2 0.1 fusion.27
  43.3 0.1 fusion.28
  43.4 1.1 broadcast_in_dim.30
  44.5 0.0 copy-start.1
  44.6 18.1 %all_to_all.31 = bf16[4,64,1024]{2,1,0:T(8,128)(2,1)S(1)} all-to-all(bf16[4,64,1024]{2,1,0:T(8,128)(2,1)S(1)} %broadcast_in_dim.29), channel_id=1, replica_groups=mesh['x'=4,'ya'=4,'yb'=2,'c'=2,'zl'=8,'zh'=2] {'ya'}, dimensions={0} | all-to-all | bytes 1048576 | tf_op jit(solution)/shard_map/all_to_all | solution.py:20
  62.7 4.3 %all-to-all-start.2 = ((bf16[8,64,1024]{2,1,0:T(8,128)(2,1)}), bf16[8,64,1024]{2,1,0:T(8,128)(2,1)S(1)}, u32[]{:S(2)}, u32[]{:S(2)}) async-start(bf16[8,64,1024]{2,1,0:T(8,128)(2,1)} %broadcast_in_dim.30), calls=%async_computation.2 | async-start | bytes 2097152 | tf_op jit(solution)/shard_map/all_to_all | solution.py:20
  68.3 0.6 iota_add_fusion
  68.9 0.1 stack.8
  69.0 0.1 stack.18
  69.1 1.9 %collective-permute-start = (bf16[256,1024]{1,0:T(8,128)(2,1)S(1)}, bf16[256,1024]{1,0:T(8,128)(2,1)}, u32[]{:S(2)}, u32[]{:S(2)}) collective-permute-start(bf16[256,1024]{1,0:T(8,128)(2,1)S(1)} %bitcast.112), channel_id=1, source_target_pairs={{0,16},{16,0},{1,17},{17,1},{2,18},{18,2},{3,19},{19,3},{4,20},{20... | collective-permute-start | bytes 1572872 | tf_op jit(solution)/shard_map/ppermute | solution.py:28
  71.0 0.5 constant_dynamic-update-slice_fusion.1
  71.5 0.5 constant_dynamic-update-slice_fusion
  72.0 0.0 copy-done.1
  72.1 0.1 constant_dynamic-slice_fusion
  72.1 0.1 reshape.770
  72.3 0.7 collective-permute-done
  73.0 5.5 %all-to-all-done.2 = bf16[8,64,1024]{2,1,0:T(8,128)(2,1)S(1)} async-done(((bf16[8,64,1024]{2,1,0:T(8,128)(2,1)}), bf16[8,64,1024]{2,1,0:T(8,128)(2,1)S(1)}, u32[]{:S(2)}, u32[]{:S(2)}) %all-to-all-start.2) | async-done | bytes 1048608 | tf_op jit(solution)/shard_map/all_to_all | solution.py:20
  78.5 1.7 %fusion.17 = bf16[256,512]{1,0:T(8,128)(2,1)S(1)} fusion(bf16[256,1024]{1,0:T(8,128)(2,1)} %collective-permute-done, bf16[512,1024]{1,0:T(8,128)(2,1)S(1)} %bitcast.97, f32[]{:T(128)} %bitcast.94, f32[]{:T(128)} %bitcast.12, s32[512]{0:T(512)S(1)} %fusion.47, s32[256]{0:T(256)} %iota_add_fusion), kind=kOutput, calls=%fused_computation.22 | convolution fusion | flops 270008320 | bytes 1838088 | tf_op jit(solution)/shard_map/ce,re->cr/dot_general | solution.py:119
  80.2 0.4 fusion.57
  80.6 1.9 %collective-permute-start.1 = (f32[256,1024]{1,0:T(8,128)S(1)}, f32[256,1024]{1,0:T(8,128)S(1)}, u32[]{:S(2)}, u32[]{:S(2)}) collective-permute-start(f32[256,1024]{1,0:T(8,128)S(1)} %fusion.57), channel_id=1, source_target_pairs={{0,16},{16,0},{1,17},{17,1},{2,18},{18,2},{3,19},{19,3},{4,20},{20... | collective-permute-start | bytes 3145736 | tf_op jit(solution)/shard_map/ppermute | solution.py:28
  82.6 0.7 exponential_divide_fusion
  83.3 0.6 fusion.18
  83.9 0.5 fusion.56
  84.4 1.5 add_convert_fusion
  85.9 0.0 collective-permute-done.1
  85.9 0.4 fusion
  86.4 20.8 %all_to_all.32 = f16[4,64,1024]{2,1,0:T(8,128)(2,1)S(1)} all-to-all(f16[4,64,1024]{2,1,0:T(8,128)(2,1)S(1)} %bitcast.115), channel_id=1, replica_groups=mesh['x'=4,'ya'=4,'yb'=2,'c'=2,'zl'=8,'zh'=2] {'ya'}, dimensions={0} | all-to-all | bytes 1048576 | tf_op jit(solution)/shard_map/all_to_all | solution.py:20
  107.1 18.5 %all_to_all.33 = f16[8,64,1024]{2,1,0:T(8,128)(2,1)S(1)} all-to-all(f16[8,64,1024]{2,1,0:T(8,128)(2,1)S(1)} %bitcast.103), channel_id=1, replica_groups=mesh['x'=4,'ya'=4,'yb'=2,'c'=2,'zl'=8,'zh'=2] {'x','yb'}, dimensions={0} | all-to-all | bytes 2097152 | tf_op jit(solution)/shard_map/all_to_all | solution.py:20
  125.6 0.2 convert_reduce_fusion
  125.9 0.1 convert_reduce_fusion.1
  126.1 0.3 fusion.33
  126.3 0.1 mul.157
  126.4 0.1 mul.161
  126.6 0.2 bitcast_subtract_fusion.1
  126.8 0.2 bitcast_subtract_fusion
  127.0 0.2 fusion.26
  127.2 0.1 pad_maximum_fusion
  127.3 0.1 copy.26
  127.4 31.5 %all_to_all.34 = f16[16,72,128]{2,1,0:T(8,128)(2,1)S(1)} all-to-all(f16[16,72,128]{2,1,0:T(8,128)(2,1)S(1)} %bitcast.116), channel_id=1, replica_groups=mesh['x'=4,'ya'=4,'yb'=2,'c'=2,'zl'=8,'zh'=2] {'zh','zl'}, dimensions={0} | all-to-all | bytes 589824 | tf_op jit(solution)/shard_map/all_to_all | solution.py:20
  158.9 0.1 convert_reduce_fusion.2
  159.1 0.1 squeeze.31
  159.1 0.1 squeeze.32
  159.3 0.8 bitcast_divide_fusion.2
  (24 shorter events, 0.5 us)
Async XLA Ops:
  0.0 1.1 copy-start
  44.5 27.5 %copy-start.1 = (s32[16384]{0:T(1024)S(1)}, s32[16384]{0:T(1024)}, u32[]{:S(2)}) copy-start(s32[16384]{0:T(1024)} %param.11) | copy-start | bytes 196612
  62.7 15.8 %all-to-all-start.2 = ((bf16[8,64,1024]{2,1,0:T(8,128)(2,1)}), bf16[8,64,1024]{2,1,0:T(8,128)(2,1)S(1)}, u32[]{:S(2)}, u32[]{:S(2)}) async-start(bf16[8,64,1024]{2,1,0:T(8,128)(2,1)} %broadcast_in_dim.30), calls=%async_computation.2 | async-start | bytes 2097152 | tf_op jit(solution)/shard_map/all_to_all | solution.py:20
  69.1 3.9 %collective-permute-start = (bf16[256,1024]{1,0:T(8,128)(2,1)S(1)}, bf16[256,1024]{1,0:T(8,128)(2,1)}, u32[]{:S(2)}, u32[]{:S(2)}) collective-permute-start(bf16[256,1024]{1,0:T(8,128)(2,1)S(1)} %bitcast.112), channel_id=1, source_target_pairs={{0,16},{16,0},{1,17},{17,1},{2,18},{18,2},{3,19},{19,3},{4,20},{20... | collective-permute-start | bytes 1572872 | tf_op jit(solution)/shard_map/ppermute | solution.py:28
  80.6 5.2 %collective-permute-start.1 = (f32[256,1024]{1,0:T(8,128)S(1)}, f32[256,1024]{1,0:T(8,128)S(1)}, u32[]{:S(2)}, u32[]{:S(2)}) collective-permute-start(f32[256,1024]{1,0:T(8,128)S(1)} %fusion.57), channel_id=1, source_target_pairs={{0,16},{16,0},{1,17},{17,1},{2,18},{18,2},{3,19},{19,3},{4,20},{20... | collective-permute-start | bytes 3145736 | tf_op jit(solution)/shard_map/ppermute | solution.py:28

commit v7 on v3

v7 whole, which is shorter than its diff:
```python
import jax
import jax.numpy as jnp
from jax import lax
from jax.sharding import Mesh, PartitionSpec as P

BLK = ("x", "y", "c")
AXES = BLK + ("zl", "zh")
COLUMN = ("zh", "zl")
F32 = jnp.float32
HALF = jnp.float16


def spread(value, axis):
    count = lax.axis_size(axis)
    copies = jnp.broadcast_to(value[None], (count,) + value.shape)
    return lax.all_to_all(copies, axis, 0, 0, tiled=True)


def summed(parts, axis):
    count = lax.axis_size(axis)
    parts = parts.reshape((count, -1) + parts.shape[1:])
    return jnp.sum(lax.all_to_all(parts, axis, 0, 0, tiled=True).astype(F32), axis=0)


def swapped(value):
    return lax.ppermute(value, "c", [(0, 1), (1, 0)])


def shifted(value, axis, steps):
    count = lax.axis_size(axis)
    return lax.ppermute(value, axis, [(k, (k + steps) % count) for k in range(count)])


def exponent(value):
    return jnp.clip(jnp.floor(jnp.log2(jnp.maximum(value, 1e-30))), -100.0, 126.0)


def with_exponents(rows, powers):
    count, width = rows.shape[-2:]
    lead = [(0, 0)] * (powers.ndim - 1)
    powers = jnp.pad(powers[..., None, :], lead + [(0, 7), (0, width - count)])
    powers = jnp.broadcast_to(powers, rows.shape[:-2] + (8, width))
    return jnp.concatenate([rows.astype(HALF), powers.astype(HALF)], axis=-2)


def without_exponents(pieces, count):
    return pieces[..., :count, :].astype(F32), pieces[..., count, :count].astype(F32)


def normalize(embed):
    norm = jnp.sqrt(jnp.sum(embed * embed, axis=1, keepdims=True) + 1e-06)
    return embed / norm, norm


def projected(grad, unit):
    return grad - unit * jnp.sum(unit * grad, axis=1, keepdims=True)


def shards(image_features, text_features, image_head, text_head, positive, log_scale, bias):
    rows = image_features.shape[0]
    planes = lax.axis_size(COLUMN)
    lanes = lax.axis_size("zl")
    images, texts = rows // 8, rows // 2
    x, y, c = (lax.axis_index(name) for name in BLK)
    zh = lax.axis_index("zh")
    image_part, text_part = lax.axis_index("zl"), zh
    scale = jnp.exp(log_scale[0])
    offset = bias[0]

    text_rows = lax.dynamic_slice_in_dim(text_features, zh * texts, texts)
    image_cols = jnp.dot(image_features, image_head, preferred_element_type=F32)
    text_cols = jnp.dot(text_rows, text_head, preferred_element_type=F32)
    width = image_cols.shape[-1]

    def scaled(cols):
        powers = exponent(jnp.max(jnp.abs(cols), axis=-1))
        cols = (cols * jnp.exp2(-powers)[:, None]).reshape(-1, texts, width)
        return cols, powers.reshape(-1, texts)

    image_cols, image_powers = scaled(image_cols)
    text_cols, text_powers = scaled(text_cols)
    pieces = jnp.concatenate(
        [
            with_exponents(image_cols.reshape(8, images, width), image_powers.reshape(8, images)),
            jnp.broadcast_to(with_exponents(text_cols, text_powers), (8, texts + 8, width)),
        ],
        axis=1,
    )
    pieces = lax.all_to_all(pieces, "zl", 0, 0, tiled=True)

    def whole(part, count):
        part, powers = without_exponents(part, count)
        part = part * jnp.exp2(powers)[..., None]
        return part.transpose(1, 0, 2).reshape(count, lanes * width)

    image_unit, image_norm = normalize(whole(pieces[:, : images + 8], images))
    text_unit, text_norm = normalize(whole(pieces[:, images + 8 :], texts))

    text_b = text_unit.astype(jnp.bfloat16)
    image_own = spread(image_unit.astype(jnp.bfloat16), "y").reshape(8 * images, -1)
    text_b = jnp.concatenate([text_b] + [shifted(text_b, "x", k) for k in range(1, 4)])
    image_own, text_b = lax.optimization_barrier((image_own, text_b))
    image_far = swapped(image_own)

    def places(core):
        keys = positive.reshape(-1, 2 * rows)
        keys = lax.dynamic_slice(keys, (x * 8, core * rows + image_part * images), (8, images))
        keys = keys.reshape(1, 8 * images)
        block, row = keys // rows, keys % rows
        place = ((x - block // 16) & 3) * texts + row % texts
        inside = (block // 2 % 8 == y) & (block % 2 == c) & (row // texts == text_part)
        return jnp.where(inside, place, -1)

    def weights(image_b, place):
        logits = scale * jnp.einsum("ce,re->cr", text_b, image_b, preferred_element_type=F32)
        logits = logits + offset
        index = lax.broadcasted_iota(jnp.int32, logits.shape, 0)
        sign = jnp.where(place == index, 1.0, -1.0)
        return (-sign * jax.nn.sigmoid(-sign * logits) * scale).astype(jnp.bfloat16)

    def to_texts(weight, image_b):
        return jnp.dot(weight, image_b, preferred_element_type=F32)

    def to_images(weight):
        return jnp.einsum("cr,ce->re", weight, text_b, preferred_element_type=F32)

    weight_own = weights(image_own, places(c))
    own_grad = to_images(weight_own)
    image_far, weight_own, own_grad = lax.optimization_barrier((image_far, weight_own, own_grad))
    weight_far = weights(image_far, places(1 - c))
    image_grad = (own_grad + swapped(to_images(weight_far))).astype(HALF)
    text_grad = to_texts(weight_far, image_far) + to_texts(weight_own, image_own)

    text_parts = text_grad.astype(HALF).reshape(4, texts, -1)
    text_grad = text_parts[0].astype(F32)
    for k in range(1, 4):
        text_grad = text_grad + shifted(text_parts[k], "x", -k).astype(F32)
    image_grad = summed(image_grad, "y")

    def outgoing(grad, unit, norm):
        powers = exponent(norm) - 3.0
        piece = projected(grad, unit) * (jnp.exp2(powers) / norm)
        piece = piece.reshape(-1, lanes, width).transpose(1, 0, 2)
        powers = powers.reshape(1, -1)
        short = texts - powers.shape[1]
        piece = jnp.pad(piece, ((0, 0), (0, short), (0, 0)))
        return with_exponents(piece, jnp.pad(powers, ((0, 0), (0, short))))

    both = jnp.concatenate(
        [outgoing(image_grad, image_unit, image_norm), outgoing(text_grad, text_unit, text_norm)]
    )
    both = lax.all_to_all(both, COLUMN, 0, 0, tiled=True)
    both, powers = without_exponents(both.reshape(2, 8, texts + 8, width), texts)
    image_sum = jnp.sum(both[:, :, :images], axis=0) / jnp.exp2(powers[0, :, :images])[..., None]
    text_sum = jnp.sum(both, axis=1) / jnp.exp2(powers[:, 0])[..., None]
    image_sum, text_sum = image_sum.reshape(1, rows, width), text_sum.reshape(1, rows, width)
    return jnp.where(zh == 0, image_sum, text_sum)


def solution(mesh):
    fine = Mesh(mesh.devices.reshape(4, 8, 2, 8, 2), AXES)
    placed = (P(BLK, None), P(BLK, None), P(None, "zl"), P(None, "zl"), P(), P(), P())
    return jax.shard_map(
        shards, mesh=fine, in_specs=placed, out_specs=P("zh", BLK, "zl"), check_vma=False
    )
```

time: 150 us -> 156 us (1.040)
  blocking collectives: 37.9 us -> 0 us
  waiting for transfers between devices: 41 us -> 69.2 us
  starting transfers between devices: 46.7 us -> 65.6 us
  other arithmetic: 3.79 us -> 8.13 us
  matrix products: 9.77 us -> 5.73 us
  local copies, waits for them, and re-layouts: 8.21 us -> 4.68 us
    all_to_all x1 -> x0, blocking collectives: 37.9 us -> none  [shards(): pieces = lax.all_to_all(pieces, COLUMN, 0, 0, tiled=True)]
    all_to_all x0 -> x1, waiting for transfers between devices: none -> 21.5 us  [shards(): pieces = lax.all_to_all(pieces, 'zl', 0, 0, tiled=True)]
    all_to_all x0 -> x1, starting transfers between devices: none -> 15.7 us  [shards(): pieces = lax.all_to_all(pieces, 'zl', 0, 0, tiled=True)]
    all_to_all x1, waiting for transfers between devices: 19.8 us -> 30 us  [shards(): both = lax.all_to_all(both, COLUMN, 0, 0, tiled=True)]
    all_to_all x1, waiting for transfers between devices: 9.87 us -> 0.01 us  [summed(): lax.all_to_all(parts, axis, 0, 0, tiled=True).astype(F32)]
    ppermute x6, waiting for transfers between devices: 9.54 us -> 15.2 us  [shifted(): lax.ppermute(value, axis, [(k, (k + steps) % count) for k in range(count)])]
    ppermute x2, waiting for transfers between devices: 0.01 us -> 2.43 us  [swapped(): return lax.ppermute(value, 'c', [(0, 1), (1, 0)])]
    all_to_all x1, starting transfers between devices: 10.2 us -> 12.6 us  [shards(): both = lax.all_to_all(both, COLUMN, 0, 0, tiled=True)]
  transfers between devices with their start and end apart: 11 -> 12, of which waited for: 8 -> 9; matrix products, arithmetic and copies ran while one was open for 6% -> 3% of each run, Pallas kernels for 0% -> 0%
where the time goes in v7:
time: 156 us; the launch traced here: 155 us
  waiting for transfers between devices  69.2 us (44%)
  starting transfers between devices  65.6 us (42%)
  other arithmetic  8.13 us (5%)
  matrix products  5.73 us (4%)
  local copies, waits for them, and re-layouts  4.68 us (3%)
  between operations  1.71 us (1%)
    all_to_all x1, waiting for transfers between devices, shards(): both = lax.all_to_all(both, COLUMN, 0, 0, tiled=True)  30 us
    all_to_all x1, waiting for transfers between devices, shards(): pieces = lax.all_to_all(pieces, 'zl', 0, 0, tiled=True)  21.5 us
    ppermute x6, starting transfers between devices, shifted(): lax.ppermute(value, axis, [(k, (k + steps) % count) for k in range(count)])  19 us
    all_to_all x1, starting transfers between devices, shards(): pieces = lax.all_to_all(pieces, 'zl', 0, 0, tiled=True)  15.7 us
    ppermute x6, waiting for transfers between devices, shifted(): lax.ppermute(value, axis, [(k, (k + steps) % count) for k in range(count)])  15.2 us
    all_to_all x1, starting transfers between devices, shards(): both = lax.all_to_all(both, COLUMN, 0, 0, tiled=True)  12.6 us
    all_to_all x1, starting transfers between devices, summed(): lax.all_to_all(parts, axis, 0, 0, tiled=True).astype(F32)  7.21 us
    all_to_all x1, starting transfers between devices, spread(): return lax.all_to_all(copies, axis, 0, 0, tiled=True)  7.1 us
  transfers between devices with their start and end apart: 12, of which 9 were waited for; matrix products, arithmetic and copies ran while one was open for 3% of the time, Pallas kernels for 0%

profile of v7, /device:TPU:6, one launch (start us, length us, event | category | flops | bytes accessed | tf_op | source)
XLA Modules:
  0.0 155.1 jit_solution(17176739980073261260)
XLA Ops:
  0.0 1.1 copy-done
  1.1 1.4 abs_reduce_fusion
  2.6 0.1 reshape.934
  2.7 1.3 abs_reduce_fusion.1
  4.0 0.1 fusion.42
  4.1 0.1 multiply_convert_fusion.1
  4.3 0.8 fusion.28
  5.1 15.7 %all-to-all-start = ((f16[8,176,128]{2,1,0:T(8,128)(2,1)}), f16[8,176,128]{2,1,0:T(8,128)(2,1)S(1)}, u32[]{:S(2)}, u32[]{:S(2)}) async-start(f16[8,176,128]{2,1,0:T(8,128)(2,1)} %fusion.28), calls=%async_computation | async-start | bytes 720896 | tf_op jit(solution)/shard_map/all_to_all | solution.py:89
  20.9 0.1 fusion.57
  21.0 0.1 reshape.903
  21.0 21.5 %all-to-all-done = f16[8,176,128]{2,1,0:T(8,128)(2,1)S(1)} async-done(((f16[8,176,128]{2,1,0:T(8,128)(2,1)}), f16[8,176,128]{2,1,0:T(8,128)(2,1)S(1)}, u32[]{:S(2)}, u32[]{:S(2)}) %all-to-all-start) | async-done | bytes 360480 | tf_op jit(solution)/shard_map/all_to_all | solution.py:89
  42.6 0.1 copy.16
  42.7 0.1 convert_multiply_fusion.1
  42.8 0.5 fusion.38
  43.3 0.1 fusion.36
  43.4 0.8 broadcast_in_dim.28
  44.2 7.1 %all-to-all-start.1 = ((bf16[8,32,1024]{2,1,0:T(8,128)(2,1)}), bf16[8,32,1024]{2,1,0:T(8,128)(2,1)S(1)}, u32[]{:S(2)}, u32[]{:S(2)}) async-start(bf16[8,32,1024]{2,1,0:T(8,128)(2,1)} %broadcast_in_dim.28), calls=%async_computation.1 | async-start | bytes 1048576 | tf_op jit(solution)/shard_map/all_to_all | solution.py:16
  51.4 0.3 fusion.25
  51.7 0.2 fusion.55
  51.9 2.7 %collective-permute-start.2 = (bf16[128,1024]{1,0:T(8,128)(2,1)S(1)}, bf16[128,1024]{1,0:T(8,128)(2,1)S(1)}, u32[]{:S(2)}, u32[]{:S(2)}) collective-permute-start(bf16[128,1024]{1,0:T(8,128)(2,1)S(1)} %fusion.55), channel_id=1, source_target_pairs={{0,768},{256,0},{512,256},{768,512},{1,769},{257,1},{513,257},{769... | collective-permute-start | bytes 786440 | tf_op jit(solution)/shard_map/ppermute | solution.py:31
  54.7 3.0 %collective-permute-start.1 = (bf16[128,1024]{1,0:T(8,128)(2,1)S(1)}, bf16[128,1024]{1,0:T(8,128)(2,1)S(1)}, u32[]{:S(2)}, u32[]{:S(2)}) collective-permute-start(bf16[128,1024]{1,0:T(8,128)(2,1)S(1)} %fusion.55), channel_id=1, source_target_pairs={{0,512},{256,768},{512,0},{768,256},{1,513},{257,769},{513,1},{769... | collective-permute-start | bytes 786440 | tf_op jit(solution)/shard_map/ppermute | solution.py:31
  57.7 4.0 %collective-permute-start = (bf16[128,1024]{1,0:T(8,128)(2,1)S(1)}, bf16[128,1024]{1,0:T(8,128)(2,1)}, u32[]{:S(2)}, u32[]{:S(2)}) collective-permute-start(bf16[128,1024]{1,0:T(8,128)(2,1)S(1)} %fusion.55), channel_id=1, source_target_pairs={{0,256},{256,512},{512,768},{768,0},{1,257},{257,513},{513,769},{7... | collective-permute-start | bytes 786440 | tf_op jit(solution)/shard_map/ppermute | solution.py:31
  63.1 0.1 reshape.904
  63.2 0.0 collective-permute-done.2
  63.2 1.2 collective-permute-done.1
  64.4 0.7 copy-done.1
  65.1 1.9 %collective-permute-done = bf16[128,1024]{1,0:T(8,128)(2,1)} collective-permute-done((bf16[128,1024]{1,0:T(8,128)(2,1)S(1)}, bf16[128,1024]{1,0:T(8,128)(2,1)}, u32[]{:S(2)}, u32[]{:S(2)}) %collective-permute-start) | collective-permute-done | bytes 262176 | tf_op jit(solution)/shard_map/ppermute | solution.py:31
  67.1 1.1 pad_maximum_fusion
  68.2 0.0 all-to-all-done.1
  68.2 1.9 %collective-permute-start.3 = (bf16[256,1024]{1,0:T(8,128)(2,1)S(1)}, bf16[256,1024]{1,0:T(8,128)(2,1)S(1)}, u32[]{:S(2)}, u32[]{:S(2)}) collective-permute-start(bf16[256,1024]{1,0:T(8,128)(2,1)S(1)} %bitcast.102), channel_id=1, source_target_pairs={{0,16},{16,0},{1,17},{17,1},{2,18},{18,2},{3,19},{19,3},{4,20},{20... | collective-permute-start | bytes 1572872 | tf_op jit(solution)/shard_map/ppermute | solution.py:26
  70.1 0.6 fusion.16
  70.7 0.5 fusion.58
  71.2 0.8 collective-permute-done.3
  72.0 0.6 fusion.17
  72.6 0.5 fusion.59
  73.0 2.0 %collective-permute-start.4 = (f32[256,1024]{1,0:T(8,128)S(1)}, f32[256,1024]{1,0:T(8,128)S(1)}, u32[]{:S(2)}, u32[]{:S(2)}) collective-permute-start(f32[256,1024]{1,0:T(8,128)S(1)} %fusion.59), channel_id=1, source_target_pairs={{0,16},{16,0},{1,17},{17,1},{2,18},{18,2},{3,19},{19,3},{4,20},{20... | collective-permute-start | bytes 3145736 | tf_op jit(solution)/shard_map/ppermute | solution.py:26
  75.1 0.4 fusion.60
  75.5 0.4 add_convert_fusion
  76.0 1.6 %collective-permute-done.4 = f32[256,1024]{1,0:T(8,128)S(1)} collective-permute-done((f32[256,1024]{1,0:T(8,128)S(1)}, f32[256,1024]{1,0:T(8,128)S(1)}, u32[]{:S(2)}, u32[]{:S(2)}) %collective-permute-start.4) | collective-permute-done | bytes 1048608 | tf_op jit(solution)/shard_map/ppermute | solution.py:26
  77.6 1.0 add_convert_fusion.1
  78.6 7.2 %all-to-all-start.2 = ((f16[8,32,1024]{2,1,0:T(8,128)(2,1)}), f16[8,32,1024]{2,1,0:T(8,128)(2,1)S(1)}, u32[]{:S(2)}, u32[]{:S(2)}) async-start(f16[8,32,1024]{2,1,0:T(8,128)(2,1)} %bitcast.11), calls=%async_computation.2 | async-start | bytes 1048576 | tf_op jit(solution)/shard_map/all_to_all | solution.py:22
  85.8 0.1 fusion.56
  86.0 4.6 %collective-permute-start.7 = (f16[128,1024]{1,0:T(8,128)(2,1)S(1)}, f16[128,1024]{1,0:T(8,128)(2,1)S(1)}, u32[]{:S(2)}, u32[]{:S(2)}) collective-permute-start(f16[128,1024]{1,0:T(8,128)(2,1)S(1)} %get-tuple-element.16), channel_id=1, source_target_pairs={{0,256},{256,512},{512,768},{768,0},{1,257},{257,513},{513,769},{7... | collective-permute-start | bytes 786440 | tf_op jit(solution)/shard_map/ppermute | solution.py:31
  90.5 2.4 %collective-permute-start.6 = (f16[128,1024]{1,0:T(8,128)(2,1)S(1)}, f16[128,1024]{1,0:T(8,128)(2,1)S(1)}, u32[]{:S(2)}, u32[]{:S(2)}) collective-permute-start(f16[128,1024]{1,0:T(8,128)(2,1)S(1)} %get-tuple-element.17), channel_id=1, source_target_pairs={{0,512},{256,768},{512,0},{768,256},{1,513},{257,769},{513,1},{769... | collective-permute-start | bytes 786440 | tf_op jit(solution)/shard_map/ppermute | solution.py:31
  93.0 2.2 %collective-permute-start.5 = (f16[128,1024]{1,0:T(8,128)(2,1)S(1)}, f16[128,1024]{1,0:T(8,128)(2,1)S(1)}, u32[]{:S(2)}, u32[]{:S(2)}) collective-permute-start(f16[128,1024]{1,0:T(8,128)(2,1)S(1)} %get-tuple-element.15), channel_id=1, source_target_pairs={{0,768},{256,0},{512,256},{768,512},{1,769},{257,1},{513,257},{769... | collective-permute-start | bytes 786440 | tf_op jit(solution)/shard_map/ppermute | solution.py:31
  95.3 6.5 %collective-permute-done.7 = f16[128,1024]{1,0:T(8,128)(2,1)S(1)} collective-permute-done((f16[128,1024]{1,0:T(8,128)(2,1)S(1)}, f16[128,1024]{1,0:T(8,128)(2,1)S(1)}, u32[]{:S(2)}, u32[]{:S(2)}) %collective-permute-start.7) | collective-permute-done | bytes 262176 | tf_op jit(solution)/shard_map/ppermute | solution.py:31
  101.8 1.4 collective-permute-done.6
  103.2 4.1 %collective-permute-done.5 = f16[128,1024]{1,0:T(8,128)(2,1)S(1)} collective-permute-done((f16[128,1024]{1,0:T(8,128)(2,1)S(1)}, f16[128,1024]{1,0:T(8,128)(2,1)S(1)}, u32[]{:S(2)}, u32[]{:S(2)}) %collective-permute-start.5) | collective-permute-done | bytes 262176 | tf_op jit(solution)/shard_map/ppermute | solution.py:31
  107.4 0.4 multiply_reduce_fusion
  107.8 0.4 fusion.29
  108.2 0.1 copy.28
  108.2 0.0 all-to-all-done.2
  108.3 0.1 convert_reduce_fusion
  108.4 0.6 fusion.33
  108.9 0.2 fusion.35
  109.2 0.2 fusion.24
  109.4 1.0 copy.18
  110.3 12.6 %all-to-all-start.3 = ((f16[16,136,128]{2,1,0:T(8,128)(2,1)}), f16[16,136,128]{2,1,0:T(8,128)(2,1)S(1)}, u32[]{:S(2)}, u32[]{:S(2)}) async-start(f16[16,136,128]{2,1,0:T(8,128)(2,1)} %copy.18), calls=%async_computation.3 | async-start | bytes 1114112 | tf_op jit(solution)/shard_map/all_to_all | solution.py:152
  122.9 30.0 %all-to-all-done.3 = f16[16,136,128]{2,1,0:T(8,128)(2,1)S(1)} async-done(((f16[16,136,128]{2,1,0:T(8,128)(2,1)}), f16[16,136,128]{2,1,0:T(8,128)(2,1)S(1)}, u32[]{:S(2)}, u32[]{:S(2)}) %all-to-all-start.3) | async-done | bytes 557088 | tf_op jit(solution)/shard_map/all_to_all | solution.py:152
  153.0 0.1 slice.70
  153.1 0.7 fusion.32
  153.8 0.3 copy_convert_fusion
  154.1 0.1 exp2.171
  154.3 0.8 fusion.37
  (28 shorter events, 0.4 us)
Async XLA Ops:
  0.0 1.1 copy-start
  0.0 20.8 %copy-start.2 = (s32[16384]{0:T(1024)S(1)}, s32[16384]{0:T(1024)}, u32[]{:S(2)}) copy-start(s32[16384]{0:T(1024)} %param.11) | copy-start | bytes 196612
  5.1 37.4 %all-to-all-start = ((f16[8,176,128]{2,1,0:T(8,128)(2,1)}), f16[8,176,128]{2,1,0:T(8,128)(2,1)S(1)}, u32[]{:S(2)}, u32[]{:S(2)}) async-start(f16[8,176,128]{2,1,0:T(8,128)(2,1)} %fusion.28), calls=%async_computation | async-start | bytes 720896 | tf_op jit(solution)/shard_map/all_to_all | solution.py:89
  44.2 23.9 %all-to-all-start.1 = ((bf16[8,32,1024]{2,1,0:T(8,128)(2,1)}), bf16[8,32,1024]{2,1,0:T(8,128)(2,1)S(1)}, u32[]{:S(2)}, u32[]{:S(2)}) async-start(bf16[8,32,1024]{2,1,0:T(8,128)(2,1)} %broadcast_in_dim.28), calls=%async_computation.1 | async-start | bytes 1048576 | tf_op jit(solution)/shard_map/all_to_all | solution.py:16
  51.9 11.3 %collective-permute-start.2 = (bf16[128,1024]{1,0:T(8,128)(2,1)S(1)}, bf16[128,1024]{1,0:T(8,128)(2,1)S(1)}, u32[]{:S(2)}, u32[]{:S(2)}) collective-permute-start(bf16[128,1024]{1,0:T(8,128)(2,1)S(1)} %fusion.55), channel_id=1, source_target_pairs={{0,768},{256,0},{512,256},{768,512},{1,769},{257,1},{513,257},{769... | collective-permute-start | bytes 786440 | tf_op jit(solution)/shard_map/ppermute | solution.py:31
  54.7 9.8 %collective-permute-start.1 = (bf16[128,1024]{1,0:T(8,128)(2,1)S(1)}, bf16[128,1024]{1,0:T(8,128)(2,1)S(1)}, u32[]{:S(2)}, u32[]{:S(2)}) collective-permute-start(bf16[128,1024]{1,0:T(8,128)(2,1)S(1)} %fusion.55), channel_id=1, source_target_pairs={{0,512},{256,768},{512,0},{768,256},{1,513},{257,769},{513,1},{769... | collective-permute-start | bytes 786440 | tf_op jit(solution)/shard_map/ppermute | solution.py:31
  57.7 9.4 %collective-permute-start = (bf16[128,1024]{1,0:T(8,128)(2,1)S(1)}, bf16[128,1024]{1,0:T(8,128)(2,1)}, u32[]{:S(2)}, u32[]{:S(2)}) collective-permute-start(bf16[128,1024]{1,0:T(8,128)(2,1)S(1)} %fusion.55), channel_id=1, source_target_pairs={{0,256},{256,512},{512,768},{768,0},{1,257},{257,513},{513,769},{7... | collective-permute-start | bytes 786440 | tf_op jit(solution)/shard_map/ppermute | solution.py:31
  64.4 0.7 copy-start.1
  68.2 3.8 %collective-permute-start.3 = (bf16[256,1024]{1,0:T(8,128)(2,1)S(1)}, bf16[256,1024]{1,0:T(8,128)(2,1)S(1)}, u32[]{:S(2)}, u32[]{:S(2)}) collective-permute-start(bf16[256,1024]{1,0:T(8,128)(2,1)S(1)} %bitcast.102), channel_id=1, source_target_pairs={{0,16},{16,0},{1,17},{17,1},{2,18},{18,2},{3,19},{19,3},{4,20},{20... | collective-permute-start | bytes 1572872 | tf_op jit(solution)/shard_map/ppermute | solution.py:26
  73.0 4.6 %collective-permute-start.4 = (f32[256,1024]{1,0:T(8,128)S(1)}, f32[256,1024]{1,0:T(8,128)S(1)}, u32[]{:S(2)}, u32[]{:S(2)}) collective-permute-start(f32[256,1024]{1,0:T(8,128)S(1)} %fusion.59), channel_id=1, source_target_pairs={{0,16},{16,0},{1,17},{17,1},{2,18},{18,2},{3,19},{19,3},{4,20},{20... | collective-permute-start | bytes 3145736 | tf_op jit(solution)/shard_map/ppermute | solution.py:26
  78.6 29.6 %all-to-all-start.2 = ((f16[8,32,1024]{2,1,0:T(8,128)(2,1)}), f16[8,32,1024]{2,1,0:T(8,128)(2,1)S(1)}, u32[]{:S(2)}, u32[]{:S(2)}) async-start(f16[8,32,1024]{2,1,0:T(8,128)(2,1)} %bitcast.11), calls=%async_computation.2 | async-start | bytes 1048576 | tf_op jit(solution)/shard_map/all_to_all | solution.py:22
  86.0 15.8 %collective-permute-start.7 = (f16[128,1024]{1,0:T(8,128)(2,1)S(1)}, f16[128,1024]{1,0:T(8,128)(2,1)S(1)}, u32[]{:S(2)}, u32[]{:S(2)}) collective-permute-start(f16[128,1024]{1,0:T(8,128)(2,1)S(1)} %get-tuple-element.16), channel_id=1, source_target_pairs={{0,256},{256,512},{512,768},{768,0},{1,257},{257,513},{513,769},{7... | collective-permute-start | bytes 786440 | tf_op jit(solution)/shard_map/ppermute | solution.py:31
  90.5 12.7 %collective-permute-start.6 = (f16[128,1024]{1,0:T(8,128)(2,1)S(1)}, f16[128,1024]{1,0:T(8,128)(2,1)S(1)}, u32[]{:S(2)}, u32[]{:S(2)}) collective-permute-start(f16[128,1024]{1,0:T(8,128)(2,1)S(1)} %get-tuple-element.17), channel_id=1, source_target_pairs={{0,512},{256,768},{512,0},{768,256},{1,513},{257,769},{513,1},{769... | collective-permute-start | bytes 786440 | tf_op jit(solution)/shard_map/ppermute | solution.py:31
  93.0 14.4 %collective-permute-start.5 = (f16[128,1024]{1,0:T(8,128)(2,1)S(1)}, f16[128,1024]{1,0:T(8,128)(2,1)S(1)}, u32[]{:S(2)}, u32[]{:S(2)}) collective-permute-start(f16[128,1024]{1,0:T(8,128)(2,1)S(1)} %get-tuple-element.15), channel_id=1, source_target_pairs={{0,768},{256,0},{512,256},{768,512},{1,769},{257,1},{513,257},{769... | collective-permute-start | bytes 786440 | tf_op jit(solution)/shard_map/ppermute | solution.py:31
  110.3 42.6 %all-to-all-start.3 = ((f16[16,136,128]{2,1,0:T(8,128)(2,1)}), f16[16,136,128]{2,1,0:T(8,128)(2,1)S(1)}, u32[]{:S(2)}, u32[]{:S(2)}) async-start(f16[16,136,128]{2,1,0:T(8,128)(2,1)} %copy.18), calls=%async_computation.3 | async-start | bytes 1114112 | tf_op jit(solution)/shard_map/all_to_all | solution.py:152

commit v8 on v7

v8 whole, which is shorter than its diff:
```python
import jax
import jax.numpy as jnp
from jax import lax
from jax.sharding import Mesh, PartitionSpec as P

BLK = ("x", "y", "c")
AXES = BLK + ("zl", "zh")
F32 = jnp.float32
HALF = jnp.float16


def spread(value, axis):
    count = lax.axis_size(axis)
    copies = jnp.broadcast_to(value[None], (count,) + value.shape)
    return lax.all_to_all(copies, axis, 0, 0, tiled=True)


def summed(parts, axis):
    count = lax.axis_size(axis)
    parts = parts.reshape((count, -1) + parts.shape[1:])
    return jnp.sum(lax.all_to_all(parts, axis, 0, 0, tiled=True).astype(F32), axis=0)


def swapped(value):
    return lax.ppermute(value, "c", [(0, 1), (1, 0)])


def shifted(value, axis, steps):
    count = lax.axis_size(axis)
    return lax.ppermute(value, axis, [(k, (k + steps) % count) for k in range(count)])


def exponent(value):
    return jnp.clip(jnp.floor(jnp.log2(jnp.maximum(value, 1e-30))), -100.0, 126.0)


def with_exponents(rows, powers):
    count, width = rows.shape[-2:]
    lead = [(0, 0)] * (powers.ndim - 1)
    powers = jnp.pad(powers[..., None, :], lead + [(0, 7), (0, width - count)])
    powers = jnp.broadcast_to(powers, rows.shape[:-2] + (8, width))
    return jnp.concatenate([rows.astype(HALF), powers.astype(HALF)], axis=-2)


def without_exponents(pieces, count):
    return pieces[..., :count, :].astype(F32), pieces[..., count, :count].astype(F32)


def normalize(embed):
    norm = jnp.sqrt(jnp.sum(embed * embed, axis=1, keepdims=True) + 1e-06)
    return embed / norm, norm


def projected(grad, unit):
    return grad - unit * jnp.sum(unit * grad, axis=1, keepdims=True)


def shards(image_features, text_features, image_head, text_head, positive, log_scale, bias):
    rows = image_features.shape[0]
    lanes = lax.axis_size("zl")
    owns, others = rows // 4, rows // 2
    x, y, c = (lax.axis_index(name) for name in BLK)
    is_image = lax.axis_index("zh") == 0
    plane = lax.axis_index("zl")
    own_part, other_part = plane // 2, plane % 2
    scale = jnp.exp(log_scale[0])
    offset = bias[0]

    image_cols = jnp.dot(image_features, image_head, preferred_element_type=F32)
    text_cols = jnp.dot(text_features, text_head, preferred_element_type=F32)
    width = image_cols.shape[-1]

    def scaled(cols):
        powers = exponent(jnp.max(jnp.abs(cols), axis=-1))
        return (cols * jnp.exp2(-powers)[:, None]).astype(HALF), powers.astype(HALF)

    image_cols, image_powers = scaled(image_cols)
    text_cols, text_powers = scaled(text_cols)

    def parted(image, text, powers_image, powers_text, count):
        cols = jnp.where(is_image, image, text).reshape(-1, count, width)
        powers = jnp.where(is_image, powers_image, powers_text).reshape(-1, count)
        return with_exponents(cols, powers)

    own = parted(image_cols, text_cols, image_powers, text_powers, owns)
    other = parted(text_cols, image_cols, text_powers, image_powers, others)
    own = jnp.broadcast_to(own[:, None], (4, 2) + own.shape[1:])
    other = jnp.broadcast_to(other[None], (4, 2) + other.shape[1:])
    pieces = jnp.concatenate([own, other], axis=2).reshape(lanes, -1, width)
    pieces = lax.all_to_all(pieces, "zl", 0, 0, tiled=True)

    def whole(part, count):
        part, powers = without_exponents(part, count)
        part = part * jnp.exp2(powers)[..., None]
        return part.transpose(1, 0, 2).reshape(count, lanes * width)

    own_unit, own_norm = normalize(whole(pieces[:, : owns + 8], owns))
    other_unit, _ = normalize(whole(pieces[:, owns + 8 :], others))

    own_b = spread(own_unit.astype(jnp.bfloat16), "y").reshape(8 * owns, -1)
    other_b = other_unit.astype(jnp.bfloat16)
    near_b = jnp.concatenate([other_b] + [shifted(other_b, "x", k) for k in range(1, 4)])
    far_b = swapped(near_b)

    table = positive.reshape(4, 8, 2 * rows)

    def keys(start, size, lane, count, image):
        found = lax.dynamic_slice(table, start + (lane,), size + (count,)).reshape(-1, count)
        block = start[0] + jnp.arange(size[0], dtype=jnp.int32)[:, None]
        block = block * 8 + start[1] + jnp.arange(size[1], dtype=jnp.int32)[None]
        index = block.reshape(-1, 1) * 2 * rows + lane + jnp.arange(count, dtype=jnp.int32)
        return jnp.where(image, found, index)

    own_keys = keys((x, 0), (1, 8), c * rows + own_part * owns, owns, is_image).reshape(1, -1)

    def other_keys(core):
        found = keys((0, y), (4, 1), core * rows + other_part * others, others, ~is_image)[::-1]
        found = jnp.concatenate([found, found])
        return lax.dynamic_slice_in_dim(found, 3 - x, 4).reshape(-1, 1)

    def gradient(b, key):
        logits = scale * jnp.einsum("ce,re->cr", b, own_b, preferred_element_type=F32) + offset
        sign = jnp.where(own_keys == key, 1.0, -1.0)
        weight = (-sign * jax.nn.sigmoid(-sign * logits) * scale).astype(jnp.bfloat16)
        return jnp.einsum("cr,ce->re", weight, b, preferred_element_type=F32)

    near_keys, far_keys = other_keys(c), other_keys(1 - c)
    grad = gradient(near_b, near_keys)
    grad, far_b, far_keys = lax.optimization_barrier((grad, far_b, far_keys))
    grad = summed((grad + gradient(far_b, far_keys)).astype(HALF), "y")

    powers = exponent(own_norm) - 3.0
    grad = projected(grad, own_unit) * (jnp.exp2(powers) / own_norm)
    grad = grad.reshape(owns, lanes, width).transpose(1, 0, 2)
    pieces = with_exponents(grad, powers.reshape(1, owns))
    pieces = lax.all_to_all(pieces, "zl", 0, 0, tiled=True)
    grad, powers = without_exponents(pieces.reshape(4, 2, owns + 8, width), owns)
    grad = jnp.sum(grad, axis=1) / jnp.exp2(powers[:, 0])[..., None]
    return grad.reshape(1, rows, width)


def solution(mesh):
    fine = Mesh(mesh.devices.reshape(4, 8, 2, 8, 2), AXES)
    placed = (P(BLK, None), P(BLK, None), P(None, "zl"), P(None, "zl"), P(), P(), P())
    return jax.shard_map(
        shards, mesh=fine, in_specs=placed, out_specs=P("zh", BLK, "zl"), check_vma=False
    )
```

time: 156 us -> 149 us (0.955)
  starting transfers between devices: 65.6 us -> 39.4 us
  blocking collectives: 0 us -> 19.7 us
  waiting for transfers between devices: 69.2 us -> 62.2 us
  matrix products: 5.73 us -> 11.2 us
  other arithmetic: 8.13 us -> 9.92 us
    all_to_all x1 -> x0, waiting for transfers between devices: 30 us -> none  [shards(): both = lax.all_to_all(both, COLUMN, 0, 0, tiled=True)]
    all_to_all x1, waiting for transfers between devices: 0.01 us -> 29.5 us  [summed(): lax.all_to_all(parts, axis, 0, 0, tiled=True).astype(F32)]
    all_to_all x0 -> x1, blocking collectives: none -> 19.7 us  [shards(): pieces = lax.all_to_all(pieces, 'zl', 0, 0, tiled=True)]
    all_to_all x1 -> x0, starting transfers between devices: 12.6 us -> none  [shards(): both = lax.all_to_all(both, COLUMN, 0, 0, tiled=True)]
    ppermute x6 -> x3, starting transfers between devices: 19 us -> 8.63 us  [shifted(): lax.ppermute(value, axis, [(k, (k + steps) % count) for k in range(count)])]
    ppermute x6 -> x3, waiting for transfers between devices: 15.2 us -> 7.39 us  [shifted(): lax.ppermute(value, axis, [(k, (k + steps) % count) for k in range(count)])]
    dot_general x7 -> x3, matrix products: 4.31 us -> 9.73 us  [the longest x2 8.22 us: gradient(): return jnp.einsum('cr,ce->re', weight, b, preferred_element_type=F32)]
    all_to_all x1, waiting for transfers between devices: 21.5 us -> 24.2 us  [shards(): pieces = lax.all_to_all(pieces, 'zl', 0, 0, tiled=True)]
  transfers between devices with their start and end apart: 12 -> 7, of which waited for: 9 -> 5; matrix products, arithmetic and copies ran while one was open for 3% -> 4% of each run, Pallas kernels for 0% -> 0%
where the time goes in v8:
time: 149 us
  waiting for transfers between devices  62.2 us (42%)
  starting transfers between devices  39.4 us (26%)
  blocking collectives  19.7 us (13%)
  matrix products  11.2 us (8%)
  other arithmetic  9.92 us (7%)
  local copies, waits for them, and re-layouts  4.57 us (3%)
  between operations  1.67 us (1%)
    all_to_all x1, waiting for transfers between devices, summed(): lax.all_to_all(parts, axis, 0, 0, tiled=True).astype(F32)  29.5 us
    all_to_all x1, waiting for transfers between devices, shards(): pieces = lax.all_to_all(pieces, 'zl', 0, 0, tiled=True)  24.2 us
    all_to_all x1, blocking collectives, shards(): pieces = lax.all_to_all(pieces, 'zl', 0, 0, tiled=True)  19.7 us
    all_to_all x1, starting transfers between devices, shards(): pieces = lax.all_to_all(pieces, 'zl', 0, 0, tiled=True)  15.7 us
    ppermute x3, starting transfers between devices, shifted(): lax.ppermute(value, axis, [(k, (k + steps) % count) for k in range(count)])  8.63 us
    dot_general x2, matrix products, gradient(): return jnp.einsum('cr,ce->re', weight, b, preferred_element_type=F32)  8.22 us
    ppermute x3, waiting for transfers between devices, shifted(): lax.ppermute(value, axis, [(k, (k + steps) % count) for k in range(count)])  7.39 us
    all_to_all x1, starting transfers between devices, spread(): return lax.all_to_all(copies, axis, 0, 0, tiled=True)  7.1 us
  transfers between devices with their start and end apart: 7, of which 5 were waited for; matrix products, arithmetic and copies ran while one was open for 4% of the time, Pallas kernels for 0%

profile of v8, /device:TPU:6, one launch (start us, length us, event | category | flops | bytes accessed | tf_op | source)
XLA Modules:
  0.0 148.6 jit_solution(2303103549141664365)
XLA Ops:
  0.0 0.0 copy-start
  0.0 1.1 copy-done
  1.1 1.4 abs_reduce_fusion.1
  2.6 0.0 copy-start.5
  2.6 1.5 %abs_reduce_fusion = (f32[256]{0:T(256)S(1)}, f32[256,128]{1,0:T(8,128)S(1)}) fusion(bf16[256,1024]{1,0:T(8,128)(2,1)} %param.8, bf16[1024,128]{1,0:T(8,128)(2,1)} %param.10), kind=kOutput, calls=%fused_computation.68 | convolution fusion | flops 67174144 | bytes 918528 | tf_op jit(solution)/shard_map/dot_general | solution.py:70
  4.1 0.1 reshape.456
  4.2 0.1 broadcast_select_fusion.1
  4.5 0.9 pad_maximum_fusion.1
  5.4 15.7 %all-to-all-start = ((f16[8,208,128]{2,1,0:T(8,128)(2,1)}), f16[8,208,128]{2,1,0:T(8,128)(2,1)S(1)}, u32[]{:S(2)}, u32[]{:S(2)}) async-start(f16[8,208,128]{2,1,0:T(8,128)(2,1)} %bitcast.6), calls=%async_computation | async-start | bytes 851968 | tf_op jit(solution)/shard_map/all_to_all | solution.py:90
  21.1 0.0 copy-done.5
  21.1 0.1 constant_dynamic-slice_fusion.1
  21.2 0.1 add_select_fusion.1
  21.4 0.1 iota_add_fusion
  21.4 24.2 %all-to-all-done = f16[8,208,128]{2,1,0:T(8,128)(2,1)S(1)} async-done(((f16[8,208,128]{2,1,0:T(8,128)(2,1)}), f16[8,208,128]{2,1,0:T(8,128)(2,1)S(1)}, u32[]{:S(2)}, u32[]{:S(2)}) %all-to-all-start) | async-done | bytes 426016 | tf_op jit(solution)/shard_map/all_to_all | solution.py:90
  45.6 0.1 copy.40
  45.8 0.9 fusion.44
  46.7 0.2 convert_multiply_fusion.1
  46.8 0.1 slice.38
  46.9 0.3 copy.45
  47.2 0.1 fusion.43
  47.3 1.2 broadcast_in_dim.20
  48.5 7.1 %all-to-all-start.1 = ((bf16[8,64,1024]{2,1,0:T(8,128)(2,1)}), bf16[8,64,1024]{2,1,0:T(8,128)(2,1)S(1)}, u32[]{:S(2)}, u32[]{:S(2)}) async-start(bf16[8,64,1024]{2,1,0:T(8,128)(2,1)} %broadcast_in_dim.20), calls=%async_computation.1 | async-start | bytes 2097152 | tf_op jit(solution)/shard_map/all_to_all | solution.py:15
  55.6 0.2 fusion.27
  55.8 0.1 fusion.26
  55.9 2.4 %collective-permute-start = (bf16[128,1024]{0,1:T(8,128)(2,1)S(1)}, bf16[128,1024]{0,1:T(8,128)(2,1)S(1)}, u32[]{:S(2)}, u32[]{:S(2)}) collective-permute-start(bf16[128,1024]{0,1:T(8,128)(2,1)S(1)} %fusion.26), channel_id=1, source_target_pairs={{0,256},{256,512},{512,768},{768,0},{1,257},{257,513},{513,769},{7... | collective-permute-start | bytes 786440 | tf_op jit(solution)/shard_map/ppermute | solution.py:30
  58.3 4.3 %collective-permute-start.1 = (bf16[128,1024]{0,1:T(8,128)(2,1)S(1)}, bf16[128,1024]{0,1:T(8,128)(2,1)S(1)}, u32[]{:S(2)}, u32[]{:S(2)}) collective-permute-start(bf16[128,1024]{0,1:T(8,128)(2,1)S(1)} %fusion.26), channel_id=1, source_target_pairs={{0,512},{256,768},{512,0},{768,256},{1,513},{257,769},{513,1},{769... | collective-permute-start | bytes 786440 | tf_op jit(solution)/shard_map/ppermute | solution.py:30
  62.6 1.9 %collective-permute-start.2 = (bf16[128,1024]{0,1:T(8,128)(2,1)S(1)}, bf16[128,1024]{0,1:T(8,128)(2,1)S(1)}, u32[]{:S(2)}, u32[]{:S(2)}) collective-permute-start(bf16[128,1024]{0,1:T(8,128)(2,1)S(1)} %fusion.26), channel_id=1, source_target_pairs={{0,768},{256,0},{512,256},{768,512},{1,769},{257,1},{513,257},{769... | collective-permute-start | bytes 786440 | tf_op jit(solution)/shard_map/ppermute | solution.py:30
  64.5 0.1 constant_dynamic-slice_fusion.3
  64.6 0.1 add_select_fusion
  64.7 0.0 collective-permute-done
  64.7 0.0 copy-start.2
  64.7 3.4 %collective-permute-done.1 = bf16[128,1024]{0,1:T(8,128)(2,1)S(1)} collective-permute-done((bf16[128,1024]{0,1:T(8,128)(2,1)S(1)}, bf16[128,1024]{0,1:T(8,128)(2,1)S(1)}, u32[]{:S(2)}, u32[]{:S(2)}) %collective-permute-start.1) | collective-permute-done | bytes 262176 | tf_op jit(solution)/shard_map/ppermute | solution.py:30
  68.0 0.0 copy-start.3
  68.0 4.0 %collective-permute-done.2 = bf16[128,1024]{0,1:T(8,128)(2,1)S(1)} collective-permute-done((bf16[128,1024]{0,1:T(8,128)(2,1)S(1)}, bf16[128,1024]{0,1:T(8,128)(2,1)S(1)}, u32[]{:S(2)}, u32[]{:S(2)}) %collective-permute-start.2) | collective-permute-done | bytes 262176 | tf_op jit(solution)/shard_map/ppermute | solution.py:30
  72.1 0.0 copy-start.4
  72.1 1.1 pad_maximum_fusion
  73.2 1.9 %collective-permute-start.3 = (bf16[512,1024]{0,1:T(8,128)(2,1)}, bf16[512,1024]{0,1:T(8,128)(2,1)}, u32[]{:S(2)}, u32[]{:S(2)}) collective-permute-start(bf16[512,1024]{0,1:T(8,128)(2,1)} %pad_maximum_fusion), channel_id=1, source_target_pairs={{0,16},{16,0},{1,17},{17,1},{2,18},{18,2},{3,19},{19,3},{4,20},{20... | collective-permute-start | bytes 3145736 | tf_op jit(solution)/shard_map/ppermute | solution.py:25
  75.1 0.1 reshape.415
  75.2 0.1 add.229
  76.7 1.2 all-to-all-done.1
  77.8 0.0 copy-start.1
  77.8 0.0 copy-done.2
  77.8 0.0 copy-done.3
  77.8 0.0 copy-done.4
  77.8 1.0 copy-done.1
  78.9 3.3 %fusion.19 = f32[512,1024]{1,0:T(8,128)S(1)} fusion(bf16[512,1024]{1,0:T(8,128)(2,1)} %bitcast.75, f32[]{:T(128)} %bitcast.72, f32[]{:T(128)} %bitcast.2, s32[512]{0:T(512)S(1)} %broadcast_select_fusion.4, s32[512]{0:T(512)S(1)} %dynamic-slice_bitcast_fusion, bf16[128,1024]{0,1:T(8,128)(2,1)} %copy-done.4, bf16[128,1024]{0,1:T(8,128)(2,1)} %copy-done.3, ...), kind=kOutput, calls=%fused_computation.23 | convolution fusion | flops 1085276160 | bytes 4198408 | tf_op jit(solution)/shard_map/cr,ce->re/dot_general | solution.py:125
  82.2 0.0 collective-permute-done.3
  82.2 4.9 %fusion.18 = f32[512,1024]{1,0:T(8,128)} fusion(bf16[512,1024]{0,1:T(8,128)(2,1)} %collective-permute-done.3, bf16[512,1024]{1,0:T(8,128)(2,1)} %bitcast.76, f32[]{:T(128)} %bitcast.73, f32[]{:T(128)} %bitcast.2, s32[512]{0:T(512)S(1)} %broadcast_select_fusion.4, s32[512]{0:T(512)S(1)} %bitcast.87), kind=kOutput, calls=%fused_computation.22 | convolution fusion | flops 1076887552 | bytes 4198408 | tf_op jit(solution)/shard_map/cr,ce->re/dot_general | solution.py:125
  87.1 3.1 %add_convert_fusion = f16[512,1024]{1,0:T(8,128)(2,1)} fusion(f32[512,1024]{1,0:T(8,128)S(1)} %fusion.19, f32[512,1024]{1,0:T(8,128)} %fusion.18), kind=kLoop, calls=%fused_computation.1 | loop fusion | flops 1048576 | bytes 5242880 | tf_op jit(solution)/shard_map/convert_element_type | solution.py:130
  90.2 6.0 %all-to-all-start.2 = ((f16[8,64,1024]{2,1,0:T(8,128)(2,1)}), f16[8,64,1024]{2,1,0:T(8,128)(2,1)S(1)}, u32[]{:S(2)}, u32[]{:S(2)}) async-start(f16[8,64,1024]{2,1,0:T(8,128)(2,1)} %bitcast.17), calls=%async_computation.2 | async-start | bytes 2097152 | tf_op jit(solution)/shard_map/all_to_all | solution.py:21
  96.2 29.5 %all-to-all-done.2 = f16[8,64,1024]{2,1,0:T(8,128)(2,1)S(1)} async-done(((f16[8,64,1024]{2,1,0:T(8,128)(2,1)}), f16[8,64,1024]{2,1,0:T(8,128)(2,1)S(1)}, u32[]{:S(2)}, u32[]{:S(2)}) %all-to-all-start.2) | async-done | bytes 1048608 | tf_op jit(solution)/shard_map/all_to_all | solution.py:21
  125.7 0.2 convert_reduce_fusion
  126.0 1.1 fusion.40
  127.1 0.3 fusion.42
  127.6 19.7 %all_to_all.20 = f16[8,72,128]{2,1,0:T(8,128)(2,1)S(1)} all-to-all(f16[8,72,128]{2,1,0:T(8,128)(2,1)S(1)} %copy.41), channel_id=1, replica_groups=mesh['x'=4,'y'=8,'c'=2,'zl'=8,'zh'=2] {'zl'}, dimensions={0} | all-to-all | bytes 294912 | tf_op jit(solution)/shard_map/all_to_all | solution.py:136
  147.3 0.4 convert_reduce_fusion.1
  147.8 0.1 exp2.125
  147.8 0.8 bitcast_divide_fusion.3
  (35 shorter events, 0.6 us)
Async XLA Ops:
  0.0 1.1 copy-start
  2.6 18.5 %copy-start.5 = (s32[16384]{0:T(1024)S(1)}, s32[16384]{0:T(1024)}, u32[]{:S(2)}) copy-start(s32[16384]{0:T(1024)} %param.11) | copy-start | bytes 196612
  5.4 40.2 %all-to-all-start = ((f16[8,208,128]{2,1,0:T(8,128)(2,1)}), f16[8,208,128]{2,1,0:T(8,128)(2,1)S(1)}, u32[]{:S(2)}, u32[]{:S(2)}) async-start(f16[8,208,128]{2,1,0:T(8,128)(2,1)} %bitcast.6), calls=%async_computation | async-start | bytes 851968 | tf_op jit(solution)/shard_map/all_to_all | solution.py:90
  48.5 29.3 %all-to-all-start.1 = ((bf16[8,64,1024]{2,1,0:T(8,128)(2,1)}), bf16[8,64,1024]{2,1,0:T(8,128)(2,1)S(1)}, u32[]{:S(2)}, u32[]{:S(2)}) async-start(bf16[8,64,1024]{2,1,0:T(8,128)(2,1)} %broadcast_in_dim.20), calls=%async_computation.1 | async-start | bytes 2097152 | tf_op jit(solution)/shard_map/all_to_all | solution.py:15
  55.9 8.8 %collective-permute-start = (bf16[128,1024]{0,1:T(8,128)(2,1)S(1)}, bf16[128,1024]{0,1:T(8,128)(2,1)S(1)}, u32[]{:S(2)}, u32[]{:S(2)}) collective-permute-start(bf16[128,1024]{0,1:T(8,128)(2,1)S(1)} %fusion.26), channel_id=1, source_target_pairs={{0,256},{256,512},{512,768},{768,0},{1,257},{257,513},{513,769},{7... | collective-permute-start | bytes 786440 | tf_op jit(solution)/shard_map/ppermute | solution.py:30
  58.3 9.8 %collective-permute-start.1 = (bf16[128,1024]{0,1:T(8,128)(2,1)S(1)}, bf16[128,1024]{0,1:T(8,128)(2,1)S(1)}, u32[]{:S(2)}, u32[]{:S(2)}) collective-permute-start(bf16[128,1024]{0,1:T(8,128)(2,1)S(1)} %fusion.26), channel_id=1, source_target_pairs={{0,512},{256,768},{512,0},{768,256},{1,513},{257,769},{513,1},{769... | collective-permute-start | bytes 786440 | tf_op jit(solution)/shard_map/ppermute | solution.py:30
  62.6 9.5 %collective-permute-start.2 = (bf16[128,1024]{0,1:T(8,128)(2,1)S(1)}, bf16[128,1024]{0,1:T(8,128)(2,1)S(1)}, u32[]{:S(2)}, u32[]{:S(2)}) collective-permute-start(bf16[128,1024]{0,1:T(8,128)(2,1)S(1)} %fusion.26), channel_id=1, source_target_pairs={{0,768},{256,0},{512,256},{768,512},{1,769},{257,1},{513,257},{769... | collective-permute-start | bytes 786440 | tf_op jit(solution)/shard_map/ppermute | solution.py:30
  64.7 13.2 %copy-start.2 = (bf16[128,1024]{0,1:T(8,128)(2,1)}, bf16[128,1024]{0,1:T(8,128)(2,1)S(1)}, u32[]{:S(2)}) copy-start(bf16[128,1024]{0,1:T(8,128)(2,1)S(1)} %collective-permute-done) | copy-start | bytes 786436
  68.0 9.8 %copy-start.3 = (bf16[128,1024]{0,1:T(8,128)(2,1)}, bf16[128,1024]{0,1:T(8,128)(2,1)S(1)}, u32[]{:S(2)}) copy-start(bf16[128,1024]{0,1:T(8,128)(2,1)S(1)} %collective-permute-done.1) | copy-start | bytes 786436
  72.1 5.8 %copy-start.4 = (bf16[128,1024]{0,1:T(8,128)(2,1)}, bf16[128,1024]{0,1:T(8,128)(2,1)S(1)}, u32[]{:S(2)}) copy-start(bf16[128,1024]{0,1:T(8,128)(2,1)S(1)} %collective-permute-done.2) | copy-start | bytes 786436
  73.2 9.0 %collective-permute-start.3 = (bf16[512,1024]{0,1:T(8,128)(2,1)}, bf16[512,1024]{0,1:T(8,128)(2,1)}, u32[]{:S(2)}, u32[]{:S(2)}) collective-permute-start(bf16[512,1024]{0,1:T(8,128)(2,1)} %pad_maximum_fusion), channel_id=1, source_target_pairs={{0,16},{16,0},{1,17},{17,1},{2,18},{18,2},{3,19},{19,3},{4,20},{20... | collective-permute-start | bytes 3145736 | tf_op jit(solution)/shard_map/ppermute | solution.py:25
  77.8 1.0 copy-start.1
  90.2 35.5 %all-to-all-start.2 = ((f16[8,64,1024]{2,1,0:T(8,128)(2,1)}), f16[8,64,1024]{2,1,0:T(8,128)(2,1)S(1)}, u32[]{:S(2)}, u32[]{:S(2)}) async-start(f16[8,64,1024]{2,1,0:T(8,128)(2,1)} %bitcast.17), calls=%async_computation.2 | async-start | bytes 2097152 | tf_op jit(solution)/shard_map/all_to_all | solution.py:21

commit v9 on v8

--- a/solution.py
+++ b/solution.py
@@ -58,11 +58,11 @@
 def shards(image_features, text_features, image_head, text_head, positive, log_scale, bias):
     rows = image_features.shape[0]
     lanes = lax.axis_size("zl")
-    owns, others = rows // 4, rows // 2
+    owns, others = rows // 2, rows // 4
     x, y, c = (lax.axis_index(name) for name in BLK)
     is_image = lax.axis_index("zh") == 0
     plane = lax.axis_index("zl")
-    own_part, other_part = plane // 2, plane % 2
+    own_part, other_part = plane // 4, plane % 4
     scale = jnp.exp(log_scale[0])
     offset = bias[0]
 
@@ -84,8 +84,8 @@
 
     own = parted(image_cols, text_cols, image_powers, text_powers, owns)
     other = parted(text_cols, image_cols, text_powers, image_powers, others)
-    own = jnp.broadcast_to(own[:, None], (4, 2) + own.shape[1:])
-    other = jnp.broadcast_to(other[None], (4, 2) + other.shape[1:])
+    own = jnp.broadcast_to(own[:, None], (2, 4) + own.shape[1:])
+    other = jnp.broadcast_to(other[None], (2, 4) + other.shape[1:])
     pieces = jnp.concatenate([own, other], axis=2).reshape(lanes, -1, width)
     pieces = lax.all_to_all(pieces, "zl", 0, 0, tiled=True)
 
@@ -97,9 +97,12 @@
     own_unit, own_norm = normalize(whole(pieces[:, : owns + 8], owns))
     other_unit, _ = normalize(whole(pieces[:, owns + 8 :], others))
 
-    own_b = spread(own_unit.astype(jnp.bfloat16), "y").reshape(8 * owns, -1)
-    other_b = other_unit.astype(jnp.bfloat16)
-    near_b = jnp.concatenate([other_b] + [shifted(other_b, "x", k) for k in range(1, 4)])
+    near_b = spread(other_unit.astype(jnp.bfloat16), "y").reshape(8 * others, -1)
+    own_b = own_unit.astype(jnp.bfloat16)
+    own_b = [shifted(own_b, "x", k) for k in (3, 2, 1)] + [own_b]
+    own_b = jnp.concatenate(own_b + own_b[:3])
+    own_b = lax.dynamic_slice_in_dim(own_b, (3 - x) * owns, 4 * owns)
+    near_b, own_b = lax.optimization_barrier((near_b, own_b))
     far_b = swapped(near_b)
 
     table = positive.reshape(4, 8, 2 * rows)
@@ -111,30 +114,30 @@
         index = block.reshape(-1, 1) * 2 * rows + lane + jnp.arange(count, dtype=jnp.int32)
         return jnp.where(image, found, index)
 
-    own_keys = keys((x, 0), (1, 8), c * rows + own_part * owns, owns, is_image).reshape(1, -1)
+    own_keys = keys((0, y), (4, 1), c * rows + own_part * owns, owns, is_image).reshape(1, -1)
 
     def other_keys(core):
-        found = keys((0, y), (4, 1), core * rows + other_part * others, others, ~is_image)[::-1]
-        found = jnp.concatenate([found, found])
-        return lax.dynamic_slice_in_dim(found, 3 - x, 4).reshape(-1, 1)
+        lane = core * rows + other_part * others
+        return keys((x, 0), (1, 8), lane, others, ~is_image).reshape(-1, 1)
 
     def gradient(b, key):
         logits = scale * jnp.einsum("ce,re->cr", b, own_b, preferred_element_type=F32) + offset
         sign = jnp.where(own_keys == key, 1.0, -1.0)
         weight = (-sign * jax.nn.sigmoid(-sign * logits) * scale).astype(jnp.bfloat16)
+        weight = lax.optimization_barrier(weight)
         return jnp.einsum("cr,ce->re", weight, b, preferred_element_type=F32)
 
     near_keys, far_keys = other_keys(c), other_keys(1 - c)
     grad = gradient(near_b, near_keys)
     grad, far_b, far_keys = lax.optimization_barrier((grad, far_b, far_keys))
-    grad = summed((grad + gradient(far_b, far_keys)).astype(HALF), "y")
+    grad = summed((grad + gradient(far_b, far_keys)).astype(HALF), "x")
 
     powers = exponent(own_norm) - 3.0
     grad = projected(grad, own_unit) * (jnp.exp2(powers) / own_norm)
     grad = grad.reshape(owns, lanes, width).transpose(1, 0, 2)
     pieces = with_exponents(grad, powers.reshape(1, owns))
     pieces = lax.all_to_all(pieces, "zl", 0, 0, tiled=True)
-    grad, powers = without_exponents(pieces.reshape(4, 2, owns + 8, width), owns)
+    grad, powers = without_exponents(pieces.reshape(2, 4, owns + 8, width), owns)
     grad = jnp.sum(grad, axis=1) / jnp.exp2(powers[:, 0])[..., None]
     return grad.reshape(1, rows, width)
 

time: 149 us -> 138 us (0.926)
  waiting for transfers between devices: 62.2 us -> 48.4 us
  blocking collectives: 19.7 us -> 27.8 us
  other arithmetic: 9.92 us -> 5.51 us
  matrix products: 11.2 us -> 7.64 us
  local copies, waits for them, and re-layouts: 4.57 us -> 6.14 us
    all_to_all x1, waiting for transfers between devices: 29.5 us -> 13.6 us  [summed(): lax.all_to_all(parts, axis, 0, 0, tiled=True).astype(F32)]
    all_to_all x1, blocking collectives: 19.7 us -> 27.8 us  [shards(): pieces = lax.all_to_all(pieces, 'zl', 0, 0, tiled=True)]
    dot_general x2, matrix products: 8.22 us -> 1.45 us  [gradient(): return jnp.einsum('cr,ce->re', weight, b, preferred_element_type=F32)]
    all_to_all x1, waiting for transfers between devices: 1.17 us -> 5.61 us  [spread(): return lax.all_to_all(copies, axis, 0, 0, tiled=True)]
    dot_general x0 -> x2, matrix products: none -> 3.26 us  [gradient(): jnp.einsum('ce,re->cr', b, own_b, preferred_element_type=F32)]
    ppermute x3, waiting for transfers between devices: 7.39 us -> 5.06 us  [shifted(): lax.ppermute(value, axis, [(k, (k + steps) % count) for k in range(count)])]
    convert_element_type x3, other arithmetic: 3.22 us -> 1.71 us  [the longest x1 1.5 us: shards(): grad = summed((grad + gradient(far_b, far_keys)).astype(HALF), 'x')]
where the time goes in v9:
time: 138 us; the launch traced here: 136 us
  waiting for transfers between devices  48.4 us (35%)
  starting transfers between devices  39.2 us (28%)
  blocking collectives  27.8 us (20%)
  matrix products  7.64 us (6%)
  local copies, waits for them, and re-layouts  6.14 us (4%)
  other arithmetic  5.51 us (4%)
  between operations  1.71 us (1%)
    all_to_all x1, blocking collectives, shards(): pieces = lax.all_to_all(pieces, 'zl', 0, 0, tiled=True)  27.8 us
    all_to_all x1, waiting for transfers between devices, shards(): pieces = lax.all_to_all(pieces, 'zl', 0, 0, tiled=True)  24.1 us
    all_to_all x1, starting transfers between devices, shards(): pieces = lax.all_to_all(pieces, 'zl', 0, 0, tiled=True)  15.7 us
    all_to_all x1, waiting for transfers between devices, summed(): lax.all_to_all(parts, axis, 0, 0, tiled=True).astype(F32)  13.6 us
    ppermute x3, starting transfers between devices, shifted(): lax.ppermute(value, axis, [(k, (k + steps) % count) for k in range(count)])  9.74 us
    all_to_all x1, starting transfers between devices, spread(): return lax.all_to_all(copies, axis, 0, 0, tiled=True)  7.1 us
    all_to_all x1, waiting for transfers between devices, spread(): return lax.all_to_all(copies, axis, 0, 0, tiled=True)  5.61 us
    ppermute x3, waiting for transfers between devices, shifted(): lax.ppermute(value, axis, [(k, (k + steps) % count) for k in range(count)])  5.06 us
  transfers between devices with their start and end apart: 7, of which 5 were waited for; matrix products, arithmetic and copies ran while one was open for 4% of the time, Pallas kernels for 0%

profile of v9, /device:TPU:6, one launch (start us, length us, event | category | flops | bytes accessed | tf_op | source)
XLA Modules:
  0.0 136.4 jit_solution(503243313841053288)
XLA Ops:
  0.0 0.0 copy-start
  0.0 1.1 copy-done
  1.1 1.4 %abs_reduce_fusion.1 = (f32[256]{0:T(256)S(1)}, f32[256,128]{1,0:T(8,128)S(1)}) fusion(bf16[256,1536]{1,0:T(8,128)(2,1)S(1)} %copy-done, bf16[1536,128]{1,0:T(8,128)(2,1)} %param.9), kind=kOutput, calls=%fused_computation.48 | convolution fusion | flops 100728576 | bytes 1311744 | tf_op jit(solution)/shard_map/dot_general | solution.py:69
  2.6 0.0 copy-start.2
  2.6 1.5 %abs_reduce_fusion = (f32[256]{0:T(256)S(1)}, f32[256,128]{1,0:T(8,128)S(1)}) fusion(bf16[256,1024]{1,0:T(8,128)(2,1)} %param.8, bf16[1024,128]{1,0:T(8,128)(2,1)} %param.10), kind=kOutput, calls=%fused_computation.46 | convolution fusion | flops 67174144 | bytes 918528 | tf_op jit(solution)/shard_map/dot_general | solution.py:70
  4.1 0.1 reshape.505
  4.2 0.1 broadcast_select_fusion.1
  4.5 0.9 pad_maximum_fusion.1
  5.4 15.7 %all-to-all-start = ((f16[8,208,128]{2,1,0:T(8,128)(2,1)}), f16[8,208,128]{2,1,0:T(8,128)(2,1)S(1)}, u32[]{:S(2)}, u32[]{:S(2)}) async-start(f16[8,208,128]{2,1,0:T(8,128)(2,1)} %bitcast.6), calls=%async_computation | async-start | bytes 851968 | tf_op jit(solution)/shard_map/all_to_all | solution.py:90
  21.1 0.0 copy-done.2
  21.1 0.1 constant_dynamic-slice_fusion
  21.2 0.1 reshape.466
  21.3 0.1 iota_add_fusion.1
  21.4 0.1 add.259
  21.5 24.1 %all-to-all-done = f16[8,208,128]{2,1,0:T(8,128)(2,1)S(1)} async-done(((f16[8,208,128]{2,1,0:T(8,128)(2,1)}), f16[8,208,128]{2,1,0:T(8,128)(2,1)S(1)}, u32[]{:S(2)}, u32[]{:S(2)}) %all-to-all-start) | async-done | bytes 426016 | tf_op jit(solution)/shard_map/all_to_all | solution.py:90
  45.6 0.1 slice.40
  45.7 0.3 copy.48
  46.0 0.2 fusion.19
  46.2 0.2 fusion.22
  46.4 0.2 fusion.21
  46.6 1.2 broadcast_in_dim.20
  47.8 7.1 %all-to-all-start.1 = ((bf16[8,64,1024]{2,1,0:T(8,128)(2,1)}), bf16[8,64,1024]{2,1,0:T(8,128)(2,1)S(1)}, u32[]{:S(2)}, u32[]{:S(2)}) async-start(bf16[8,64,1024]{2,1,0:T(8,128)(2,1)} %broadcast_in_dim.20), calls=%async_computation.1 | async-start | bytes 2097152 | tf_op jit(solution)/shard_map/all_to_all | solution.py:15
  54.9 0.1 fusion.18
  54.9 2.7 %collective-permute-start = (bf16[128,1024]{0,1:T(8,128)(2,1)S(1)}, bf16[128,1024]{0,1:T(8,128)(2,1)S(1)}, u32[]{:S(2)}, u32[]{:S(2)}) collective-permute-start(bf16[128,1024]{0,1:T(8,128)(2,1)S(1)} %fusion.18), channel_id=1, source_target_pairs={{0,768},{256,0},{512,256},{768,512},{1,769},{257,1},{513,257},{769... | collective-permute-start | bytes 786440 | tf_op jit(solution)/shard_map/ppermute | solution.py:30
  57.7 0.1 iota_add_fusion
  57.8 3.0 %collective-permute-start.1 = (bf16[128,1024]{0,1:T(8,128)(2,1)S(1)}, bf16[128,1024]{0,1:T(8,128)(2,1)S(1)}, u32[]{:S(2)}, u32[]{:S(2)}) collective-permute-start(bf16[128,1024]{0,1:T(8,128)(2,1)S(1)} %fusion.18), channel_id=1, source_target_pairs={{0,512},{256,768},{512,0},{768,256},{1,513},{257,769},{513,1},{769... | collective-permute-start | bytes 786440 | tf_op jit(solution)/shard_map/ppermute | solution.py:30
  60.8 0.1 constant_dynamic-slice_fusion.3
  60.9 4.0 %collective-permute-start.2 = (bf16[128,1024]{0,1:T(8,128)(2,1)S(1)}, bf16[128,1024]{0,1:T(8,128)(2,1)S(1)}, u32[]{:S(2)}, u32[]{:S(2)}) collective-permute-start(bf16[128,1024]{0,1:T(8,128)(2,1)S(1)} %fusion.18), channel_id=1, source_target_pairs={{0,256},{256,512},{512,768},{768,0},{1,257},{257,513},{513,769},{7... | collective-permute-start | bytes 786440 | tf_op jit(solution)/shard_map/ppermute | solution.py:30
  64.9 0.0 collective-permute-done
  64.9 2.6 %collective-permute-done.1 = bf16[128,1024]{0,1:T(8,128)(2,1)S(1)} collective-permute-done((bf16[128,1024]{0,1:T(8,128)(2,1)S(1)}, bf16[128,1024]{0,1:T(8,128)(2,1)S(1)}, u32[]{:S(2)}, u32[]{:S(2)}) %collective-permute-start.1) | collective-permute-done | bytes 262176 | tf_op jit(solution)/shard_map/ppermute | solution.py:30
  67.5 0.1 constant_dynamic-update-slice_fusion.5
  67.6 2.5 %collective-permute-done.2 = bf16[128,1024]{0,1:T(8,128)(2,1)S(1)} collective-permute-done((bf16[128,1024]{0,1:T(8,128)(2,1)S(1)}, bf16[128,1024]{0,1:T(8,128)(2,1)S(1)}, u32[]{:S(2)}, u32[]{:S(2)}) %collective-permute-start.2) | collective-permute-done | bytes 262176 | tf_op jit(solution)/shard_map/ppermute | solution.py:30
  70.1 0.1 constant_dynamic-update-slice_fusion.4
  70.1 0.1 constant_dynamic-update-slice_fusion.3
  70.2 0.1 constant_dynamic-update-slice_fusion.2
  70.3 0.1 constant_dynamic-update-slice_fusion.1
  70.3 0.1 constant_dynamic-update-slice_fusion
  70.4 1.1 constant_dynamic-slice_fusion.1
  71.5 5.6 %all-to-all-done.1 = bf16[8,64,1024]{2,1,0:T(8,128)(2,1)S(1)} async-done(((bf16[8,64,1024]{2,1,0:T(8,128)(2,1)}), bf16[8,64,1024]{2,1,0:T(8,128)(2,1)S(1)}, u32[]{:S(2)}, u32[]{:S(2)}) %all-to-all-start.1) | async-done | bytes 1048608 | tf_op jit(solution)/shard_map/all_to_all | solution.py:15
  77.1 1.9 %collective-permute-start.3 = (bf16[512,1024]{1,0:T(8,128)(2,1)S(1)}, bf16[512,1024]{1,0:T(8,128)(2,1)S(1)}, u32[]{:S(2)}, u32[]{:S(2)}) collective-permute-start(bf16[512,1024]{1,0:T(8,128)(2,1)S(1)} %bitcast.73), channel_id=1, source_target_pairs={{0,16},{16,0},{1,17},{17,1},{2,18},{18,2},{3,19},{19,3},{4,20},{20... | collective-permute-start | bytes 3145736 | tf_op jit(solution)/shard_map/ppermute | solution.py:25
  79.0 0.1 bitcast_select_fusion
  80.4 0.1 reshape.473
  80.5 0.1 add.275
  80.6 2.2 %fusion.16 = bf16[512,512]{1,0:T(8,128)(2,1)S(1)} fusion(bf16[512,1024]{1,0:T(8,128)(2,1)S(1)} %bitcast.74, bf16[512,1024]{0,1:T(8,128)(2,1)} %constant_dynamic-slice_fusion.1, f32[]{:T(128)} %bitcast.71, f32[]{:T(128)} %bitcast.2, s32[512]{0:T(512)S(1)} %bitcast_select_fusion, s32[512]{0:T(512)S(1)} %broadcast_select_fusion.5), kind=kOutput, calls=%fused_computation.20 | convolution fusion | flops 540016640 | bytes 2625544 | tf_op jit(solution)/shard_map/ce,re->cr/dot_general | solution.py:124
  82.8 0.0 copy-start.1
  82.9 0.7 fusion.33
  83.6 0.0 collective-permute-done.3
  83.6 0.5 copy-done.1
  84.1 1.0 fusion.17
  85.1 0.7 fusion.34
  85.8 1.5 %add_convert_fusion = f16[512,1024]{1,0:T(8,128)(2,1)} fusion(f32[512,1024]{1,0:T(8,128)S(1)} %fusion.33, f32[512,1024]{1,0:T(8,128)S(1)} %fusion.34), kind=kLoop, calls=%fused_computation.1 | loop fusion | flops 1048576 | bytes 5242880 | tf_op jit(solution)/shard_map/convert_element_type | solution.py:133
  87.3 4.8 %all-to-all-start.2 = ((f16[4,128,1024]{2,1,0:T(8,128)(2,1)}), f16[4,128,1024]{2,1,0:T(8,128)(2,1)S(1)}, u32[]{:S(2)}, u32[]{:S(2)}) async-start(f16[4,128,1024]{2,1,0:T(8,128)(2,1)} %bitcast.15), calls=%async_computation.2 | async-start | bytes 2097152 | tf_op jit(solution)/shard_map/all_to_all | solution.py:21
  92.1 0.1 copy.42
  92.2 13.6 %all-to-all-done.2 = f16[4,128,1024]{2,1,0:T(8,128)(2,1)S(1)} async-done(((f16[4,128,1024]{2,1,0:T(8,128)(2,1)}), f16[4,128,1024]{2,1,0:T(8,128)(2,1)S(1)}, u32[]{:S(2)}, u32[]{:S(2)}) %all-to-all-start.2) | async-done | bytes 1048608 | tf_op jit(solution)/shard_map/all_to_all | solution.py:21
  105.8 0.2 convert_reduce_fusion
  106.0 0.2 copy.41
  106.2 0.2 multiply_reduce_fusion
  106.4 0.1 fusion.20
  106.6 0.2 pad_maximum_fusion
  106.7 0.4 copy.43
  107.2 27.8 %all_to_all.20 = f16[8,136,128]{2,1,0:T(8,128)(2,1)S(1)} all-to-all(f16[8,136,128]{2,1,0:T(8,128)(2,1)S(1)} %copy.43), channel_id=1, replica_groups=mesh['x'=4,'y'=8,'c'=2,'zl'=8,'zh'=2] {'zl'}, dimensions={0} | all-to-all | bytes 557056 | tf_op jit(solution)/shard_map/all_to_all | solution.py:139
  135.0 0.1 slice.42
  135.1 0.5 convert_reduce_fusion.1
  135.6 0.8 bitcast_divide_fusion.3
  (26 shorter events, 0.4 us)
Async XLA Ops:
  0.0 1.1 copy-start
  2.6 18.5 %copy-start.2 = (s32[16384]{0:T(1024)S(1)}, s32[16384]{0:T(1024)}, u32[]{:S(2)}) copy-start(s32[16384]{0:T(1024)} %param.11) | copy-start | bytes 196612
  5.4 40.2 %all-to-all-start = ((f16[8,208,128]{2,1,0:T(8,128)(2,1)}), f16[8,208,128]{2,1,0:T(8,128)(2,1)S(1)}, u32[]{:S(2)}, u32[]{:S(2)}) async-start(f16[8,208,128]{2,1,0:T(8,128)(2,1)} %bitcast.6), calls=%async_computation | async-start | bytes 851968 | tf_op jit(solution)/shard_map/all_to_all | solution.py:90
  47.8 29.3 %all-to-all-start.1 = ((bf16[8,64,1024]{2,1,0:T(8,128)(2,1)}), bf16[8,64,1024]{2,1,0:T(8,128)(2,1)S(1)}, u32[]{:S(2)}, u32[]{:S(2)}) async-start(bf16[8,64,1024]{2,1,0:T(8,128)(2,1)} %broadcast_in_dim.20), calls=%async_computation.1 | async-start | bytes 2097152 | tf_op jit(solution)/shard_map/all_to_all | solution.py:15
  54.9 9.9 %collective-permute-start = (bf16[128,1024]{0,1:T(8,128)(2,1)S(1)}, bf16[128,1024]{0,1:T(8,128)(2,1)S(1)}, u32[]{:S(2)}, u32[]{:S(2)}) collective-permute-start(bf16[128,1024]{0,1:T(8,128)(2,1)S(1)} %fusion.18), channel_id=1, source_target_pairs={{0,768},{256,0},{512,256},{768,512},{1,769},{257,1},{513,257},{769... | collective-permute-start | bytes 786440 | tf_op jit(solution)/shard_map/ppermute | solution.py:30
  57.8 9.8 %collective-permute-start.1 = (bf16[128,1024]{0,1:T(8,128)(2,1)S(1)}, bf16[128,1024]{0,1:T(8,128)(2,1)S(1)}, u32[]{:S(2)}, u32[]{:S(2)}) collective-permute-start(bf16[128,1024]{0,1:T(8,128)(2,1)S(1)} %fusion.18), channel_id=1, source_target_pairs={{0,512},{256,768},{512,0},{768,256},{1,513},{257,769},{513,1},{769... | collective-permute-start | bytes 786440 | tf_op jit(solution)/shard_map/ppermute | solution.py:30
  60.9 9.2 %collective-permute-start.2 = (bf16[128,1024]{0,1:T(8,128)(2,1)S(1)}, bf16[128,1024]{0,1:T(8,128)(2,1)S(1)}, u32[]{:S(2)}, u32[]{:S(2)}) collective-permute-start(bf16[128,1024]{0,1:T(8,128)(2,1)S(1)} %fusion.18), channel_id=1, source_target_pairs={{0,256},{256,512},{512,768},{768,0},{1,257},{257,513},{513,769},{7... | collective-permute-start | bytes 786440 | tf_op jit(solution)/shard_map/ppermute | solution.py:30
  77.1 6.5 %collective-permute-start.3 = (bf16[512,1024]{1,0:T(8,128)(2,1)S(1)}, bf16[512,1024]{1,0:T(8,128)(2,1)S(1)}, u32[]{:S(2)}, u32[]{:S(2)}) collective-permute-start(bf16[512,1024]{1,0:T(8,128)(2,1)S(1)} %bitcast.73), channel_id=1, source_target_pairs={{0,16},{16,0},{1,17},{17,1},{2,18},{18,2},{3,19},{19,3},{4,20},{20... | collective-permute-start | bytes 3145736 | tf_op jit(solution)/shard_map/ppermute | solution.py:25
  82.8 1.2 copy-start.1
  87.3 18.4 %all-to-all-start.2 = ((f16[4,128,1024]{2,1,0:T(8,128)(2,1)}), f16[4,128,1024]{2,1,0:T(8,128)(2,1)S(1)}, u32[]{:S(2)}, u32[]{:S(2)}) async-start(f16[4,128,1024]{2,1,0:T(8,128)(2,1)} %bitcast.15), calls=%async_computation.2 | async-start | bytes 2097152 | tf_op jit(solution)/shard_map/all_to_all | solution.py:21

commit v10 on v9

--- a/solution.py
+++ b/solution.py
@@ -66,8 +66,9 @@
     scale = jnp.exp(log_scale[0])
     offset = bias[0]
 
+    text_cols = jnp.dot(text_features, text_head, preferred_element_type=F32)
+    text_cols, image_features = lax.optimization_barrier((text_cols, image_features))
     image_cols = jnp.dot(image_features, image_head, preferred_element_type=F32)
-    text_cols = jnp.dot(text_features, text_head, preferred_element_type=F32)
     width = image_cols.shape[-1]
 
     def scaled(cols):
@@ -77,34 +78,35 @@
     image_cols, image_powers = scaled(image_cols)
     text_cols, text_powers = scaled(text_cols)
 
-    def parted(image, text, powers_image, powers_text, count):
-        cols = jnp.where(is_image, image, text).reshape(-1, count, width)
-        powers = jnp.where(is_image, powers_image, powers_text).reshape(-1, count)
-        return with_exponents(cols, powers)
-
-    own = parted(image_cols, text_cols, image_powers, text_powers, owns)
-    other = parted(text_cols, image_cols, text_powers, image_powers, others)
-    own = jnp.broadcast_to(own[:, None], (2, 4) + own.shape[1:])
-    other = jnp.broadcast_to(other[None], (2, 4) + other.shape[1:])
-    pieces = jnp.concatenate([own, other], axis=2).reshape(lanes, -1, width)
+    own_cols = jnp.where(is_image, image_cols, text_cols).reshape(2, 1, owns, width)
+    other_cols = jnp.where(is_image, text_cols, image_cols).reshape(1, 4, others, width)
+    own_powers = jnp.where(is_image, image_powers, text_powers).reshape(2, 1, 1, owns)
+    other_powers = jnp.where(is_image, text_powers, image_powers).reshape(1, 4, 1, others)
+    own_powers = jnp.pad(own_powers, ((0, 0), (0, 0), (0, 7), (0, width - owns)))
+    other_powers = jnp.pad(other_powers, ((0, 0), (0, 0), (1, 6), (0, width - others)))
+    pieces = [
+        jnp.broadcast_to(own_cols, (2, 4, owns, width)),
+        jnp.broadcast_to(other_cols, (2, 4, others, width)),
+        own_powers + other_powers,
+    ]
+    pieces = jnp.concatenate(pieces, axis=2).reshape(lanes, -1, width)
     pieces = lax.all_to_all(pieces, "zl", 0, 0, tiled=True)
 
-    def whole(part, count):
-        part, powers = without_exponents(part, count)
-        part = part * jnp.exp2(powers)[..., None]
-        return part.transpose(1, 0, 2).reshape(count, lanes * width)
+    def whole(part, powers):
+        part = part.astype(F32) * jnp.exp2(powers.astype(F32))[..., None]
+        return part.transpose(1, 0, 2).reshape(-1, lanes * width)
 
-    own_unit, own_norm = normalize(whole(pieces[:, : owns + 8], owns))
-    other_unit, _ = normalize(whole(pieces[:, owns + 8 :], others))
+    received = owns + others
+    own_unit, own_norm = normalize(whole(pieces[:, :owns], pieces[:, received, :owns]))
+    other_unit, _ = normalize(
+        whole(pieces[:, owns:received], pieces[:, received + 1, :others])
+    )
 
     near_b = spread(other_unit.astype(jnp.bfloat16), "y").reshape(8 * others, -1)
     own_b = own_unit.astype(jnp.bfloat16)
     own_b = [shifted(own_b, "x", k) for k in (3, 2, 1)] + [own_b]
     own_b = jnp.concatenate(own_b + own_b[:3])
     own_b = lax.dynamic_slice_in_dim(own_b, (3 - x) * owns, 4 * owns)
-    near_b, own_b = lax.optimization_barrier((near_b, own_b))
-    far_b = swapped(near_b)
-
     table = positive.reshape(4, 8, 2 * rows)
 
     def keys(start, size, lane, count, image):
@@ -127,7 +129,10 @@
         weight = lax.optimization_barrier(weight)
         return jnp.einsum("cr,ce->re", weight, b, preferred_element_type=F32)
 
-    near_keys, far_keys = other_keys(c), other_keys(1 - c)
+    near_b, own_b, own_keys, near_keys, far_keys = lax.optimization_barrier(
+        (near_b, own_b, own_keys, other_keys(c), other_keys(1 - c))
+    )
+    far_b = swapped(near_b)
     grad = gradient(near_b, near_keys)
     grad, far_b, far_keys = lax.optimization_barrier((grad, far_b, far_keys))
     grad = summed((grad + gradient(far_b, far_keys)).astype(HALF), "x")

time: 138 us -> 134 us (0.971)
  local copies, waits for them, and re-layouts: 6.14 us -> 3.45 us
    unnamed x15 -> x12, local copies, waits for them, and re-layouts: 2.26 us -> 0.64 us
  transfers between devices with their start and end apart: 7 -> 7, of which waited for: 5 -> 5; matrix products, arithmetic and copies ran while one was open for 4% -> 2% of each run, Pallas kernels for 0% -> 0%
where the time goes in v10:
time: 134 us; the launch traced here: 133 us
  waiting for transfers between devices  48.7 us (36%)
  starting transfers between devices  39.2 us (29%)
  blocking collectives  27.5 us (21%)
  matrix products  6.42 us (5%)
  other arithmetic  5.67 us (4%)
  local copies, waits for them, and re-layouts  3.45 us (3%)
  between operations  1.71 us (1%)
    all_to_all x1, blocking collectives, shards(): pieces = lax.all_to_all(pieces, 'zl', 0, 0, tiled=True)  27.5 us
    all_to_all x1, waiting for transfers between devices, shards(): pieces = lax.all_to_all(pieces, 'zl', 0, 0, tiled=True)  23.2 us
    all_to_all x1, starting transfers between devices, shards(): pieces = lax.all_to_all(pieces, 'zl', 0, 0, tiled=True)  15.7 us
    all_to_all x1, waiting for transfers between devices, summed(): lax.all_to_all(parts, axis, 0, 0, tiled=True).astype(F32)  13.6 us
    ppermute x3, starting transfers between devices, shifted(): lax.ppermute(value, axis, [(k, (k + steps) % count) for k in range(count)])  9.75 us
    all_to_all x1, starting transfers between devices, spread(): return lax.all_to_all(copies, axis, 0, 0, tiled=True)  7.1 us
    all_to_all x1, waiting for transfers between devices, spread(): return lax.all_to_all(copies, axis, 0, 0, tiled=True)  6.87 us
    ppermute x3, waiting for transfers between devices, shifted(): lax.ppermute(value, axis, [(k, (k + steps) % count) for k in range(count)])  5.07 us
  transfers between devices with their start and end apart: 7, of which 5 were waited for; matrix products, arithmetic and copies ran while one was open for 2% of the time, Pallas kernels for 0%

profile of v10, /device:TPU:6, one launch (start us, length us, event | category | flops | bytes accessed | tf_op | source)
XLA Modules:
  0.0 132.7 jit_solution(16754217206043068331)
XLA Ops:
  0.0 0.0 copy-start
  0.0 1.5 %fusion.29 = f32[256,128]{1,0:T(8,128)S(1)} fusion(bf16[256,1024]{1,0:T(8,128)(2,1)} %param.8, bf16[1024,128]{1,0:T(8,128)(2,1)} %param.10), kind=kOutput, calls=%fused_computation.89 | convolution fusion | flops 67108864 | bytes 917504 | tf_op jit(solution)/shard_map/dot_general | solution.py:69
  1.5 0.1 abs_reduce_fusion
  1.6 0.0 copy-done
  1.6 0.0 copy-start.1
  1.6 1.5 %abs_reduce_fusion.1 = (f32[256]{0:T(256)S(1)}, f32[256,128]{1,0:T(8,128)S(1)}) fusion(bf16[256,1536]{1,0:T(8,128)(2,1)S(1)} %copy-done, bf16[1536,128]{1,0:T(8,128)(2,1)} %param.9), kind=kOutput, calls=%fused_computation.44 | convolution fusion | flops 100728576 | bytes 1311744 | tf_op jit(solution)/shard_map/dot_general | solution.py:71
  3.1 0.1 reshape.523
  3.3 0.1 broadcast_select_fusion.1
  3.5 0.9 pad_maximum_fusion.1
  4.4 15.7 %all-to-all-start = ((f16[8,200,128]{2,1,0:T(8,128)(2,1)}), f16[8,200,128]{2,1,0:T(8,128)(2,1)S(1)}, u32[]{:S(2)}, u32[]{:S(2)}) async-start(f16[8,200,128]{2,1,0:T(8,128)(2,1)} %pad_maximum_fusion.1), calls=%async_computation | async-start | bytes 819200 | tf_op jit(solution)/shard_map/all_to_all | solution.py:93
  20.1 0.0 copy-done.1
  20.1 0.1 constant_dynamic-slice_fusion
  20.2 0.1 reshape.498
  20.3 0.1 iota_add_fusion
  20.4 0.1 add.305
  20.4 0.1 reshape.497
  20.5 0.1 iota_add_fusion.1
  20.6 0.1 add.297
  20.7 23.2 %all-to-all-done = f16[8,200,128]{2,1,0:T(8,128)(2,1)S(1)} async-done(((f16[8,200,128]{2,1,0:T(8,128)(2,1)}), f16[8,200,128]{2,1,0:T(8,128)(2,1)S(1)}, u32[]{:S(2)}, u32[]{:S(2)}) %all-to-all-start) | async-done | bytes 409632 | tf_op jit(solution)/shard_map/all_to_all | solution.py:93
  43.9 0.1 slice.34
  44.0 0.3 copy.46
  44.2 0.2 fusion.19
  44.5 0.2 fusion.22
  44.7 0.2 fusion.21
  44.9 1.1 broadcast_in_dim.26
  46.0 7.1 %all-to-all-start.1 = ((bf16[8,64,1024]{2,1,0:T(8,128)(2,1)}), bf16[8,64,1024]{2,1,0:T(8,128)(2,1)S(1)}, u32[]{:S(2)}, u32[]{:S(2)}) async-start(bf16[8,64,1024]{2,1,0:T(8,128)(2,1)} %broadcast_in_dim.26), calls=%async_computation.1 | async-start | bytes 2097152 | tf_op jit(solution)/shard_map/all_to_all | solution.py:15
  53.1 0.1 fusion.18
  53.2 2.7 %collective-permute-start = (bf16[128,1024]{0,1:T(8,128)(2,1)S(1)}, bf16[128,1024]{0,1:T(8,128)(2,1)S(1)}, u32[]{:S(2)}, u32[]{:S(2)}) collective-permute-start(bf16[128,1024]{0,1:T(8,128)(2,1)S(1)} %fusion.18), channel_id=1, source_target_pairs={{0,768},{256,0},{512,256},{768,512},{1,769},{257,1},{513,257},{769... | collective-permute-start | bytes 786440 | tf_op jit(solution)/shard_map/ppermute | solution.py:30
  55.9 0.1 iota_add_fusion.2
  56.0 3.0 %collective-permute-start.1 = (bf16[128,1024]{0,1:T(8,128)(2,1)S(1)}, bf16[128,1024]{0,1:T(8,128)(2,1)S(1)}, u32[]{:S(2)}, u32[]{:S(2)}) collective-permute-start(bf16[128,1024]{0,1:T(8,128)(2,1)S(1)} %fusion.18), channel_id=1, source_target_pairs={{0,512},{256,768},{512,0},{768,256},{1,513},{257,769},{513,1},{769... | collective-permute-start | bytes 786440 | tf_op jit(solution)/shard_map/ppermute | solution.py:30
  59.0 4.0 %collective-permute-start.2 = (bf16[128,1024]{0,1:T(8,128)(2,1)S(1)}, bf16[128,1024]{0,1:T(8,128)(2,1)S(1)}, u32[]{:S(2)}, u32[]{:S(2)}) collective-permute-start(bf16[128,1024]{0,1:T(8,128)(2,1)S(1)} %fusion.18), channel_id=1, source_target_pairs={{0,256},{256,512},{512,768},{768,0},{1,257},{257,513},{513,769},{7... | collective-permute-start | bytes 786440 | tf_op jit(solution)/shard_map/ppermute | solution.py:30
  63.0 0.1 broadcast_select_fusion.4
  63.1 0.0 collective-permute-done
  63.2 2.6 %collective-permute-done.1 = bf16[128,1024]{0,1:T(8,128)(2,1)S(1)} collective-permute-done((bf16[128,1024]{0,1:T(8,128)(2,1)S(1)}, bf16[128,1024]{0,1:T(8,128)(2,1)S(1)}, u32[]{:S(2)}, u32[]{:S(2)}) %collective-permute-start.1) | collective-permute-done | bytes 262176 | tf_op jit(solution)/shard_map/ppermute | solution.py:30
  65.8 0.1 constant_dynamic-update-slice_fusion.5
  65.8 2.5 %collective-permute-done.2 = bf16[128,1024]{0,1:T(8,128)(2,1)S(1)} collective-permute-done((bf16[128,1024]{0,1:T(8,128)(2,1)S(1)}, bf16[128,1024]{0,1:T(8,128)(2,1)S(1)}, u32[]{:S(2)}, u32[]{:S(2)}) %collective-permute-start.2) | collective-permute-done | bytes 262176 | tf_op jit(solution)/shard_map/ppermute | solution.py:30
  68.3 0.1 constant_dynamic-update-slice_fusion.4
  68.4 0.1 constant_dynamic-update-slice_fusion.3
  68.5 0.1 constant_dynamic-update-slice_fusion.2
  68.5 0.1 constant_dynamic-update-slice_fusion.1
  68.6 0.1 constant_dynamic-update-slice_fusion
  68.7 0.1 constant_dynamic-slice_fusion.2
  68.8 6.9 %all-to-all-done.1 = bf16[8,64,1024]{2,1,0:T(8,128)(2,1)S(1)} async-done(((bf16[8,64,1024]{2,1,0:T(8,128)(2,1)}), bf16[8,64,1024]{2,1,0:T(8,128)(2,1)S(1)}, u32[]{:S(2)}, u32[]{:S(2)}) %all-to-all-start.1) | async-done | bytes 1048608 | tf_op jit(solution)/shard_map/all_to_all | solution.py:15
  75.6 1.9 %collective-permute-start.3 = (bf16[512,1024]{1,0:T(8,128)(2,1)S(1)}, bf16[512,1024]{1,0:T(8,128)(2,1)S(1)}, u32[]{:S(2)}, u32[]{:S(2)}) collective-permute-start(bf16[512,1024]{1,0:T(8,128)(2,1)S(1)} %bitcast.81), channel_id=1, source_target_pairs={{0,16},{16,0},{1,17},{17,1},{2,18},{18,2},{3,19},{19,3},{4,20},{20... | collective-permute-start | bytes 3145736 | tf_op jit(solution)/shard_map/ppermute | solution.py:25
  78.9 1.0 fusion.16
  79.9 0.7 fusion.30
  80.6 0.0 collective-permute-done.3
  80.6 1.0 fusion.17
  81.7 0.7 fusion.31
  82.4 1.5 %add_convert_fusion = f16[512,1024]{1,0:T(8,128)(2,1)} fusion(f32[512,1024]{1,0:T(8,128)S(1)} %fusion.30, f32[512,1024]{1,0:T(8,128)S(1)} %fusion.31), kind=kLoop, calls=%fused_computation.1 | loop fusion | flops 1048576 | bytes 5242880 | tf_op jit(solution)/shard_map/convert_element_type | solution.py:138
  83.9 4.8 %all-to-all-start.2 = ((f16[4,128,1024]{2,1,0:T(8,128)(2,1)}), f16[4,128,1024]{2,1,0:T(8,128)(2,1)S(1)}, u32[]{:S(2)}, u32[]{:S(2)}) async-start(f16[4,128,1024]{2,1,0:T(8,128)(2,1)} %bitcast.21), calls=%async_computation.2 | async-start | bytes 2097152 | tf_op jit(solution)/shard_map/all_to_all | solution.py:21
  88.7 0.1 copy.40
  88.8 13.6 %all-to-all-done.2 = f16[4,128,1024]{2,1,0:T(8,128)(2,1)S(1)} async-done(((f16[4,128,1024]{2,1,0:T(8,128)(2,1)}), f16[4,128,1024]{2,1,0:T(8,128)(2,1)S(1)}, u32[]{:S(2)}, u32[]{:S(2)}) %all-to-all-start.2) | async-done | bytes 1048608 | tf_op jit(solution)/shard_map/all_to_all | solution.py:21
  102.4 0.2 convert_reduce_fusion
  102.6 0.2 copy.39
  102.8 0.2 multiply_reduce_fusion
  103.0 0.1 fusion.20
  103.2 0.2 pad_maximum_fusion
  103.3 0.4 copy.41
  103.8 27.5 %all_to_all.20 = f16[8,136,128]{2,1,0:T(8,128)(2,1)S(1)} all-to-all(f16[8,136,128]{2,1,0:T(8,128)(2,1)S(1)} %copy.41), channel_id=1, replica_groups=mesh['x'=4,'y'=8,'c'=2,'zl'=8,'zh'=2] {'zl'}, dimensions={0} | all-to-all | bytes 557056 | tf_op jit(solution)/shard_map/all_to_all | solution.py:144
  131.3 0.1 slice.36
  131.4 0.5 convert_reduce_fusion.1
  132.0 0.8 bitcast_divide_fusion.3
  (28 shorter events, 0.4 us)
Async XLA Ops:
  0.0 1.6 %copy-start = (bf16[256,1536]{1,0:T(8,128)(2,1)S(1)}, bf16[256,1536]{1,0:T(8,128)(2,1)}, u32[]{:S(2)}) copy-start(bf16[256,1536]{1,0:T(8,128)(2,1)} %param.7) | copy-start | bytes 2359300
  1.6 18.5 %copy-start.1 = (s32[16384]{0:T(1024)S(1)}, s32[16384]{0:T(1024)}, u32[]{:S(2)}) copy-start(s32[16384]{0:T(1024)} %param.11) | copy-start | bytes 196612
  4.4 39.5 %all-to-all-start = ((f16[8,200,128]{2,1,0:T(8,128)(2,1)}), f16[8,200,128]{2,1,0:T(8,128)(2,1)S(1)}, u32[]{:S(2)}, u32[]{:S(2)}) async-start(f16[8,200,128]{2,1,0:T(8,128)(2,1)} %pad_maximum_fusion.1), calls=%async_computation | async-start | bytes 819200 | tf_op jit(solution)/shard_map/all_to_all | solution.py:93
  46.0 29.6 %all-to-all-start.1 = ((bf16[8,64,1024]{2,1,0:T(8,128)(2,1)}), bf16[8,64,1024]{2,1,0:T(8,128)(2,1)S(1)}, u32[]{:S(2)}, u32[]{:S(2)}) async-start(bf16[8,64,1024]{2,1,0:T(8,128)(2,1)} %broadcast_in_dim.26), calls=%async_computation.1 | async-start | bytes 2097152 | tf_op jit(solution)/shard_map/all_to_all | solution.py:15
  53.2 9.9 %collective-permute-start = (bf16[128,1024]{0,1:T(8,128)(2,1)S(1)}, bf16[128,1024]{0,1:T(8,128)(2,1)S(1)}, u32[]{:S(2)}, u32[]{:S(2)}) collective-permute-start(bf16[128,1024]{0,1:T(8,128)(2,1)S(1)} %fusion.18), channel_id=1, source_target_pairs={{0,768},{256,0},{512,256},{768,512},{1,769},{257,1},{513,257},{769... | collective-permute-start | bytes 786440 | tf_op jit(solution)/shard_map/ppermute | solution.py:30
  56.0 9.8 %collective-permute-start.1 = (bf16[128,1024]{0,1:T(8,128)(2,1)S(1)}, bf16[128,1024]{0,1:T(8,128)(2,1)S(1)}, u32[]{:S(2)}, u32[]{:S(2)}) collective-permute-start(bf16[128,1024]{0,1:T(8,128)(2,1)S(1)} %fusion.18), channel_id=1, source_target_pairs={{0,512},{256,768},{512,0},{768,256},{1,513},{257,769},{513,1},{769... | collective-permute-start | bytes 786440 | tf_op jit(solution)/shard_map/ppermute | solution.py:30
  59.0 9.3 %collective-permute-start.2 = (bf16[128,1024]{0,1:T(8,128)(2,1)S(1)}, bf16[128,1024]{0,1:T(8,128)(2,1)S(1)}, u32[]{:S(2)}, u32[]{:S(2)}) collective-permute-start(bf16[128,1024]{0,1:T(8,128)(2,1)S(1)} %fusion.18), channel_id=1, source_target_pairs={{0,256},{256,512},{512,768},{768,0},{1,257},{257,513},{513,769},{7... | collective-permute-start | bytes 786440 | tf_op jit(solution)/shard_map/ppermute | solution.py:30
  75.6 5.0 %collective-permute-start.3 = (bf16[512,1024]{1,0:T(8,128)(2,1)S(1)}, bf16[512,1024]{1,0:T(8,128)(2,1)S(1)}, u32[]{:S(2)}, u32[]{:S(2)}) collective-permute-start(bf16[512,1024]{1,0:T(8,128)(2,1)S(1)} %bitcast.81), channel_id=1, source_target_pairs={{0,16},{16,0},{1,17},{17,1},{2,18},{18,2},{3,19},{19,3},{4,20},{20... | collective-permute-start | bytes 3145736 | tf_op jit(solution)/shard_map/ppermute | solution.py:25
  83.9 18.5 %all-to-all-start.2 = ((f16[4,128,1024]{2,1,0:T(8,128)(2,1)}), f16[4,128,1024]{2,1,0:T(8,128)(2,1)S(1)}, u32[]{:S(2)}, u32[]{:S(2)}) async-start(f16[4,128,1024]{2,1,0:T(8,128)(2,1)} %bitcast.21), calls=%async_computation.2 | async-start | bytes 2097152 | tf_op jit(solution)/shard_map/all_to_all | solution.py:21

commit v11 on v10

--- a/solution.py
+++ b/solution.py
@@ -63,8 +63,6 @@
     is_image = lax.axis_index("zh") == 0
     plane = lax.axis_index("zl")
     own_part, other_part = plane // 4, plane % 4
-    scale = jnp.exp(log_scale[0])
-    offset = bias[0]
 
     text_cols = jnp.dot(text_features, text_head, preferred_element_type=F32)
     text_cols, image_features = lax.optimization_barrier((text_cols, image_features))
@@ -122,6 +120,12 @@
         lane = core * rows + other_part * others
         return keys((x, 0), (1, 8), lane, others, ~is_image).reshape(-1, 1)
 
+    near_b, own_b, own_keys, near_keys, far_keys, scale, offset = lax.optimization_barrier(
+        (near_b, own_b, own_keys, other_keys(c), other_keys(1 - c), jnp.exp(log_scale), bias)
+    )
+    scale, offset = scale[0], offset[0]
+    far_b = swapped(near_b)
+
     def gradient(b, key):
         logits = scale * jnp.einsum("ce,re->cr", b, own_b, preferred_element_type=F32) + offset
         sign = jnp.where(own_keys == key, 1.0, -1.0)
@@ -129,10 +133,6 @@
         weight = lax.optimization_barrier(weight)
         return jnp.einsum("cr,ce->re", weight, b, preferred_element_type=F32)
 
-    near_b, own_b, own_keys, near_keys, far_keys = lax.optimization_barrier(
-        (near_b, own_b, own_keys, other_keys(c), other_keys(1 - c))
-    )
-    far_b = swapped(near_b)
     grad = gradient(near_b, near_keys)
     grad, far_b, far_keys = lax.optimization_barrier((grad, far_b, far_keys))
     grad = summed((grad + gradient(far_b, far_keys)).astype(HALF), "x")

time: 134 us -> 133 us (level)
  transfers between devices with their start and end apart: 7 -> 7, of which waited for: 5 -> 6; matrix products, arithmetic and copies ran while one was open for 2% -> 2% of each run, Pallas kernels for 0% -> 0%
where the time goes in v11:
time: 133 us; the launch traced here: 132 us
  waiting for transfers between devices  48 us (36%)
  starting transfers between devices  39.2 us (29%)
  blocking collectives  27.3 us (21%)
  matrix products  6.41 us (5%)
  other arithmetic  5.67 us (4%)
  local copies, waits for them, and re-layouts  3.45 us (3%)
  between operations  1.72 us (1%)
    all_to_all x1, blocking collectives, shards(): pieces = lax.all_to_all(pieces, 'zl', 0, 0, tiled=True)  27.3 us
    all_to_all x1, waiting for transfers between devices, shards(): pieces = lax.all_to_all(pieces, 'zl', 0, 0, tiled=True)  23.2 us
    all_to_all x1, starting transfers between devices, shards(): pieces = lax.all_to_all(pieces, 'zl', 0, 0, tiled=True)  15.7 us
    all_to_all x1, waiting for transfers between devices, summed(): lax.all_to_all(parts, axis, 0, 0, tiled=True).astype(F32)  13.3 us
    ppermute x3, starting transfers between devices, shifted(): lax.ppermute(value, axis, [(k, (k + steps) % count) for k in range(count)])  9.75 us
    all_to_all x1, starting transfers between devices, spread(): return lax.all_to_all(copies, axis, 0, 0, tiled=True)  7.1 us
    all_to_all x1, waiting for transfers between devices, spread(): return lax.all_to_all(copies, axis, 0, 0, tiled=True)  6.87 us
    all_to_all x1, starting transfers between devices, summed(): lax.all_to_all(parts, axis, 0, 0, tiled=True).astype(F32)  4.77 us
  transfers between devices with their start and end apart: 7, of which 6 were waited for; matrix products, arithmetic and copies ran while one was open for 2% of the time, Pallas kernels for 0%

profile of v11, /device:TPU:6, one launch (start us, length us, event | category | flops | bytes accessed | tf_op | source)
XLA Modules:
  0.0 131.8 jit_solution(18446180774598286553)
XLA Ops:
  0.0 0.0 copy-start
  0.0 1.5 %fusion.29 = f32[256,128]{1,0:T(8,128)S(1)} fusion(bf16[256,1024]{1,0:T(8,128)(2,1)} %param.8, bf16[1024,128]{1,0:T(8,128)(2,1)} %param.10), kind=kOutput, calls=%fused_computation.89 | convolution fusion | flops 67108864 | bytes 917504 | tf_op jit(solution)/shard_map/dot_general | solution.py:67
  1.5 0.1 abs_reduce_fusion
  1.6 0.0 copy-done
  1.6 0.0 copy-start.1
  1.6 1.5 %abs_reduce_fusion.1 = (f32[256]{0:T(256)S(1)}, f32[256,128]{1,0:T(8,128)S(1)}) fusion(bf16[256,1536]{1,0:T(8,128)(2,1)S(1)} %copy-done, bf16[1536,128]{1,0:T(8,128)(2,1)} %param.9), kind=kOutput, calls=%fused_computation.44 | convolution fusion | flops 100728576 | bytes 1311744 | tf_op jit(solution)/shard_map/dot_general | solution.py:69
  3.1 0.1 reshape.522
  3.3 0.1 broadcast_select_fusion.1
  3.5 0.9 pad_maximum_fusion.1
  4.4 15.7 %all-to-all-start = ((f16[8,200,128]{2,1,0:T(8,128)(2,1)}), f16[8,200,128]{2,1,0:T(8,128)(2,1)S(1)}, u32[]{:S(2)}, u32[]{:S(2)}) async-start(f16[8,200,128]{2,1,0:T(8,128)(2,1)} %pad_maximum_fusion.1), calls=%async_computation | async-start | bytes 819200 | tf_op jit(solution)/shard_map/all_to_all | solution.py:91
  20.1 0.0 copy-done.1
  20.1 0.1 constant_dynamic-slice_fusion
  20.2 0.1 reshape.497
  20.3 0.1 iota_add_fusion
  20.4 0.1 add.305
  20.4 0.1 reshape.496
  20.5 0.1 iota_add_fusion.1
  20.6 0.1 add.297
  20.7 23.2 %all-to-all-done = f16[8,200,128]{2,1,0:T(8,128)(2,1)S(1)} async-done(((f16[8,200,128]{2,1,0:T(8,128)(2,1)}), f16[8,200,128]{2,1,0:T(8,128)(2,1)S(1)}, u32[]{:S(2)}, u32[]{:S(2)}) %all-to-all-start) | async-done | bytes 409632 | tf_op jit(solution)/shard_map/all_to_all | solution.py:91
  43.9 0.1 slice.34
  44.0 0.3 copy.46
  44.2 0.2 fusion.19
  44.5 0.2 fusion.22
  44.7 0.2 fusion.21
  44.9 1.1 broadcast_in_dim.26
  46.0 7.1 %all-to-all-start.1 = ((bf16[8,64,1024]{2,1,0:T(8,128)(2,1)}), bf16[8,64,1024]{2,1,0:T(8,128)(2,1)S(1)}, u32[]{:S(2)}, u32[]{:S(2)}) async-start(bf16[8,64,1024]{2,1,0:T(8,128)(2,1)} %broadcast_in_dim.26), calls=%async_computation.1 | async-start | bytes 2097152 | tf_op jit(solution)/shard_map/all_to_all | solution.py:15
  53.1 0.1 fusion.18
  53.2 2.7 %collective-permute-start = (bf16[128,1024]{0,1:T(8,128)(2,1)S(1)}, bf16[128,1024]{0,1:T(8,128)(2,1)S(1)}, u32[]{:S(2)}, u32[]{:S(2)}) collective-permute-start(bf16[128,1024]{0,1:T(8,128)(2,1)S(1)} %fusion.18), channel_id=1, source_target_pairs={{0,768},{256,0},{512,256},{768,512},{1,769},{257,1},{513,257},{769... | collective-permute-start | bytes 786440 | tf_op jit(solution)/shard_map/ppermute | solution.py:30
  55.9 0.1 iota_add_fusion.2
  56.0 3.0 %collective-permute-start.1 = (bf16[128,1024]{0,1:T(8,128)(2,1)S(1)}, bf16[128,1024]{0,1:T(8,128)(2,1)S(1)}, u32[]{:S(2)}, u32[]{:S(2)}) collective-permute-start(bf16[128,1024]{0,1:T(8,128)(2,1)S(1)} %fusion.18), channel_id=1, source_target_pairs={{0,512},{256,768},{512,0},{768,256},{1,513},{257,769},{513,1},{769... | collective-permute-start | bytes 786440 | tf_op jit(solution)/shard_map/ppermute | solution.py:30
  59.0 4.0 %collective-permute-start.2 = (bf16[128,1024]{0,1:T(8,128)(2,1)S(1)}, bf16[128,1024]{0,1:T(8,128)(2,1)S(1)}, u32[]{:S(2)}, u32[]{:S(2)}) collective-permute-start(bf16[128,1024]{0,1:T(8,128)(2,1)S(1)} %fusion.18), channel_id=1, source_target_pairs={{0,256},{256,512},{512,768},{768,0},{1,257},{257,513},{513,769},{7... | collective-permute-start | bytes 786440 | tf_op jit(solution)/shard_map/ppermute | solution.py:30
  63.0 0.1 broadcast_select_fusion.4
  63.8 0.0 collective-permute-done
  63.9 1.9 %collective-permute-done.1 = bf16[128,1024]{0,1:T(8,128)(2,1)S(1)} collective-permute-done((bf16[128,1024]{0,1:T(8,128)(2,1)S(1)}, bf16[128,1024]{0,1:T(8,128)(2,1)S(1)}, u32[]{:S(2)}, u32[]{:S(2)}) %collective-permute-start.1) | collective-permute-done | bytes 262176 | tf_op jit(solution)/shard_map/ppermute | solution.py:30
  65.8 0.1 constant_dynamic-update-slice_fusion.5
  65.8 2.5 %collective-permute-done.2 = bf16[128,1024]{0,1:T(8,128)(2,1)S(1)} collective-permute-done((bf16[128,1024]{0,1:T(8,128)(2,1)S(1)}, bf16[128,1024]{0,1:T(8,128)(2,1)S(1)}, u32[]{:S(2)}, u32[]{:S(2)}) %collective-permute-start.2) | collective-permute-done | bytes 262176 | tf_op jit(solution)/shard_map/ppermute | solution.py:30
  68.3 0.1 constant_dynamic-update-slice_fusion.4
  68.4 0.1 constant_dynamic-update-slice_fusion.3
  68.5 0.1 constant_dynamic-update-slice_fusion.2
  68.5 0.1 constant_dynamic-update-slice_fusion.1
  68.6 0.1 constant_dynamic-update-slice_fusion
  68.7 0.1 constant_dynamic-slice_fusion.2
  68.8 6.9 %all-to-all-done.1 = bf16[8,64,1024]{2,1,0:T(8,128)(2,1)S(1)} async-done(((bf16[8,64,1024]{2,1,0:T(8,128)(2,1)}), bf16[8,64,1024]{2,1,0:T(8,128)(2,1)S(1)}, u32[]{:S(2)}, u32[]{:S(2)}) %all-to-all-start.1) | async-done | bytes 1048608 | tf_op jit(solution)/shard_map/all_to_all | solution.py:15
  75.6 1.9 %collective-permute-start.3 = (bf16[512,1024]{1,0:T(8,128)(2,1)S(1)}, bf16[512,1024]{1,0:T(8,128)(2,1)S(1)}, u32[]{:S(2)}, u32[]{:S(2)}) collective-permute-start(bf16[512,1024]{1,0:T(8,128)(2,1)S(1)} %bitcast.81), channel_id=1, source_target_pairs={{0,16},{16,0},{1,17},{17,1},{2,18},{18,2},{3,19},{19,3},{4,20},{20... | collective-permute-start | bytes 3145736 | tf_op jit(solution)/shard_map/ppermute | solution.py:25
  78.2 1.0 fusion.16
  79.2 0.7 fusion.30
  79.9 0.2 collective-permute-done.3
  80.2 1.0 fusion.17
  81.2 0.7 fusion.31
  81.9 1.5 %add_convert_fusion = f16[512,1024]{1,0:T(8,128)(2,1)} fusion(f32[512,1024]{1,0:T(8,128)S(1)} %fusion.30, f32[512,1024]{1,0:T(8,128)S(1)} %fusion.31), kind=kLoop, calls=%fused_computation.1 | loop fusion | flops 1048576 | bytes 5242880 | tf_op jit(solution)/shard_map/convert_element_type | solution.py:138
  83.4 4.8 %all-to-all-start.2 = ((f16[4,128,1024]{2,1,0:T(8,128)(2,1)}), f16[4,128,1024]{2,1,0:T(8,128)(2,1)S(1)}, u32[]{:S(2)}, u32[]{:S(2)}) async-start(f16[4,128,1024]{2,1,0:T(8,128)(2,1)} %bitcast.21), calls=%async_computation.2 | async-start | bytes 2097152 | tf_op jit(solution)/shard_map/all_to_all | solution.py:21
  88.2 0.1 copy.40
  88.3 13.3 %all-to-all-done.2 = f16[4,128,1024]{2,1,0:T(8,128)(2,1)S(1)} async-done(((f16[4,128,1024]{2,1,0:T(8,128)(2,1)}), f16[4,128,1024]{2,1,0:T(8,128)(2,1)S(1)}, u32[]{:S(2)}, u32[]{:S(2)}) %all-to-all-start.2) | async-done | bytes 1048608 | tf_op jit(solution)/shard_map/all_to_all | solution.py:21
  101.7 0.2 convert_reduce_fusion
  101.9 0.2 copy.39
  102.1 0.2 multiply_reduce_fusion
  102.3 0.1 fusion.20
  102.5 0.2 pad_maximum_fusion
  102.7 0.4 copy.41
  103.1 27.3 %all_to_all.20 = f16[8,136,128]{2,1,0:T(8,128)(2,1)S(1)} all-to-all(f16[8,136,128]{2,1,0:T(8,128)(2,1)S(1)} %copy.41), channel_id=1, replica_groups=mesh['x'=4,'y'=8,'c'=2,'zl'=8,'zh'=2] {'zl'}, dimensions={0} | all-to-all | bytes 557056 | tf_op jit(solution)/shard_map/all_to_all | solution.py:144
  130.4 0.1 slice.36
  130.5 0.5 convert_reduce_fusion.1
  131.0 0.8 bitcast_divide_fusion.3
  (28 shorter events, 0.4 us)
Async XLA Ops:
  0.0 1.6 %copy-start = (bf16[256,1536]{1,0:T(8,128)(2,1)S(1)}, bf16[256,1536]{1,0:T(8,128)(2,1)}, u32[]{:S(2)}) copy-start(bf16[256,1536]{1,0:T(8,128)(2,1)} %param.7) | copy-start | bytes 2359300
  1.6 18.5 %copy-start.1 = (s32[16384]{0:T(1024)S(1)}, s32[16384]{0:T(1024)}, u32[]{:S(2)}) copy-start(s32[16384]{0:T(1024)} %param.11) | copy-start | bytes 196612
  4.4 39.5 %all-to-all-start = ((f16[8,200,128]{2,1,0:T(8,128)(2,1)}), f16[8,200,128]{2,1,0:T(8,128)(2,1)S(1)}, u32[]{:S(2)}, u32[]{:S(2)}) async-start(f16[8,200,128]{2,1,0:T(8,128)(2,1)} %pad_maximum_fusion.1), calls=%async_computation | async-start | bytes 819200 | tf_op jit(solution)/shard_map/all_to_all | solution.py:91
  46.0 29.6 %all-to-all-start.1 = ((bf16[8,64,1024]{2,1,0:T(8,128)(2,1)}), bf16[8,64,1024]{2,1,0:T(8,128)(2,1)S(1)}, u32[]{:S(2)}, u32[]{:S(2)}) async-start(bf16[8,64,1024]{2,1,0:T(8,128)(2,1)} %broadcast_in_dim.26), calls=%async_computation.1 | async-start | bytes 2097152 | tf_op jit(solution)/shard_map/all_to_all | solution.py:15
  53.2 10.6 %collective-permute-start = (bf16[128,1024]{0,1:T(8,128)(2,1)S(1)}, bf16[128,1024]{0,1:T(8,128)(2,1)S(1)}, u32[]{:S(2)}, u32[]{:S(2)}) collective-permute-start(bf16[128,1024]{0,1:T(8,128)(2,1)S(1)} %fusion.18), channel_id=1, source_target_pairs={{0,768},{256,0},{512,256},{768,512},{1,769},{257,1},{513,257},{769... | collective-permute-start | bytes 786440 | tf_op jit(solution)/shard_map/ppermute | solution.py:30
  56.0 9.8 %collective-permute-start.1 = (bf16[128,1024]{0,1:T(8,128)(2,1)S(1)}, bf16[128,1024]{0,1:T(8,128)(2,1)S(1)}, u32[]{:S(2)}, u32[]{:S(2)}) collective-permute-start(bf16[128,1024]{0,1:T(8,128)(2,1)S(1)} %fusion.18), channel_id=1, source_target_pairs={{0,512},{256,768},{512,0},{768,256},{1,513},{257,769},{513,1},{769... | collective-permute-start | bytes 786440 | tf_op jit(solution)/shard_map/ppermute | solution.py:30
  59.0 9.3 %collective-permute-start.2 = (bf16[128,1024]{0,1:T(8,128)(2,1)S(1)}, bf16[128,1024]{0,1:T(8,128)(2,1)S(1)}, u32[]{:S(2)}, u32[]{:S(2)}) collective-permute-start(bf16[128,1024]{0,1:T(8,128)(2,1)S(1)} %fusion.18), channel_id=1, source_target_pairs={{0,256},{256,512},{512,768},{768,0},{1,257},{257,513},{513,769},{7... | collective-permute-start | bytes 786440 | tf_op jit(solution)/shard_map/ppermute | solution.py:30
  75.6 4.5 %collective-permute-start.3 = (bf16[512,1024]{1,0:T(8,128)(2,1)S(1)}, bf16[512,1024]{1,0:T(8,128)(2,1)S(1)}, u32[]{:S(2)}, u32[]{:S(2)}) collective-permute-start(bf16[512,1024]{1,0:T(8,128)(2,1)S(1)} %bitcast.81), channel_id=1, source_target_pairs={{0,16},{16,0},{1,17},{17,1},{2,18},{18,2},{3,19},{19,3},{4,20},{20... | collective-permute-start | bytes 3145736 | tf_op jit(solution)/shard_map/ppermute | solution.py:25
  83.4 18.2 %all-to-all-start.2 = ((f16[4,128,1024]{2,1,0:T(8,128)(2,1)}), f16[4,128,1024]{2,1,0:T(8,128)(2,1)S(1)}, u32[]{:S(2)}, u32[]{:S(2)}) async-start(f16[4,128,1024]{2,1,0:T(8,128)(2,1)} %bitcast.21), calls=%async_computation.2 | async-start | bytes 2097152 | tf_op jit(solution)/shard_map/all_to_all | solution.py:21

commit v12 on v11

--- a/solution.py
+++ b/solution.py
@@ -32,14 +32,6 @@
 
 def exponent(value):
     return jnp.clip(jnp.floor(jnp.log2(jnp.maximum(value, 1e-30))), -100.0, 126.0)
-
-
-def with_exponents(rows, powers):
-    count, width = rows.shape[-2:]
-    lead = [(0, 0)] * (powers.ndim - 1)
-    powers = jnp.pad(powers[..., None, :], lead + [(0, 7), (0, width - count)])
-    powers = jnp.broadcast_to(powers, rows.shape[:-2] + (8, width))
-    return jnp.concatenate([rows.astype(HALF), powers.astype(HALF)], axis=-2)
 
 
 def without_exponents(pieces, count):
@@ -135,12 +127,16 @@
 
     grad = gradient(near_b, near_keys)
     grad, far_b, far_keys = lax.optimization_barrier((grad, far_b, far_keys))
-    grad = summed((grad + gradient(far_b, far_keys)).astype(HALF), "x")
+    grad = (grad + gradient(far_b, far_keys)).astype(HALF)
 
     powers = exponent(own_norm) - 3.0
-    grad = projected(grad, own_unit) * (jnp.exp2(powers) / own_norm)
-    grad = grad.reshape(owns, lanes, width).transpose(1, 0, 2)
-    pieces = with_exponents(grad, powers.reshape(1, owns))
+    factors = jnp.exp2(powers) / own_norm
+    power_rows = jnp.pad(powers.reshape(1, owns), ((0, 7), (0, width - owns))).astype(HALF)
+    power_rows = jnp.broadcast_to(power_rows, (lanes, 8, width))
+    grad, factors, power_rows = lax.optimization_barrier((grad, factors, power_rows))
+    grad = projected(summed(grad, "x"), own_unit) * factors
+    grad = grad.reshape(owns, lanes, width).transpose(1, 0, 2).astype(HALF)
+    pieces = jnp.concatenate([grad, power_rows], axis=1)
     pieces = lax.all_to_all(pieces, "zl", 0, 0, tiled=True)
     grad, powers = without_exponents(pieces.reshape(2, 4, owns + 8, width), owns)
     grad = jnp.sum(grad, axis=1) / jnp.exp2(powers[:, 0])[..., None]

time: 133 us -> 134 us (level)
  blocking collectives: 27.3 us -> 45.8 us
  waiting for transfers between devices: 48 us -> 32.3 us
  starting transfers between devices: 39.2 us -> 34.5 us
  local copies, waits for them, and re-layouts: 3.45 us -> 5.31 us
    all_to_all x0 -> x1, blocking collectives: none -> 18.3 us  [summed(): lax.all_to_all(parts, axis, 0, 0, tiled=True).astype(F32)]
    all_to_all x1 -> x0, waiting for transfers between devices: 13.3 us -> none  [summed(): lax.all_to_all(parts, axis, 0, 0, tiled=True).astype(F32)]
    all_to_all x1 -> x0, starting transfers between devices: 4.77 us -> none  [summed(): lax.all_to_all(parts, axis, 0, 0, tiled=True).astype(F32)]
  transfers between devices with their start and end apart: 7 -> 6, of which waited for: 6 -> 4; matrix products, arithmetic and copies ran while one was open for 2% -> 5% of each run, Pallas kernels for 0% -> 0%
where the time goes in v12:
time: 134 us; the launch traced here: 133 us
  blocking collectives  45.8 us (34%)
  starting transfers between devices  34.5 us (26%)
  waiting for transfers between devices  32.3 us (24%)
  matrix products  7.64 us (6%)
  other arithmetic  5.82 us (4%)
  local copies, waits for them, and re-layouts  5.31 us (4%)
  between operations  1.78 us (1%)
    all_to_all x1, blocking collectives, shards(): pieces = lax.all_to_all(pieces, 'zl', 0, 0, tiled=True)  27.5 us
    all_to_all x1, waiting for transfers between devices, shards(): pieces = lax.all_to_all(pieces, 'zl', 0, 0, tiled=True)  22.1 us
    all_to_all x1, blocking collectives, summed(): lax.all_to_all(parts, axis, 0, 0, tiled=True).astype(F32)  18.3 us
    all_to_all x1, starting transfers between devices, shards(): pieces = lax.all_to_all(pieces, 'zl', 0, 0, tiled=True)  15.7 us
    ppermute x3, starting transfers between devices, shifted(): lax.ppermute(value, axis, [(k, (k + steps) % count) for k in range(count)])  9.75 us
    all_to_all x1, starting transfers between devices, spread(): return lax.all_to_all(copies, axis, 0, 0, tiled=True)  7.1 us
    all_to_all x1, waiting for transfers between devices, spread(): return lax.all_to_all(copies, axis, 0, 0, tiled=True)  5.88 us
    ppermute x3, waiting for transfers between devices, shifted(): lax.ppermute(value, axis, [(k, (k + steps) % count) for k in range(count)])  4.37 us
  transfers between devices with their start and end apart: 6, of which 4 were waited for; matrix products, arithmetic and copies ran while one was open for 5% of the time, Pallas kernels for 0%

profile of v12, /device:TPU:6, one launch (start us, length us, event | category | flops | bytes accessed | tf_op | source)
XLA Modules:
  0.0 133.1 jit_solution(15526987759570178324)
XLA Ops:
  0.0 1.5 %fusion.36 = f32[256,128]{1,0:T(8,128)S(1)} fusion(bf16[256,1024]{1,0:T(8,128)(2,1)} %param.8, bf16[1024,128]{1,0:T(8,128)(2,1)} %param.10), kind=kOutput, calls=%fused_computation.95 | convolution fusion | flops 67108864 | bytes 917504 | tf_op jit(solution)/shard_map/dot_general | solution.py:59
  1.5 0.1 abs_reduce_fusion
  1.6 0.0 copy-start.4
  1.6 1.5 %abs_reduce_fusion.1 = (f32[256]{0:T(256)S(1)}, f32[256,128]{1,0:T(8,128)S(1)}) fusion(bf16[256,1536]{1,0:T(8,128)(2,1)S(1)} %copy-done, bf16[1536,128]{1,0:T(8,128)(2,1)} %param.9), kind=kOutput, calls=%fused_computation.44 | convolution fusion | flops 100728576 | bytes 1311744 | tf_op jit(solution)/shard_map/dot_general | solution.py:61
  3.1 0.1 reshape.549
  3.3 0.1 broadcast_select_fusion.1
  3.5 0.9 pad_maximum_fusion.1
  4.4 15.7 %all-to-all-start = ((f16[8,200,128]{2,1,0:T(8,128)(2,1)}), f16[8,200,128]{2,1,0:T(8,128)(2,1)S(1)}, u32[]{:S(2)}, u32[]{:S(2)}) async-start(f16[8,200,128]{2,1,0:T(8,128)(2,1)} %pad_maximum_fusion.1), calls=%async_computation | async-start | bytes 819200 | tf_op jit(solution)/shard_map/all_to_all | solution.py:83
  20.1 0.1 constant_dynamic-slice_fusion
  20.2 0.1 reshape.524
  20.3 0.1 iota_add_fusion
  20.4 0.1 add.312
  20.4 0.1 reshape.523
  20.5 0.1 iota_add_fusion.1
  20.6 0.1 add.304
  20.7 0.6 broadcast_select_fusion.2
  21.3 0.6 broadcast_select_fusion.3
  21.8 22.1 %all-to-all-done = f16[8,200,128]{2,1,0:T(8,128)(2,1)S(1)} async-done(((f16[8,200,128]{2,1,0:T(8,128)(2,1)}), f16[8,200,128]{2,1,0:T(8,128)(2,1)S(1)}, u32[]{:S(2)}, u32[]{:S(2)}) %all-to-all-start) | async-done | bytes 409632 | tf_op jit(solution)/shard_map/all_to_all | solution.py:83
  43.9 0.1 slice.34
  44.0 0.3 copy.46
  44.3 0.0 copy-start.2
  44.3 0.2 fusion.19
  44.5 0.2 fusion.22
  44.7 0.1 copy-done.2
  44.9 0.1 fusion.21
  45.0 1.1 broadcast_in_dim.26
  46.2 7.1 %all-to-all-start.1 = ((bf16[8,64,1024]{2,1,0:T(8,128)(2,1)}), bf16[8,64,1024]{2,1,0:T(8,128)(2,1)S(1)}, u32[]{:S(2)}, u32[]{:S(2)}) async-start(bf16[8,64,1024]{2,1,0:T(8,128)(2,1)} %broadcast_in_dim.26), calls=%async_computation.1 | async-start | bytes 2097152 | tf_op jit(solution)/shard_map/all_to_all | solution.py:15
  53.3 0.1 fusion.18
  53.4 2.7 %collective-permute-start = (bf16[128,1024]{0,1:T(8,128)(2,1)S(1)}, bf16[128,1024]{0,1:T(8,128)(2,1)S(1)}, u32[]{:S(2)}, u32[]{:S(2)}) collective-permute-start(bf16[128,1024]{0,1:T(8,128)(2,1)S(1)} %fusion.18), channel_id=1, source_target_pairs={{0,768},{256,0},{512,256},{768,512},{1,769},{257,1},{513,257},{769... | collective-permute-start | bytes 786440 | tf_op jit(solution)/shard_map/ppermute | solution.py:30
  56.1 0.1 iota_add_fusion.2
  56.2 3.0 %collective-permute-start.1 = (bf16[128,1024]{0,1:T(8,128)(2,1)S(1)}, bf16[128,1024]{0,1:T(8,128)(2,1)S(1)}, u32[]{:S(2)}, u32[]{:S(2)}) collective-permute-start(bf16[128,1024]{0,1:T(8,128)(2,1)S(1)} %fusion.18), channel_id=1, source_target_pairs={{0,512},{256,768},{512,0},{768,256},{1,513},{257,769},{513,1},{769... | collective-permute-start | bytes 786440 | tf_op jit(solution)/shard_map/ppermute | solution.py:30
  59.2 4.0 %collective-permute-start.2 = (bf16[128,1024]{0,1:T(8,128)(2,1)S(1)}, bf16[128,1024]{0,1:T(8,128)(2,1)S(1)}, u32[]{:S(2)}, u32[]{:S(2)}) collective-permute-start(bf16[128,1024]{0,1:T(8,128)(2,1)S(1)} %fusion.18), channel_id=1, source_target_pairs={{0,256},{256,512},{512,768},{768,0},{1,257},{257,513},{513,769},{7... | collective-permute-start | bytes 786440 | tf_op jit(solution)/shard_map/ppermute | solution.py:30
  63.2 0.1 broadcast_select_fusion.4
  64.0 0.0 collective-permute-done
  64.0 1.9 %collective-permute-done.1 = bf16[128,1024]{0,1:T(8,128)(2,1)S(1)} collective-permute-done((bf16[128,1024]{0,1:T(8,128)(2,1)S(1)}, bf16[128,1024]{0,1:T(8,128)(2,1)S(1)}, u32[]{:S(2)}, u32[]{:S(2)}) %collective-permute-start.1) | collective-permute-done | bytes 262176 | tf_op jit(solution)/shard_map/ppermute | solution.py:30
  65.9 0.1 constant_dynamic-update-slice_fusion.5
  66.0 2.5 %collective-permute-done.2 = bf16[128,1024]{0,1:T(8,128)(2,1)S(1)} collective-permute-done((bf16[128,1024]{0,1:T(8,128)(2,1)S(1)}, bf16[128,1024]{0,1:T(8,128)(2,1)S(1)}, u32[]{:S(2)}, u32[]{:S(2)}) %collective-permute-start.2) | collective-permute-done | bytes 262176 | tf_op jit(solution)/shard_map/ppermute | solution.py:30
  68.5 0.1 constant_dynamic-update-slice_fusion.4
  68.5 0.1 constant_dynamic-update-slice_fusion.3
  68.6 0.1 constant_dynamic-update-slice_fusion.2
  68.7 0.1 constant_dynamic-update-slice_fusion.1
  68.8 0.1 constant_dynamic-update-slice_fusion
  68.8 1.1 constant_dynamic-slice_fusion.2
  69.9 5.9 %all-to-all-done.1 = bf16[8,64,1024]{2,1,0:T(8,128)(2,1)S(1)} async-done(((bf16[8,64,1024]{2,1,0:T(8,128)(2,1)}), bf16[8,64,1024]{2,1,0:T(8,128)(2,1)S(1)}, u32[]{:S(2)}, u32[]{:S(2)}) %all-to-all-start.1) | async-done | bytes 1048608 | tf_op jit(solution)/shard_map/all_to_all | solution.py:15
  75.8 1.9 %collective-permute-start.3 = (bf16[512,1024]{1,0:T(8,128)(2,1)S(1)}, bf16[512,1024]{1,0:T(8,128)(2,1)S(1)}, u32[]{:S(2)}, u32[]{:S(2)}) collective-permute-start(bf16[512,1024]{1,0:T(8,128)(2,1)S(1)} %bitcast.99), channel_id=1, source_target_pairs={{0,16},{16,0},{1,17},{17,1},{2,18},{18,2},{3,19},{19,3},{4,20},{20... | collective-permute-start | bytes 3145736 | tf_op jit(solution)/shard_map/ppermute | solution.py:25
  78.3 0.1 copy.50
  78.5 2.2 %fusion.16 = bf16[512,512]{1,0:T(8,128)(2,1)S(1)} fusion(bf16[512,1024]{1,0:T(8,128)(2,1)S(1)} %bitcast.100, bf16[512,1024]{0,1:T(8,128)(2,1)} %constant_dynamic-slice_fusion.2, f32[]{:T(128)} %bitcast.97, f32[]{:T(128)} %bitcast.18, s32[512]{0:T(512)S(1)} %bitcast.116, s32[512]{0:T(512)S(1)} %bitcast.115), kind=kOutput, calls=%fused_computation.20 | convolution fusion | flops 540016640 | bytes 2625544 | tf_op jit(solution)/shard_map/ce,re->cr/dot_general | solution.py:122
  80.8 0.7 fusion.37
  81.6 0.5 copy-done.1
  82.0 1.0 fusion.17
  83.0 0.7 fusion.38
  83.8 0.5 add_convert_fusion
  84.3 18.3 %all_to_all.20 = f16[4,128,1024]{2,1,0:T(8,128)(2,1)S(1)} all-to-all(f16[4,128,1024]{2,1,0:T(8,128)(2,1)S(1)} %bitcast.102), channel_id=1, replica_groups=mesh['x'=4,'y'=8,'c'=2,'zl'=8,'zh'=2] {'x'}, dimensions={0} | all-to-all | bytes 2097152 | tf_op jit(solution)/shard_map/all_to_all | solution.py:21
  102.6 0.2 convert_reduce_fusion
  102.8 0.2 copy.40
  103.0 0.2 copy-done.3
  103.3 0.2 multiply_reduce_fusion
  103.4 0.1 fusion.20
  103.6 0.2 pad_maximum_fusion
  103.8 0.4 copy.41
  104.2 27.5 %all_to_all.21 = f16[8,136,128]{2,1,0:T(8,128)(2,1)S(1)} all-to-all(f16[8,136,128]{2,1,0:T(8,128)(2,1)S(1)} %copy.41), channel_id=1, replica_groups=mesh['x'=4,'y'=8,'c'=2,'zl'=8,'zh'=2] {'zl'}, dimensions={0} | all-to-all | bytes 557056 | tf_op jit(solution)/shard_map/all_to_all | solution.py:140
  131.7 0.1 slice.36
  131.8 0.5 convert_reduce_fusion.1
  132.4 0.8 bitcast_divide_fusion.3
  (41 shorter events, 0.4 us)
Async XLA Ops:
  0.0 1.6 %copy-start = (bf16[256,1536]{1,0:T(8,128)(2,1)S(1)}, bf16[256,1536]{1,0:T(8,128)(2,1)}, u32[]{:S(2)}) copy-start(bf16[256,1536]{1,0:T(8,128)(2,1)} %param.7) | copy-start | bytes 2359300
  1.6 18.5 %copy-start.4 = (s32[16384]{0:T(1024)S(1)}, s32[16384]{0:T(1024)}, u32[]{:S(2)}) copy-start(s32[16384]{0:T(1024)} %param.11) | copy-start | bytes 196612
  4.4 39.5 %all-to-all-start = ((f16[8,200,128]{2,1,0:T(8,128)(2,1)}), f16[8,200,128]{2,1,0:T(8,128)(2,1)S(1)}, u32[]{:S(2)}, u32[]{:S(2)}) async-start(f16[8,200,128]{2,1,0:T(8,128)(2,1)} %pad_maximum_fusion.1), calls=%async_computation | async-start | bytes 819200 | tf_op jit(solution)/shard_map/all_to_all | solution.py:83
  44.3 0.6 copy-start.2
  44.4 8.8 %copy-start.7 = (f32[128]{0:T(128)}, f32[128]{0:T(128)S(1)}, u32[]{:S(2)}) copy-start(f32[128]{0:T(128)S(1)} %fusion.19) | copy-start | bytes 1540
  46.2 29.6 %all-to-all-start.1 = ((bf16[8,64,1024]{2,1,0:T(8,128)(2,1)}), bf16[8,64,1024]{2,1,0:T(8,128)(2,1)S(1)}, u32[]{:S(2)}, u32[]{:S(2)}) async-start(bf16[8,64,1024]{2,1,0:T(8,128)(2,1)} %broadcast_in_dim.26), calls=%async_computation.1 | async-start | bytes 2097152 | tf_op jit(solution)/shard_map/all_to_all | solution.py:15
  53.4 10.6 %collective-permute-start = (bf16[128,1024]{0,1:T(8,128)(2,1)S(1)}, bf16[128,1024]{0,1:T(8,128)(2,1)S(1)}, u32[]{:S(2)}, u32[]{:S(2)}) collective-permute-start(bf16[128,1024]{0,1:T(8,128)(2,1)S(1)} %fusion.18), channel_id=1, source_target_pairs={{0,768},{256,0},{512,256},{768,512},{1,769},{257,1},{513,257},{769... | collective-permute-start | bytes 786440 | tf_op jit(solution)/shard_map/ppermute | solution.py:30
  56.2 9.8 %collective-permute-start.1 = (bf16[128,1024]{0,1:T(8,128)(2,1)S(1)}, bf16[128,1024]{0,1:T(8,128)(2,1)S(1)}, u32[]{:S(2)}, u32[]{:S(2)}) collective-permute-start(bf16[128,1024]{0,1:T(8,128)(2,1)S(1)} %fusion.18), channel_id=1, source_target_pairs={{0,512},{256,768},{512,0},{768,256},{1,513},{257,769},{513,1},{769... | collective-permute-start | bytes 786440 | tf_op jit(solution)/shard_map/ppermute | solution.py:30
  59.2 9.3 %collective-permute-start.2 = (bf16[128,1024]{0,1:T(8,128)(2,1)S(1)}, bf16[128,1024]{0,1:T(8,128)(2,1)S(1)}, u32[]{:S(2)}, u32[]{:S(2)}) collective-permute-start(bf16[128,1024]{0,1:T(8,128)(2,1)S(1)} %fusion.18), channel_id=1, source_target_pairs={{0,256},{256,512},{512,768},{768,0},{1,257},{257,513},{513,769},{7... | collective-permute-start | bytes 786440 | tf_op jit(solution)/shard_map/ppermute | solution.py:30
  68.6 9.9 %copy-start.8 = (f32[128]{0:T(128)S(1)}, f32[128]{0:T(128)}, u32[]{:S(2)}) copy-start(f32[128]{0:T(128)} %copy-done.7) | copy-start | bytes 1540
  68.6 9.9 %copy-start.6 = (s32[512,1]{0,1:T(1,128)S(1)}, s32[512,1]{0,1:T(1,128)}, u32[]{:S(2)}) copy-start(s32[512,1]{0,1:T(1,128)} %broadcast_select_fusion.3) | copy-start | bytes 6148
  75.8 5.8 %collective-permute-start.3 = (bf16[512,1024]{1,0:T(8,128)(2,1)S(1)}, bf16[512,1024]{1,0:T(8,128)(2,1)S(1)}, u32[]{:S(2)}, u32[]{:S(2)}) collective-permute-start(bf16[512,1024]{1,0:T(8,128)(2,1)S(1)} %bitcast.99), channel_id=1, source_target_pairs={{0,16},{16,0},{1,17},{17,1},{2,18},{18,2},{3,19},{19,3},{4,20},{20... | collective-permute-start | bytes 3145736 | tf_op jit(solution)/shard_map/ppermute | solution.py:25
  80.8 1.2 copy-start.1
  80.8 1.2 copy-start.5
  102.6 0.7 copy-start.3
